TPU v7x, 128 devices: a whole 4x4x4 slice. The times are simulated.
128 devices in a mesh: depth: 2 (over core), batch: 64 (over z, y, x).
Axes of the slice: x: 4, y: 4, z: 4, core: 2. Of those that a mesh axis runs over, the one named last changes fastest.
Arguments:
- initial: float32 [64, 32, 32, 128], P('batch'), may hold values from -18 to 18
- guess: float32 [2, 64, 32, 32, 128], P('depth', 'batch'), may hold values from -6 to 6
- conv_in: float32 [8, 3, 3, 128, 128], P('depth'), may hold values from -0.1875 to 0.1875
- conv_out: float32 [8, 3, 3, 128, 128], P('depth'), may hold values from -0.1875 to 0.1875
Outputs:
- corrected: float32 [2, 64, 32, 32, 128], P('depth', 'batch')
- relaxed: float32 [2, 64, 32, 32, 128], P('depth', 'batch')
All inputs are finite; a program needn't handle non-finite values.
Results may differ from a plain program's by a relative error of at most 0.0001.
Values sent between devices are 32-bit elements; how exact they have to be, the bound alone decides.
No kernel may reach another device: no remote copies, remote signals or barrier semaphores. Data moves between devices by JAX's collectives and lax.ppermute only.
A program may use at most 64 MiB of HBM per device.

v0:
```python
import functools

import jax
import jax.numpy as jnp
from jax import lax
from jax.sharding import Mesh
from jax.sharding import PartitionSpec as P

FACTOR = 4
BATCH = ("batch_0", "batch_1", "batch_2")


EPSILON = 1e-05
STEP_SIZE = 0.25


def by_axis(x, axes):
    return functools.reduce(lax.psum, axes, x)


def passed_along(x, axis, by):
    devices = lax.axis_size(axis)
    pairs = [(i, i + by) for i in range(devices) if 0 <= i + by < devices]
    return lax.ppermute(x, axis, pairs)


def convolve(states, kernel):
    return lax.conv_general_dilated(
        states,
        kernel,
        (1, 1),
        "SAME",
        dimension_numbers=("NHWC", "HWIO", "NHWC"),
        precision=lax.Precision.HIGHEST,
    )


def finish(convolved, totals, counted, kernel_out):
    average = totals[0] / counted
    spread = totals[1] / counted - average * average
    normed = jax.nn.relu((convolved - average) * lax.rsqrt(spread + EPSILON))
    return convolve(normed, kernel_out)


def branch(states, kernel_in, kernel_out, counted):
    convolved = convolve(states, kernel_in)
    totals = (
        by_axis(jnp.sum(convolved, axis=(0, 1, 2)), BATCH),
        by_axis(jnp.sum(convolved * convolved, axis=(0, 1, 2)), BATCH),
    )
    return finish(convolved, totals, counted, kernel_out)


def sweep(start, conv_in, conv_out, counted):
    current = start
    first = start
    for layer in range(FACTOR):
        current = current + STEP_SIZE * branch(current, conv_in[layer], conv_out[layer], counted)
        if layer == 0:
            first = current
    return (current, first)


def body(initial, guess, conv_in, conv_out):
    counted = initial.shape[0] * initial.shape[1] * initial.shape[2] * lax.axis_size(BATCH)
    position = lax.axis_index("depth")
    is_first = position == 0
    before = passed_along(guess, "depth", 1)[0]
    start = jnp.where(is_first, initial, before)
    ends, unused = sweep(start, conv_in, conv_out, counted)
    handed = passed_along(ends, "depth", 1)
    restart = jnp.where(is_first, initial, handed)
    fine, first = sweep(restart, conv_in, conv_out, counted)
    tau = fine - (restart + FACTOR * (first - restart))
    kernel_in = conv_in[0]
    kernel_out = conv_out[0]

    def active_conv(current):
        return convolve(current, kernel_in)

    def skipped_conv(current):
        return jnp.zeros_like(current)

    def active_step(operands):
        current, convolved, totals = operands
        return current + FACTOR * STEP_SIZE * finish(convolved, totals, counted, kernel_out) + tau

    def skipped_step(operands):
        return jnp.zeros_like(operands[0])

    def turn_step(turn, carried):
        current, result = carried
        active = position == turn
        convolved = lax.cond(active, active_conv, skipped_conv, current)
        totals = (
            by_axis(jnp.sum(convolved, axis=(0, 1, 2)), BATCH),
            by_axis(jnp.sum(convolved * convolved, axis=(0, 1, 2)), BATCH),
        )
        produced = lax.cond(active, active_step, skipped_step, (current, convolved, totals))
        result = jnp.where(active, produced, result)
        current = passed_along(produced, "depth", 1)
        return (current, result)

    unused_last, result = lax.fori_loop(
        0, lax.axis_size("depth"), turn_step, (initial, jnp.zeros_like(initial))
    )
    return (result[None], ends[None])


def solution(mesh):
    split = Mesh(
        mesh.devices.reshape(mesh.shape["depth"], 4, 4, 4),
        ("depth", "batch_0", "batch_1", "batch_2"),
    )
    placed = (
        P(BATCH, None, None, None),
        P("depth", BATCH, None, None, None),
        P("depth", None, None, None, None),
        P("depth", None, None, None, None),
    )
    return jax.shard_map(
        body,
        mesh=split,
        in_specs=placed,
        out_specs=(P("depth", BATCH, None, None, None), P("depth", BATCH, None, None, None)),
        check_vma=False,
    )
```

profile of v0, /device:TPU:1, one launch (start us, length us, event | category | flops | bytes accessed | tf_op | source)
XLA Modules:
  0.0 415.9 jit_solution(17645317683429111156)
XLA Ops:
  14.0 10.3 %all-reduce.26 = (f32[128]{0:T(128)S(1)}, f32[128]{0:T(128)S(1)}) all-reduce(f32[128]{0:T(128)S(1)} %get-tuple-element.215, f32[128]{0:T(128)S(1)} %get-tuple-element.214), channel_id=1, replica_groups=mesh['depth'=2,'batch_0'=4,'batch_1'=4,'batch_2'=4] {'batch_0'}, use_global_device_ids=true, to_apply=%region_5.6 | all-reduce | flops 256 | bytes 2048 | tf_op jit(solution)/shard_map/psum | solution.py:18
  24.3 8.7 %all-reduce.18 = (f32[128]{0:T(128)S(1)}, f32[128]{0:T(128)S(1)}) all-reduce(f32[128]{0:T(128)S(1)} %get-tuple-element.282, f32[128]{0:T(128)S(1)} %get-tuple-element.283), channel_id=1, replica_groups=mesh['depth'=2,'batch_0'=4,'batch_1'=4,'batch_2'=4] {'batch_1'}, use_global_device_ids=true, to_apply=%region_6.7 | all-reduce | flops 256 | bytes 2048 | tf_op jit(solution)/shard_map/psum | solution.py:18
  33.0 8.9 %all-reduce.10 = (f32[128]{0:T(128)S(1)}, f32[128]{0:T(128)S(1)}) all-reduce(f32[128]{0:T(128)S(1)} %get-tuple-element.266, f32[128]{0:T(128)S(1)} %get-tuple-element.267), channel_id=1, replica_groups=mesh['depth'=2,'batch_0'=4,'batch_1'=4,'batch_2'=4] {'batch_2'}, use_global_device_ids=true, to_apply=%region_7.8 | all-reduce | flops 256 | bytes 2048 | tf_op jit(solution)/shard_map/psum | solution.py:18
  67.2 6.2 %all-reduce.9 = (f32[128]{0:T(128)S(1)}, f32[128]{0:T(128)S(1)}) all-reduce(f32[128]{0:T(128)S(1)} %get-tuple-element.264, f32[128]{0:T(128)S(1)} %get-tuple-element.265), channel_id=1, replica_groups=mesh['depth'=2,'batch_0'=4,'batch_1'=4,'batch_2'=4] {'batch_2'}, use_global_device_ids=true, to_apply=%region_15.16 | all-reduce | flops 256 | bytes 2048 | tf_op jit(solution)/shard_map/psum | solution.py:18
  86.3 7.4 %all-reduce.24 = (f32[128]{0:T(128)S(1)}, f32[128]{0:T(128)S(1)}) all-reduce(f32[128]{0:T(128)S(1)} %get-tuple-element.211, f32[128]{0:T(128)S(1)} %get-tuple-element.210), channel_id=1, replica_groups=mesh['depth'=2,'batch_0'=4,'batch_1'=4,'batch_2'=4] {'batch_0'}, use_global_device_ids=true, to_apply=%region_21.22 | all-reduce | flops 256 | bytes 2048 | tf_op jit(solution)/shard_map/psum | solution.py:18
  93.8 7.5 %all-reduce.16 = (f32[128]{0:T(128)S(1)}, f32[128]{0:T(128)S(1)}) all-reduce(f32[128]{0:T(128)S(1)} %get-tuple-element.278, f32[128]{0:T(128)S(1)} %get-tuple-element.279), channel_id=1, replica_groups=mesh['depth'=2,'batch_0'=4,'batch_1'=4,'batch_2'=4] {'batch_1'}, use_global_device_ids=true, to_apply=%region_22.23 | all-reduce | flops 256 | bytes 2048 | tf_op jit(solution)/shard_map/psum | solution.py:18
  101.3 7.8 %all-reduce.8 = (f32[128]{0:T(128)S(1)}, f32[128]{0:T(128)S(1)}) all-reduce(f32[128]{0:T(128)S(1)} %get-tuple-element.262, f32[128]{0:T(128)S(1)} %get-tuple-element.263), channel_id=1, replica_groups=mesh['depth'=2,'batch_0'=4,'batch_1'=4,'batch_2'=4] {'batch_2'}, use_global_device_ids=true, to_apply=%region_23.24 | all-reduce | flops 256 | bytes 2048 | tf_op jit(solution)/shard_map/psum | solution.py:18
  134.2 6.5 %all-reduce.7 = (f32[128]{0:T(128)S(1)}, f32[128]{0:T(128)S(1)}) all-reduce(f32[128]{0:T(128)S(1)} %get-tuple-element.260, f32[128]{0:T(128)S(1)} %get-tuple-element.261), channel_id=1, replica_groups=mesh['depth'=2,'batch_0'=4,'batch_1'=4,'batch_2'=4] {'batch_2'}, use_global_device_ids=true, to_apply=%region_31.32 | all-reduce | flops 256 | bytes 2048 | tf_op jit(solution)/shard_map/psum | solution.py:18
  153.5 19.5 %collective-permute-done.2 = f32[1,32,32,128]{3,1,2,0:T(8,128)S(1)} collective-permute-done((f32[1,32,32,128]{3,1,2,0:T(8,128)S(1)}, f32[1,32,32,128]{3,1,2,0:T(8,128)S(1)}, u32[]{:S(2)}, u32[]{:S(2)}) %collective-permute-start.2) | collective-permute-done | bytes 524320 | tf_op jit(solution)/shard_map/ppermute | solution.py:24
  179.9 7.9 %all-reduce.22 = (f32[128]{0:T(128)S(1)}, f32[128]{0:T(128)S(1)}) all-reduce(f32[128]{0:T(128)S(1)} %get-tuple-element.207, f32[128]{0:T(128)S(1)} %get-tuple-element.206), channel_id=1, replica_groups=mesh['depth'=2,'batch_0'=4,'batch_1'=4,'batch_2'=4] {'batch_0'}, use_global_device_ids=true, to_apply=%region_37.38 | all-reduce | flops 256 | bytes 2048 | tf_op jit(solution)/shard_map/psum | solution.py:18
  187.8 8.0 %all-reduce.14 = (f32[128]{0:T(128)S(1)}, f32[128]{0:T(128)S(1)}) all-reduce(f32[128]{0:T(128)S(1)} %get-tuple-element.274, f32[128]{0:T(128)S(1)} %get-tuple-element.275), channel_id=1, replica_groups=mesh['depth'=2,'batch_0'=4,'batch_1'=4,'batch_2'=4] {'batch_1'}, use_global_device_ids=true, to_apply=%region_38.39 | all-reduce | flops 256 | bytes 2048 | tf_op jit(solution)/shard_map/psum | solution.py:18
  195.8 7.7 %all-reduce.6 = (f32[128]{0:T(128)S(1)}, f32[128]{0:T(128)S(1)}) all-reduce(f32[128]{0:T(128)S(1)} %get-tuple-element.258, f32[128]{0:T(128)S(1)} %get-tuple-element.259), channel_id=1, replica_groups=mesh['depth'=2,'batch_0'=4,'batch_1'=4,'batch_2'=4] {'batch_2'}, use_global_device_ids=true, to_apply=%region_39.40 | all-reduce | flops 256 | bytes 2048 | tf_op jit(solution)/shard_map/psum | solution.py:18
  228.4 6.4 %all-reduce.5 = (f32[128]{0:T(128)S(1)}, f32[128]{0:T(128)S(1)}) all-reduce(f32[128]{0:T(128)S(1)} %get-tuple-element.256, f32[128]{0:T(128)S(1)} %get-tuple-element.257), channel_id=1, replica_groups=mesh['depth'=2,'batch_0'=4,'batch_1'=4,'batch_2'=4] {'batch_2'}, use_global_device_ids=true, to_apply=%region_47.48 | all-reduce | flops 256 | bytes 2048 | tf_op jit(solution)/shard_map/psum | solution.py:18
  248.0 7.4 %all-reduce.20 = (f32[128]{0:T(128)S(1)}, f32[128]{0:T(128)S(1)}) all-reduce(f32[128]{0:T(128)S(1)} %get-tuple-element.203, f32[128]{0:T(128)S(1)} %get-tuple-element.202), channel_id=1, replica_groups=mesh['depth'=2,'batch_0'=4,'batch_1'=4,'batch_2'=4] {'batch_0'}, use_global_device_ids=true, to_apply=%region_53.54 | all-reduce | flops 256 | bytes 2048 | tf_op jit(solution)/shard_map/psum | solution.py:18
  255.5 7.4 %all-reduce.12 = (f32[128]{0:T(128)S(1)}, f32[128]{0:T(128)S(1)}) all-reduce(f32[128]{0:T(128)S(1)} %get-tuple-element.270, f32[128]{0:T(128)S(1)} %get-tuple-element.271), channel_id=1, replica_groups=mesh['depth'=2,'batch_0'=4,'batch_1'=4,'batch_2'=4] {'batch_1'}, use_global_device_ids=true, to_apply=%region_54.55 | all-reduce | flops 256 | bytes 2048 | tf_op jit(solution)/shard_map/psum | solution.py:18
  262.9 7.7 %all-reduce.4 = (f32[128]{0:T(128)S(1)}, f32[128]{0:T(128)S(1)}) all-reduce(f32[128]{0:T(128)S(1)} %get-tuple-element.254, f32[128]{0:T(128)S(1)} %get-tuple-element.255), channel_id=1, replica_groups=mesh['depth'=2,'batch_0'=4,'batch_1'=4,'batch_2'=4] {'batch_2'}, use_global_device_ids=true, to_apply=%region_55.56 | all-reduce | flops 256 | bytes 2048 | tf_op jit(solution)/shard_map/psum | solution.py:18
  284.0 6.4 %all-reduce.19 = (f32[128]{0:T(128)S(1)}, f32[128]{0:T(128)S(1)}) all-reduce(f32[128]{0:T(128)S(1)} %get-tuple-element.201, f32[128]{0:T(128)S(1)} %get-tuple-element.200), channel_id=1, replica_groups=mesh['depth'=2,'batch_0'=4,'batch_1'=4,'batch_2'=4] {'batch_0'}, use_global_device_ids=true, to_apply=%region_61.62 | all-reduce | flops 256 | bytes 2048 | tf_op jit(solution)/shard_map/psum | solution.py:18
  302.5 6.1 %convolution_multiply_fusion = f32[32,8,5,128]{3,1,2,0:T(8,128)S(1)} fusion(f32[32,1,7,1,128]{4,2,3,0,1:T(8,128)S(1)} %get-tuple-element.287, f32[32,1,7,1,128]{4,2,3,0,1:T(8,128)S(1)} %get-tuple-element.286, f32[32,1,8,5,128]{4,2,3,0,1:T(8,128)S(1)} %select_bitcast_fusion, f32[4,3,3,128,128]{4,3,2,1,0:T(8,128)} %param.13), kind=kOutput, calls=%fused_computation.31 | convolution fusion | flops 2219278336 | bytes 2129920 | tf_op jit(solution)/shard_map/conv_general_dilated | solution.py:28
  309.7 104.7 %while.16 = (s32[]{:T(128)}, f32[1,32,32,128]{3,1,2,0:T(8,128)S(1)}, f32[1,32,32,128]{3,1,2,0:T(8,128)S(1)}, s32[]{:T(128)}, f32[3,3,128,128]{3,2,1,0:T(8,128)},...) while((s32[]{:T(128)}, ...), condition=%wide.region_77.78_spmd.clone, body=%wide.region_64.77_spmd.clone.sunk | while | flops 4438492160 | bytes 23538396 | solution.py:104
  310.2 7.2 %all-reduce.30 = (f32[128]{0:T(128)S(1)}, f32[128]{0:T(128)S(1)}) all-reduce(f32[128]{0:T(128)S(1)} %get-tuple-element.379, f32[128]{0:T(128)S(1)} %get-tuple-element.380), channel_id=1, replica_groups=mesh['depth'=2,'batch_0'=4,'batch_1'=4,'batch_2'=4] {'batch_0'}, use_global_device_ids=true, to_apply=%region_68.68 | all-reduce | flops 256 | bytes 2048 | tf_op jit(solution)/shard_map/while/body/eval_jaxpr/psum | solution.py:18
  317.4 7.4 %all-reduce.31 = (f32[128]{0:T(128)S(1)}, f32[128]{0:T(128)S(1)}) all-reduce(f32[128]{0:T(128)S(1)} %get-tuple-element.381, f32[128]{0:T(128)S(1)} %get-tuple-element.382), channel_id=1, replica_groups=mesh['depth'=2,'batch_0'=4,'batch_1'=4,'batch_2'=4] {'batch_1'}, use_global_device_ids=true, to_apply=%region_69.69 | all-reduce | flops 256 | bytes 2048 | tf_op jit(solution)/shard_map/while/body/eval_jaxpr/psum | solution.py:18
  324.8 7.5 %all-reduce.32 = (f32[128]{0:T(128)S(1)}, f32[128]{0:T(128)S(1)}) all-reduce(f32[128]{0:T(128)S(1)} %get-tuple-element.383, f32[128]{0:T(128)S(1)} %get-tuple-element.384), channel_id=1, replica_groups=mesh['depth'=2,'batch_0'=4,'batch_1'=4,'batch_2'=4] {'batch_2'}, use_global_device_ids=true, to_apply=%region_70.70 | all-reduce | flops 256 | bytes 2048 | tf_op jit(solution)/shard_map/while/body/eval_jaxpr/psum | solution.py:18
  333.8 46.5 %collective-permute-done = f32[1,32,32,128]{3,1,2,0:T(8,128)S(1)} collective-permute-done((f32[1,32,32,128]{3,1,2,0:T(8,128)S(1)}, f32[1,32,32,128]{3,1,2,0:T(8,128)S(1)}, u32[]{:S(2)}, u32[]{:S(2)}) %collective-permute-start) | collective-permute-done | bytes 524320 | tf_op jit(solution)/shard_map/while/body/eval_jaxpr/ppermute | solution.py:24
  380.3 6.2 %conditional.6 = (f32[1,32,32,128]{3,1,2,0:T(8,128)S(1)}) conditional(s32[]{:T(128)} %convert_element_type.10, () %tuple.96, (f32[1,32,32,128]{3,1,2,0:T(8,128)S(1)}, f32[3,3,128,128]{3,2,1,0:T(8,128)}) %tuple.97), branch_computations={%region_65.65_spmd, %region_66.66_spmd} | conditional | flops 2218590208 | bytes 9797900 | solution.py:94
  (149 shorter events, 203.2 us)
Async XLA Ops:
  2.0 6.0 %copy-start.8 = (pred[8,5]{0,1:T(8,128)(4,1)S(1)}, pred[8,5]{0,1:T(8,128)(4,1)}, u32[]{:S(2)}) copy-start(pred[8,5]{0,1:T(8,128)(4,1)} %constant.154) | copy-start | bytes 124
  2.0 4.1 collective-permute-start.1
  42.1 6.2 %copy-start.3 = (f32[1,32,32,128]{3,2,1,0:T(8,128)S(1)}, f32[1,32,32,128]{3,2,1,0:T(8,128)}, u32[]{:S(2)}) copy-start(f32[1,32,32,128]{3,2,1,0:T(8,128)} %param.10) | copy-start | bytes 1572868
  147.2 25.8 %collective-permute-start.2 = (f32[1,32,32,128]{3,1,2,0:T(8,128)S(1)}, f32[1,32,32,128]{3,1,2,0:T(8,128)S(1)}, u32[]{:S(2)}, u32[]{:S(2)}) collective-permute-start(f32[1,32,32,128]{3,1,2,0:T(8,128)S(1)} %fusion.121), channel_id=1, source_target_pairs={{0,64},{1,65},{2,66},{3,67},{4,68},{5,69},{6,70},{7,71},{8,72},{9,... | collective-permute-start | bytes 1572872 | tf_op jit(solution)/shard_map/ppermute | solution.py:24
  241.2 0.8 copy-start
  270.8 6.2 %copy-start.1 = (f32[32,8,5,128]{3,0,2,1:T(8,128)S(1)}, f32[32,8,5,128]{3,0,2,1:T(8,128)}, u32[]{:S(2)}) copy-start(f32[32,8,5,128]{3,0,2,1:T(8,128)} %copy-done) | copy-start | bytes 1966084
  277.0 0.9 copy-start.4
  302.5 6.3 %copy-start.2 = (f32[32,8,5,128]{3,0,2,1:T(8,128)S(1)}, f32[32,8,5,128]{3,0,2,1:T(8,128)}, u32[]{:S(2)}) copy-start(f32[32,8,5,128]{3,0,2,1:T(8,128)} %copy-done) | copy-start | bytes 1966084
  302.5 6.3 %copy-start.5 = (f32[32,8,5,128]{3,0,2,1:T(8,128)S(1)}, f32[32,8,5,128]{3,0,2,1:T(8,128)}, u32[]{:S(2)}) copy-start(f32[32,8,5,128]{3,0,2,1:T(8,128)} %copy-done.4) | copy-start | bytes 1966084
  308.7 1.1 copy-start.6
  332.3 48.0 %collective-permute-start = (f32[1,32,32,128]{3,1,2,0:T(8,128)S(1)}, f32[1,32,32,128]{3,1,2,0:T(8,128)S(1)}, u32[]{:S(2)}, u32[]{:S(2)}) collective-permute-start(f32[1,32,32,128]{3,1,2,0:T(8,128)S(1)} %get-tuple-element.415), channel_id=1, source_target_pairs={{0,64},{1,65},{2,66},{3,67},{4,68},{5,69},{6,70},{7,71},{8,72},{9,... | collective-permute-start | bytes 1572872 | tf_op jit(solution)/shard_map/while/body/eval_jaxpr/ppermute | solution.py:24
  380.3 0.7 copy-start.10
  380.3 1.1 copy-start.7
  404.7 0.7 copy-start.9
  410.6 3.8 collective-permute-start
where the time goes:
time: 423 us; the launch traced here: 416 us
  blocking collectives  210 us (50%)
  matrix products  107 us (25%)
  waiting for transfers between devices  71.2 us (17%)
  local copies, waits for them, and re-layouts  15.4 us (4%)
  other arithmetic  5.19 us (1%)
  starting transfers between devices  5.17 us (1%)
    psum x30, blocking collectives, by_axis(): return functools.reduce(lax.psum, axes, x)  210 us
    conv_general_dilated x18, matrix products, convolve(): lax.conv_general_dilated(states, kernel, (1, 1), 'SAME', dimension_number...  107 us
    ppermute x4, waiting for transfers between devices, passed_along(): return lax.ppermute(x, axis, pairs)  71.2 us
  transfers between devices with their start and end apart: 4, of which 4 were waited for; matrix products, arithmetic and copies ran while one was open for 1% of the time, Pallas kernels for 0%

commit v1 on v0

v1 whole, which is shorter than its diff:
```python
import functools

import jax
import jax.numpy as jnp
from jax import lax
from jax.experimental import pallas as pl
from jax.experimental.pallas import tpu as pltpu
from jax.sharding import Mesh
from jax.sharding import PartitionSpec as P

FACTOR = 4
BATCH = ("batch_0", "batch_1", "batch_2")
WORLD = ("depth",) + BATCH

EPSILON = 1e-05
STEP_SIZE = 0.25

ROWS = 32
COLS = 32
CHANNELS = 128
PAIRS = ROWS // 2
CELLS = ROWS * COLS
VMEM_LIMIT = 24 * 2**20


def split(x):
    high = x.astype(jnp.bfloat16)
    low = (x - high.astype(jnp.float32)).astype(jnp.bfloat16)
    return high, low


def place(row, value, high_ref, low_ref):
    at = (row + 1) // 2 * COLS
    lane = 0 if row % 2 else CHANNELS
    high, low = split(value)
    high_ref[at : at + COLS, lane : lane + CHANNELS] = high
    low_ref[at : at + COLS, lane : lane + CHANNELS] = low


def clear_edges(high_ref, low_ref):
    zeros = jnp.zeros((COLS, CHANNELS), jnp.bfloat16)
    for ref in (high_ref, low_ref):
        ref[0:COLS, 0:CHANNELS] = zeros
        ref[PAIRS * COLS : (PAIRS + 1) * COLS, CHANNELS:] = zeros


def convolve(high_ref, low_ref, weights_ref):
    many = PAIRS * COLS
    high0, high1 = high_ref[0:many, :], high_ref[COLS : COLS + many, :]
    low0, low1 = low_ref[0:many, :], low_ref[COLS : COLS + many, :]
    left = jnp.concatenate([high0, high1, low0, low1, high0, high1], axis=1)

    def part(shift):
        high = weights_ref[shift, 0 : 4 * CHANNELS, :]
        low = weights_ref[shift, 4 * CHANNELS : 8 * CHANNELS, :]
        return jnp.dot(
            left, jnp.concatenate([high, high, low], axis=0), preferred_element_type=jnp.float32
        )

    column = lax.broadcasted_iota(jnp.int32, (many, 2 * CHANNELS), 0) % COLS
    out = part(1)
    out = out + jnp.where(column == 0, 0.0, pltpu.roll(part(0), 1, 0))
    return out + jnp.where(column == COLS - 1, 0.0, pltpu.roll(part(2), many - 1, 0))


def pair_rows(out, pair):
    block = out[pair * COLS : (pair + 1) * COLS, :]
    return block[:, :CHANNELS], block[:, CHANNELS:]


def fold(x):
    total = jnp.sum(x, axis=0, keepdims=True)
    return total[:, :CHANNELS] + total[:, CHANNELS:]


def statistics(out):
    total = fold(out)
    own = total * (1.0 / CELLS)
    away = out - jnp.concatenate([own, own], axis=1)
    return total, fold(away * away)


def emit_statistics(out, send_ref, other=None):
    total, square = statistics(out)
    both = jnp.concatenate([total, square], axis=0)
    if other is not None:
        flag, alternative = other
        both = jnp.where(flag == 1, alternative, both)
    send_ref[...] = jnp.broadcast_to(both[None], send_ref.shape)


def combined(received_ref, base):
    rows = received_ref[pl.ds(base, received_ref.shape[0] // 2)]
    samples = rows.shape[0]
    totals = rows[:, 0:1, :]
    average = jnp.sum(totals, axis=0) * (1.0 / (samples * CELLS))
    away = totals * (1.0 / CELLS) - average[None]
    square = jnp.sum(rows[:, 1:2, :], axis=0) + CELLS * jnp.sum(away * away, axis=0)
    return average, lax.rsqrt(square * (1.0 / (samples * CELLS)) + EPSILON)


def normalise(received_ref, base, z_ref, high_ref, low_ref):
    average, factor = combined(received_ref, base)
    for row in range(ROWS):
        place(row, jnp.maximum((z_ref[row] - average) * factor, 0.0), high_ref, low_ref)


def open_kernel(u_ref, win_ref, z_ref, send_ref, high_ref, low_ref):
    clear_edges(high_ref, low_ref)
    for row in range(ROWS):
        place(row, u_ref[row], high_ref, low_ref)
    out = convolve(high_ref, low_ref, win_ref)
    for pair in range(PAIRS):
        z_ref[2 * pair], z_ref[2 * pair + 1] = pair_rows(out, pair)
    emit_statistics(out, send_ref)


def step_kernel(first, mixed, *refs):
    flags_ref, scale_ref, received_ref, z_ref, u_ref, wout_ref, win_ref, *refs = refs
    if mixed:
        other_ref, *refs = refs
    unew_ref, znew_ref, send_ref, *refs = refs
    if first:
        rest_ref, *refs = refs
    high_ref, low_ref = refs
    clear_edges(high_ref, low_ref)
    normalise(received_ref, flags_ref[0], z_ref, high_ref, low_ref)
    out = convolve(high_ref, low_ref, wout_ref)
    scale = scale_ref[0]
    for pair in range(PAIRS):
        for half, block in enumerate(pair_rows(out, pair)):
            row = 2 * pair + half
            before = u_ref[row]
            after = before + scale * block
            unew_ref[row] = after
            place(row, after, high_ref, low_ref)
            if first:
                coarse = before + FACTOR * STEP_SIZE * block
                rest_ref[row] = coarse - (before + FACTOR * (after - before))
    out = convolve(high_ref, low_ref, win_ref)
    for pair in range(PAIRS):
        znew_ref[2 * pair], znew_ref[2 * pair + 1] = pair_rows(out, pair)
    emit_statistics(out, send_ref, (flags_ref[1], other_ref[...]) if mixed else None)


def coarse_kernel(e_ref, rest_ref, win_ref, v_ref, z_ref, stats_ref, high_ref, low_ref):
    clear_edges(high_ref, low_ref)
    for row in range(ROWS):
        value = e_ref[row] + rest_ref[row]
        v_ref[row] = value
        place(row, value, high_ref, low_ref)
    out = convolve(high_ref, low_ref, win_ref)
    for pair in range(PAIRS):
        z_ref[2 * pair], z_ref[2 * pair + 1] = pair_rows(out, pair)
    total, square = statistics(out)
    stats_ref[...] = jnp.concatenate([total, square], axis=0)


def close_kernel(flags_ref, received_ref, z_ref, u_ref, wout_ref, rest_ref, out_ref, high_ref, low_ref):
    first = flags_ref[1] == 1

    @pl.when(first)
    def _():
        out_ref[...] = rest_ref[...]

    @pl.when(jnp.logical_not(first))
    def _():
        clear_edges(high_ref, low_ref)
        normalise(received_ref, flags_ref[0], z_ref, high_ref, low_ref)
        out = convolve(high_ref, low_ref, wout_ref)
        for pair in range(PAIRS):
            for half, block in enumerate(pair_rows(out, pair)):
                row = 2 * pair + half
                out_ref[row] = (u_ref[row] + STEP_SIZE * block) + rest_ref[row]


def prepare_kernel(w_ref, out_ref):
    zeros = jnp.zeros((CHANNELS, CHANNELS), jnp.bfloat16)
    for shift in range(3):
        parts = [split(w_ref[up, shift]) for up in range(3)]
        for kind in range(2):
            w0, w1, w2 = (parts[up][kind] for up in range(3))
            blocks = ((w0, zeros), (w1, w0), (w2, w1), (zeros, w2))
            for at, (one, two) in enumerate(blocks):
                rows = slice((kind * 4 + at) * CHANNELS, (kind * 4 + at + 1) * CHANNELS)
                out_ref[shift, rows, :CHANNELS] = one
                out_ref[shift, rows, CHANNELS:] = two


STATE = jax.ShapeDtypeStruct((ROWS, COLS, CHANNELS), jnp.float32)
PREPARED = jax.ShapeDtypeStruct((3, 8 * CHANNELS, 2 * CHANNELS), jnp.bfloat16)
SMEM = pl.BlockSpec(memory_space=pltpu.SMEM)
VMEM = pl.BlockSpec(memory_space=pltpu.VMEM)
CONV_FLOPS = 2 * 3 * 512 * 1536 * 256


def call(kernel, name, outs, scalars, convs, *args):
    held = [pltpu.VMEM(((PAIRS + 1) * COLS, 2 * CHANNELS), jnp.bfloat16)] * 2
    touched = sum(a.size * a.dtype.itemsize for a in (*args, *outs))
    return pl.pallas_call(
        kernel,
        name=name,
        out_shape=tuple(outs),
        in_specs=[SMEM] * scalars + [VMEM] * (len(args) - scalars),
        out_specs=(VMEM,) * len(outs),
        scratch_shapes=held if convs else [],
        compiler_params=pltpu.CompilerParams(vmem_limit_bytes=VMEM_LIMIT),
        cost_estimate=pl.CostEstimate(
            flops=convs * CONV_FLOPS + 1000, bytes_accessed=touched, transcendentals=0
        ),
    )(*args)


def prepare(weights):
    return call(prepare_kernel, "prepare", (PREPARED,), 0, 0, weights)[0]


def handed(x, pairs):
    return lax.ppermute(x, "depth", pairs)


def exchange(send):
    return lax.all_to_all(send, WORLD, 0, 0)


def body(initial, guess, conv_in, conv_out):
    devices = lax.axis_size(WORLD)
    group = devices // 2
    sent = jax.ShapeDtypeStruct((devices, 2, CHANNELS), jnp.float32)
    small = jax.ShapeDtypeStruct((2, CHANNELS), jnp.float32)
    position = lax.axis_index("depth")
    is_first = position == 0
    flag = is_first.astype(jnp.int32)
    own = jnp.stack([position * group, flag]).astype(jnp.int32)
    of_first = jnp.stack([jnp.zeros_like(position), flag]).astype(jnp.int32)
    fine_scale = jnp.full((1,), STEP_SIZE, jnp.float32)

    onward = [(0, 1)]
    back = [(1, 0)]

    def step(kernel, outs, flags, scale, received, z, u, wout, win, *more):
        return call(
            kernel, "step", outs, 2, 2, flags, scale, received, z, u, wout, win, *more
        )

    plain = functools.partial(step_kernel, False, False)
    before = handed(guess[0, 0], onward)
    start = jnp.where(is_first, initial[0], before)
    z, send = call(open_kernel, "open", (STATE, sent), 0, 1, start, prepare(conv_in[0]))
    received = exchange(send)
    u = start

    next_in = handed(conv_in[0], back)
    next_out = handed(conv_out[0], back)

    u, z, send, rest = step(
        functools.partial(step_kernel, True, False), (STATE, STATE, sent, STATE),
        own, fine_scale, received, z, u, prepare(conv_out[0]), prepare(conv_in[1]),
    )
    received = exchange(send)
    for layer in (1, 2):
        u, z, send = step(
            plain, (STATE, STATE, sent), own, fine_scale, received, z, u,
            prepare(conv_out[layer]), prepare(conv_in[layer + 1]),
        )
        received = exchange(send)
    coarse_in = prepare(next_in)
    ends, z, send = step(
        plain, (STATE, STATE, sent), own, fine_scale, received, z, u,
        prepare(conv_out[3]), coarse_in,
    )
    received = exchange(send)
    t1 = handed(ends, onward)
    zt = handed(z, onward)
    v1, zv, stats = call(
        coarse_kernel, "coarse", (STATE, STATE, small), 0, 1, ends, rest, coarse_in
    )

    a1, z, send = step(
        functools.partial(step_kernel, False, True), (STATE, STATE, sent),
        of_first, fine_scale, received, zt, t1, prepare(conv_out[0]), prepare(conv_in[1]), stats,
    )
    received = exchange(send)
    u = jnp.where(is_first, v1, a1)
    z = jnp.where(is_first, zv, z)
    scale = jnp.where(is_first, FACTOR * STEP_SIZE, STEP_SIZE).reshape(1).astype(jnp.float32)
    u, z, send = step(
        plain, (STATE, STATE, sent), own, scale, received, z, u,
        prepare(jnp.where(is_first, next_out, conv_out[1])), prepare(conv_in[2]),
    )
    received = exchange(send)
    coarse = handed(u, onward)
    rest = jnp.where(is_first, v1, coarse - (t1 + FACTOR * (a1 - t1)))
    u, z, send = step(
        plain, (STATE, STATE, sent), own, fine_scale, received, z, u,
        prepare(conv_out[2]), prepare(conv_in[3]),
    )
    received = exchange(send)
    (result,) = call(
        close_kernel, "close", (STATE,), 1, 1, own, received, z, u, prepare(conv_out[3]), rest
    )
    return (result[None, None], ends[None, None])


def solution(mesh):
    split_mesh = Mesh(
        mesh.devices.reshape(mesh.shape["depth"], 4, 4, 4),
        ("depth", "batch_0", "batch_1", "batch_2"),
    )
    placed = (
        P(BATCH, None, None, None),
        P("depth", BATCH, None, None, None),
        P("depth", None, None, None, None),
        P("depth", None, None, None, None),
    )
    return jax.shard_map(
        body,
        mesh=split_mesh,
        in_specs=placed,
        out_specs=(P("depth", BATCH, None, None, None), P("depth", BATCH, None, None, None)),
        check_vma=False,
    )
```

time: 423 us -> 216 us (0.51); the launches traced: 416 us -> 214 us
  blocking collectives: 210 us -> 15.1 us
  matrix products: 107 us -> 0 us
  starting transfers between devices: 5.17 us -> 59.8 us
  Pallas kernels: 0 us -> 44.7 us
  local copies, waits for them, and re-layouts: 15.4 us -> 53.5 us
  waiting for transfers between devices: 71.2 us -> 34.3 us
    psum x30 -> x0, blocking collectives: 210 us -> none  [by_axis(): return functools.reduce(lax.psum, axes, x)]
    conv_general_dilated x18 -> x0, matrix products: 107 us -> none  [convolve(): lax.conv_general_dilated(states, kernel, (1, 1), 'SAME', dimension_number...]
    ppermute x4 -> x6, waiting for transfers between devices: 71.2 us -> 0.02 us  [handed(): return lax.ppermute(x, 'depth', pairs)]
    all_to_all x0 -> x7, starting transfers between devices: none -> 46.9 us  [exchange(): return lax.all_to_all(send, WORLD, 0, 0)]
    unnamed x18 -> x120, local copies, waits for them, and re-layouts: 3.39 us -> 48.2 us
    pallas_call x0 -> x20, Pallas kernels: none -> 44.7 us  [call(): pl.pallas_call(kernel, name=name, out_shape=tuple(outs), in_specs=[SMEM]...]
    all_to_all x0 -> x7, waiting for transfers between devices: none -> 34.3 us  [exchange(): return lax.all_to_all(send, WORLD, 0, 0)]
    all_to_all x0 -> x1, blocking collectives: none -> 15.1 us  [exchange(): return lax.all_to_all(send, WORLD, 0, 0)]
  transfers between devices with their start and end apart: 4 -> 13, of which waited for: 4 -> 7; matrix products, arithmetic and copies ran while one was open for 1% -> 5% of each run, Pallas kernels for 0% -> 12%
where the time goes in v1:
time: 216 us; the launch traced here: 214 us
  starting transfers between devices  59.8 us (28%)
  local copies, waits for them, and re-layouts  53.5 us (25%)
  Pallas kernels  44.7 us (21%)
  waiting for transfers between devices  34.3 us (16%)
  blocking collectives  15.1 us (7%)
  other arithmetic  5.84 us (3%)
    unnamed x120, local copies, waits for them, and re-layouts  48.2 us
    all_to_all x7, starting transfers between devices, exchange(): return lax.all_to_all(send, WORLD, 0, 0)  46.9 us
    pallas_call x20, Pallas kernels, call(): pl.pallas_call(kernel, name=name, out_shape=tuple(outs), in_specs=[SMEM]...  44.7 us
    all_to_all x7, waiting for transfers between devices, exchange(): return lax.all_to_all(send, WORLD, 0, 0)  34.3 us
    all_to_all x1, blocking collectives, exchange(): return lax.all_to_all(send, WORLD, 0, 0)  15.1 us
    ppermute x6, starting transfers between devices, handed(): return lax.ppermute(x, 'depth', pairs)  13 us
  transfers between devices with their start and end apart: 13, of which 7 were waited for; matrix products, arithmetic and copies ran while one was open for 5% of the time, Pallas kernels for 12%

profile of v1, /device:TPU:1, one launch (start us, length us, event | category | flops | bytes accessed | tf_op | source)
XLA Modules:
  0.0 214.2 jit_solution(8907653937957367970)
XLA Ops:
  10.3 12.4 %all-to-all-start = ((f32[128,2,128]{2,1,0:T(2,128)}), f32[128,2,128]{2,1,0:T(2,128)}, u32[]{:S(2)}, u32[]{:S(2)}) async-start(f32[128,2,128]{2,1,0:T(2,128)} %get-tuple-element.29), calls=%async_computation | async-start | bytes 262144 | tf_op jit(solution)/shard_map/all_to_all | solution.py:223
  28.1 4.1 %all-to-all-done.refs_2_ = f32[128,2,128]{2,1,0:T(2,128)} async-done(((f32[128,2,128]{2,1,0:T(2,128)}), f32[128,2,128]{2,1,0:T(2,128)}, u32[]{:S(2)}, u32[]{:S(2)}) %all-to-all-start) | async-done | bytes 131104 | tf_op jit(solution)/shard_map/all_to_all | solution.py:223
  37.2 4.8 %step.7 = (f32[32,32,128]{2,1,0:T(8,128)S(1)}, f32[32,32,128]{2,1,0:T(8,128)S(1)}, f32[128,2,128]{2,1,0:T(2,128)S(1)}, f32[32,32,128]{2,1,0:T(8,128)S(1)}) custom-call(s32[2]{0:T(128)S(1)} %pad_add_fusion.refs_0_.flags_ref, f32[1]{0:T(128)} %constant.6.clone.1.refs_1_, f32[128,2,128]{2,1,0:T(2,128)} %all-to-all-done.refs_2_, f32[32,32,128]{2,1,0:T(8,128)S(1)} %copy-done.46, ...), custom_call_target="tpu_custom_call" | custom-call | flops 2415920128 | bytes 6029324 | tf_op jit(solution)/shard_map/step/pallas_call | solution.py:200
  45.0 6.1 %all-to-all-start.1 = ((f32[128,2,128]{2,1,0:T(2,128)}), f32[128,2,128]{2,1,0:T(2,128)}, u32[]{:S(2)}, u32[]{:S(2)}) async-start(f32[128,2,128]{2,1,0:T(2,128)} %copy-done.37), calls=%async_computation.1 | async-start | bytes 262144 | tf_op jit(solution)/shard_map/all_to_all | solution.py:223
  51.1 4.0 %collective-permute-start.1 = (f32[3,3,128,128]{3,2,1,0:T(8,128)S(1)}, f32[3,3,128,128]{3,2,1,0:T(8,128)}, u32[]{:S(2)}, u32[]{:S(2)}) collective-permute-start(f32[3,3,128,128]{3,2,1,0:T(8,128)S(1)} %get-tuple-element.62.w_ref), channel_id=1, source_target_pairs={{64,0},{65,1},{66,2},{67,3},{68,4},{69,5},{70,6},{71,7},{72,8},{73... | collective-permute-start | bytes 1769480 | tf_op jit(solution)/shard_map/ppermute | solution.py:219
  57.9 2.8 %all-to-all-done.1.refs_2_ = f32[128,2,128]{2,1,0:T(2,128)} async-done(((f32[128,2,128]{2,1,0:T(2,128)}), f32[128,2,128]{2,1,0:T(2,128)}, u32[]{:S(2)}, u32[]{:S(2)}) %all-to-all-start.1) | async-done | bytes 131104 | tf_op jit(solution)/shard_map/all_to_all | solution.py:223
  64.5 4.7 %step.8 = (f32[32,32,128]{2,1,0:T(8,128)S(1)}, f32[32,32,128]{2,1,0:T(8,128)S(1)}, f32[128,2,128]{2,1,0:T(2,128)S(1)}) custom-call(s32[2]{0:T(128)S(1)} %pad_add_fusion.refs_0_.flags_ref, f32[1]{0:T(128)} %constant.6.clone.1.refs_1_, f32[128,2,128]{2,1,0:T(2,128)} %all-to-all-done.1.refs_2_, f32[32,32,128]{2,1,0:T(8,128)S(1)} %copy-done.54, ...), custom_call_target="tpu_custom_call" | custom-call | flops 2415920128 | bytes 5505036 | tf_op jit(solution)/shard_map/step/pallas_call | solution.py:200
  71.5 6.0 %all-to-all-start.2 = ((f32[128,2,128]{2,1,0:T(2,128)}), f32[128,2,128]{2,1,0:T(2,128)S(1)}, u32[]{:S(2)}, u32[]{:S(2)}) async-start(f32[128,2,128]{2,1,0:T(2,128)} %copy-done.36), calls=%async_computation.2 | async-start | bytes 262144 | tf_op jit(solution)/shard_map/all_to_all | solution.py:223
  77.4 3.8 %collective-permute-start.4 = (f32[3,3,128,128]{3,2,1,0:T(8,128)S(1)}, f32[3,3,128,128]{3,2,1,0:T(8,128)}, u32[]{:S(2)}, u32[]{:S(2)}) collective-permute-start(f32[3,3,128,128]{3,2,1,0:T(8,128)S(1)} %get-tuple-element.58.w_ref), channel_id=1, source_target_pairs={{64,0},{65,1},{66,2},{67,3},{68,4},{69,5},{70,6},{71,7},{72,8},{73... | collective-permute-start | bytes 1769480 | tf_op jit(solution)/shard_map/ppermute | solution.py:219
  84.0 3.3 %all-to-all-done.2.refs_2_ = f32[128,2,128]{2,1,0:T(2,128)S(1)} async-done(((f32[128,2,128]{2,1,0:T(2,128)}), f32[128,2,128]{2,1,0:T(2,128)S(1)}, u32[]{:S(2)}, u32[]{:S(2)}) %all-to-all-start.2) | async-done | bytes 131104 | tf_op jit(solution)/shard_map/all_to_all | solution.py:223
  90.2 5.0 %step.9 = (f32[32,32,128]{2,1,0:T(8,128)S(1)}, f32[32,32,128]{2,1,0:T(8,128)S(1)}, f32[128,2,128]{2,1,0:T(2,128)}) custom-call(s32[2]{0:T(128)S(1)} %pad_add_fusion.refs_0_.flags_ref, f32[1]{0:T(128)} %constant.6.clone.1.refs_1_, f32[128,2,128]{2,1,0:T(2,128)S(1)} %all-to-all-done.2.refs_2_, f32[32,32,128]{2,1,0:T(8,128)S(1)} %copy-done.50, ...), custom_call_target="tpu_custom_call" | custom-call | flops 2415920128 | bytes 5505036 | tf_op jit(solution)/shard_map/step/pallas_call | solution.py:200
  96.8 5.5 %all-to-all-start.3 = ((f32[128,2,128]{2,1,0:T(2,128)}), f32[128,2,128]{2,1,0:T(2,128)S(1)}, u32[]{:S(2)}, u32[]{:S(2)}) async-start(f32[128,2,128]{2,1,0:T(2,128)} %get-tuple-element.37), calls=%async_computation.3 | async-start | bytes 262144 | tf_op jit(solution)/shard_map/all_to_all | solution.py:223
  106.3 5.9 %all-to-all-done.3.refs_2_ = f32[128,2,128]{2,1,0:T(2,128)S(1)} async-done(((f32[128,2,128]{2,1,0:T(2,128)}), f32[128,2,128]{2,1,0:T(2,128)S(1)}, u32[]{:S(2)}, u32[]{:S(2)}) %all-to-all-start.3) | async-done | bytes 131104 | tf_op jit(solution)/shard_map/all_to_all | solution.py:223
  114.6 5.0 %step.10 = (f32[32,32,128]{2,1,0:T(8,128)}, f32[32,32,128]{2,1,0:T(8,128)}, f32[128,2,128]{2,1,0:T(2,128)}) custom-call(s32[2]{0:T(128)S(1)} %pad_add_fusion.refs_0_.flags_ref, f32[1]{0:T(128)} %constant.6.clone.1.refs_1_, f32[128,2,128]{2,1,0:T(2,128)S(1)} %all-to-all-done.3.refs_2_, f32[32,32,128]{2,1,0:T(8,128)S(1)} %copy-done.58, ...), custom_call_target="tpu_custom_call" | custom-call | flops 2415920128 | bytes 5505036 | tf_op jit(solution)/shard_map/step/pallas_call | solution.py:200
  122.3 5.5 %all-to-all-start.4 = ((f32[128,2,128]{2,1,0:T(2,128)}), f32[128,2,128]{2,1,0:T(2,128)S(1)}, u32[]{:S(2)}, u32[]{:S(2)}) async-start(f32[128,2,128]{2,1,0:T(2,128)} %get-tuple-element.40), calls=%async_computation.4 | async-start | bytes 262144 | tf_op jit(solution)/shard_map/all_to_all | solution.py:223
  139.1 5.5 %step.11 = (f32[32,32,128]{2,1,0:T(8,128)S(1)}, f32[32,32,128]{2,1,0:T(8,128)S(1)}, f32[128,2,128]{2,1,0:T(2,128)}) custom-call(s32[2]{0:T(128)S(1)} %pad_add_fusion.1.refs_0_, f32[1]{0:T(128)} %constant.6.clone.1.refs_1_, f32[128,2,128]{2,1,0:T(2,128)S(1)} %all-to-all-done.4.refs_2_, f32[32,32,128]{2,1,0:T(8,128)} %collective-permute-done.2.refs_3_, ...), custom_call_target="tpu_custom_call" | custom-call | flops 2415920128 | bytes 5506060 | tf_op jit(solution)/shard_map/step/pallas_call | solution.py:200
  145.4 7.4 %all-to-all-start.5 = ((f32[128,2,128]{2,1,0:T(2,128)}), f32[128,2,128]{2,1,0:T(2,128)S(1)}, u32[]{:S(2)}, u32[]{:S(2)}) async-start(f32[128,2,128]{2,1,0:T(2,128)} %get-tuple-element.45), calls=%async_computation.5 | async-start | bytes 262144 | tf_op jit(solution)/shard_map/all_to_all | solution.py:223
  155.2 7.6 %all-to-all-done.5.refs_2_ = f32[128,2,128]{2,1,0:T(2,128)S(1)} async-done(((f32[128,2,128]{2,1,0:T(2,128)}), f32[128,2,128]{2,1,0:T(2,128)S(1)}, u32[]{:S(2)}, u32[]{:S(2)}) %all-to-all-start.5) | async-done | bytes 131104 | tf_op jit(solution)/shard_map/all_to_all | solution.py:223
  166.2 4.3 %step.12 = (f32[32,32,128]{2,1,0:T(8,128)}, f32[32,32,128]{2,1,0:T(8,128)S(1)}, f32[128,2,128]{2,1,0:T(2,128)S(1)}) custom-call(s32[2]{0:T(128)S(1)} %pad_add_fusion.refs_0_.flags_ref, f32[1]{0:T(128)} %bitcast.2.refs_1_, f32[128,2,128]{2,1,0:T(2,128)S(1)} %all-to-all-done.5.refs_2_, f32[32,32,128]{2,1,0:T(8,128)S(1)} %copy-done.34, ...), custom_call_target="tpu_custom_call" | custom-call | flops 2415920128 | bytes 5505036 | tf_op jit(solution)/shard_map/step/pallas_call | solution.py:200
  171.9 15.1 %all_to_all.40.refs_2_ = f32[128,2,128]{2,1,0:T(2,128)S(1)} all-to-all(f32[128,2,128]{2,1,0:T(2,128)S(1)} %get-tuple-element.50), channel_id=1, replica_groups=mesh['depth'=2,'batch_0'=4,'batch_1'=4,'batch_2'=4] {'depth','batch_0','..., dimensions={0} | all-to-all | bytes 262144 | tf_op jit(solution)/shard_map/all_to_all | solution.py:223
  186.9 5.5 %step.13 = (f32[32,32,128]{2,1,0:T(8,128)S(1)}, f32[32,32,128]{2,1,0:T(8,128)S(1)}, f32[128,2,128]{2,1,0:T(2,128)}) custom-call(s32[2]{0:T(128)S(1)} %pad_add_fusion.refs_0_.flags_ref, f32[1]{0:T(128)} %constant.6.clone.1.refs_1_, f32[128,2,128]{2,1,0:T(2,128)S(1)} %all_to_all.40.refs_2_, f32[32,32,128]{2,1,0:T(8,128)S(1)} %get-tuple-element.51.refs_3_, ...), custom_call_target="tpu_custom_call" | custom-call | flops 2415920128 | bytes 5505036 | tf_op jit(solution)/shard_map/step/pallas_call | solution.py:200
  194.0 4.1 %all-to-all-start.7 = ((f32[128,2,128]{2,1,0:T(2,128)}), f32[128,2,128]{2,1,0:T(2,128)S(1)}, u32[]{:S(2)}, u32[]{:S(2)}) async-start(f32[128,2,128]{2,1,0:T(2,128)} %get-tuple-element.53), calls=%async_computation.7 | async-start | bytes 262144 | tf_op jit(solution)/shard_map/all_to_all | solution.py:223
  200.2 8.0 %all-to-all-done.7.received_ref = f32[128,2,128]{2,1,0:T(2,128)S(1)} async-done(((f32[128,2,128]{2,1,0:T(2,128)}), f32[128,2,128]{2,1,0:T(2,128)S(1)}, u32[]{:S(2)}, u32[]{:S(2)}) %all-to-all-start.7) | async-done | bytes 131104 | tf_op jit(solution)/shard_map/all_to_all | solution.py:223
  211.3 2.9 %close.1 = f32[32,32,128]{2,1,0:T(8,128)} custom-call(s32[2]{0:T(128)S(1)} %pad_add_fusion.refs_0_.flags_ref, f32[128,2,128]{2,1,0:T(2,128)S(1)} %all-to-all-done.7.received_ref, f32[32,32,128]{2,1,0:T(8,128)S(1)} %copy-done.42, f32[32,32,128]{2,1,0:T(8,128)S(1)} %copy-done.40, bf16[3,1024,256]{2,1,0:T(8,128)(2,1)S(1)} %copy-done.13, ...), custom_call_target="tpu_custom_call" | custom-call | flops 1207960576 | bytes 3801096 | tf_op jit(solution)/shard_map/close/pallas_call | solution.py:200
  (151 shorter events, 74.1 us)
Async XLA Ops:
  0.6 5.3 %collective-permute-start = (f32[32,32,128]{2,1,0:T(8,128)}, f32[32,32,128]{2,1,0:T(8,128)S(1)}, u32[]{:S(2)}, u32[]{:S(2)}) collective-permute-start(f32[32,32,128]{2,1,0:T(8,128)} %bitcast.27), channel_id=1, source_target_pairs={{0,64},{1,65},{2,66},{3,67},{4,68},{5,69},{6,70},{7,71},{8,72},{9,... | collective-permute-start | bytes 1572872 | tf_op jit(solution)/shard_map/ppermute | solution.py:219
  10.3 22.0 %all-to-all-start = ((f32[128,2,128]{2,1,0:T(2,128)}), f32[128,2,128]{2,1,0:T(2,128)}, u32[]{:S(2)}, u32[]{:S(2)}) async-start(f32[128,2,128]{2,1,0:T(2,128)} %get-tuple-element.29), calls=%async_computation | async-start | bytes 262144 | tf_op jit(solution)/shard_map/all_to_all | solution.py:223
  45.0 15.6 %all-to-all-start.1 = ((f32[128,2,128]{2,1,0:T(2,128)}), f32[128,2,128]{2,1,0:T(2,128)}, u32[]{:S(2)}, u32[]{:S(2)}) async-start(f32[128,2,128]{2,1,0:T(2,128)} %copy-done.37), calls=%async_computation.1 | async-start | bytes 262144 | tf_op jit(solution)/shard_map/all_to_all | solution.py:223
  51.1 5.4 %copy-start = (f32[3,3,128,128]{3,2,1,0:T(8,128)S(1)}, f32[3,3,128,128]{3,2,1,0:T(8,128)}, u32[]{:S(2)}) copy-start(f32[3,3,128,128]{3,2,1,0:T(8,128)} %get-tuple-element.57.w_ref) | copy-start | bytes 1769476
  51.1 52.5 %collective-permute-start.1 = (f32[3,3,128,128]{3,2,1,0:T(8,128)S(1)}, f32[3,3,128,128]{3,2,1,0:T(8,128)}, u32[]{:S(2)}, u32[]{:S(2)}) collective-permute-start(f32[3,3,128,128]{3,2,1,0:T(8,128)S(1)} %get-tuple-element.62.w_ref), channel_id=1, source_target_pairs={{64,0},{65,1},{66,2},{67,3},{68,4},{69,5},{70,6},{71,7},{72,8},{73... | collective-permute-start | bytes 1769480 | tf_op jit(solution)/shard_map/ppermute | solution.py:219
  56.5 4.1 %copy-start.52 = (f32[32,32,128]{2,1,0:T(8,128)S(1)}, f32[32,32,128]{2,1,0:T(8,128)}, u32[]{:S(2)}) copy-start(f32[32,32,128]{2,1,0:T(8,128)} %copy-done.51) | copy-start | bytes 1572868
  71.5 15.9 %all-to-all-start.2 = ((f32[128,2,128]{2,1,0:T(2,128)}), f32[128,2,128]{2,1,0:T(2,128)S(1)}, u32[]{:S(2)}, u32[]{:S(2)}) async-start(f32[128,2,128]{2,1,0:T(2,128)} %copy-done.36), calls=%async_computation.2 | async-start | bytes 262144 | tf_op jit(solution)/shard_map/all_to_all | solution.py:223
  77.4 50.3 %collective-permute-start.4 = (f32[3,3,128,128]{3,2,1,0:T(8,128)S(1)}, f32[3,3,128,128]{3,2,1,0:T(8,128)}, u32[]{:S(2)}, u32[]{:S(2)}) collective-permute-start(f32[3,3,128,128]{3,2,1,0:T(8,128)S(1)} %get-tuple-element.58.w_ref), channel_id=1, source_target_pairs={{64,0},{65,1},{66,2},{67,3},{68,4},{69,5},{70,6},{71,7},{72,8},{73... | collective-permute-start | bytes 1769480 | tf_op jit(solution)/shard_map/ppermute | solution.py:219
  82.7 4.7 %copy-start.48 = (f32[32,32,128]{2,1,0:T(8,128)S(1)}, f32[32,32,128]{2,1,0:T(8,128)}, u32[]{:S(2)}) copy-start(f32[32,32,128]{2,1,0:T(8,128)} %copy-done.47) | copy-start | bytes 1572868
  82.7 4.7 %copy-start.50 = (f32[32,32,128]{2,1,0:T(8,128)S(1)}, f32[32,32,128]{2,1,0:T(8,128)}, u32[]{:S(2)}) copy-start(f32[32,32,128]{2,1,0:T(8,128)} %copy-done.49) | copy-start | bytes 1572868
  96.8 15.4 %all-to-all-start.3 = ((f32[128,2,128]{2,1,0:T(2,128)}), f32[128,2,128]{2,1,0:T(2,128)S(1)}, u32[]{:S(2)}, u32[]{:S(2)}) async-start(f32[128,2,128]{2,1,0:T(2,128)} %get-tuple-element.37), calls=%async_computation.3 | async-start | bytes 262144 | tf_op jit(solution)/shard_map/all_to_all | solution.py:223
  103.6 8.5 %copy-start.56 = (f32[32,32,128]{2,1,0:T(8,128)S(1)}, f32[32,32,128]{2,1,0:T(8,128)}, u32[]{:S(2)}) copy-start(f32[32,32,128]{2,1,0:T(8,128)} %copy-done.55) | copy-start | bytes 1572868
  103.6 8.5 %copy-start.12 = (bf16[3,1024,256]{2,1,0:T(8,128)(2,1)S(1)}, bf16[3,1024,256]{2,1,0:T(8,128)(2,1)}, u32[]{:S(2)}) copy-start(bf16[3,1024,256]{2,1,0:T(8,128)(2,1)} %copy-done.11) | copy-start | bytes 4718596
  119.6 18.1 %collective-permute-start.2 = (f32[32,32,128]{2,1,0:T(8,128)}, f32[32,32,128]{2,1,0:T(8,128)}, u32[]{:S(2)}, u32[]{:S(2)}) collective-permute-start(f32[32,32,128]{2,1,0:T(8,128)} %get-tuple-element.41), channel_id=1, source_target_pairs={{0,64},{1,65},{2,66},{3,67},{4,68},{5,69},{6,70},{7,71},{8,72},{9,... | collective-permute-start | bytes 1572872 | tf_op jit(solution)/shard_map/ppermute | solution.py:219
  120.9 16.8 %collective-permute-start.3 = (f32[32,32,128]{2,1,0:T(8,128)}, f32[32,32,128]{2,1,0:T(8,128)S(1)}, u32[]{:S(2)}, u32[]{:S(2)}) collective-permute-start(f32[32,32,128]{2,1,0:T(8,128)} %get-tuple-element.42.e_ref), channel_id=1, source_target_pairs={{0,64},{1,65},{2,66},{3,67},{4,68},{5,69},{6,70},{7,71},{8,72},{9,... | collective-permute-start | bytes 1572872 | tf_op jit(solution)/shard_map/ppermute | solution.py:219
  122.3 15.4 %all-to-all-start.4 = ((f32[128,2,128]{2,1,0:T(2,128)}), f32[128,2,128]{2,1,0:T(2,128)S(1)}, u32[]{:S(2)}, u32[]{:S(2)}) async-start(f32[128,2,128]{2,1,0:T(2,128)} %get-tuple-element.40), calls=%async_computation.4 | async-start | bytes 262144 | tf_op jit(solution)/shard_map/all_to_all | solution.py:223
  132.8 4.9 %copy-start.4 = (bf16[3,1024,256]{2,1,0:T(8,128)(2,1)S(1)}, bf16[3,1024,256]{2,1,0:T(8,128)(2,1)}, u32[]{:S(2)}) copy-start(bf16[3,1024,256]{2,1,0:T(8,128)(2,1)} %copy-done.2) | copy-start | bytes 4718596
  145.4 17.3 %all-to-all-start.5 = ((f32[128,2,128]{2,1,0:T(2,128)}), f32[128,2,128]{2,1,0:T(2,128)S(1)}, u32[]{:S(2)}, u32[]{:S(2)}) async-start(f32[128,2,128]{2,1,0:T(2,128)} %get-tuple-element.45), calls=%async_computation.5 | async-start | bytes 262144 | tf_op jit(solution)/shard_map/all_to_all | solution.py:223
  152.8 9.9 %copy-start.10 = (bf16[3,1024,256]{2,1,0:T(8,128)(2,1)S(1)}, bf16[3,1024,256]{2,1,0:T(8,128)(2,1)}, u32[]{:S(2)}) copy-start(bf16[3,1024,256]{2,1,0:T(8,128)(2,1)} %copy-done.8) | copy-start | bytes 4718596
  166.2 20.7 %copy-start.16 = (bf16[3,1024,256]{2,1,0:T(8,128)(2,1)S(1)}, bf16[3,1024,256]{2,1,0:T(8,128)(2,1)}, u32[]{:S(2)}) copy-start(bf16[3,1024,256]{2,1,0:T(8,128)(2,1)} %copy-done.14) | copy-start | bytes 4718596
  166.2 20.7 %copy-start.19 = (bf16[3,1024,256]{2,1,0:T(8,128)(2,1)S(1)}, bf16[3,1024,256]{2,1,0:T(8,128)(2,1)}, u32[]{:S(2)}) copy-start(bf16[3,1024,256]{2,1,0:T(8,128)(2,1)} %copy-done.17) | copy-start | bytes 4718596
  170.6 27.5 %collective-permute-start.5 = (f32[32,32,128]{2,1,0:T(8,128)}, f32[32,32,128]{2,1,0:T(8,128)}, u32[]{:S(2)}, u32[]{:S(2)}) collective-permute-start(f32[32,32,128]{2,1,0:T(8,128)} %get-tuple-element.52.refs_4_), channel_id=1, source_target_pairs={{0,64},{1,65},{2,66},{3,67},{4,68},{5,69},{6,70},{7,71},{8,72},{9,... | collective-permute-start | bytes 1572872 | tf_op jit(solution)/shard_map/ppermute | solution.py:219
  194.0 14.1 %copy-start.13 = (bf16[3,1024,256]{2,1,0:T(8,128)(2,1)S(1)}, bf16[3,1024,256]{2,1,0:T(8,128)(2,1)}, u32[]{:S(2)}) copy-start(bf16[3,1024,256]{2,1,0:T(8,128)(2,1)} %copy-done.11) | copy-start | bytes 4718596
  194.0 14.1 %all-to-all-start.7 = ((f32[128,2,128]{2,1,0:T(2,128)}), f32[128,2,128]{2,1,0:T(2,128)S(1)}, u32[]{:S(2)}, u32[]{:S(2)}) async-start(f32[128,2,128]{2,1,0:T(2,128)} %get-tuple-element.53), calls=%async_computation.7 | async-start | bytes 262144 | tf_op jit(solution)/shard_map/all_to_all | solution.py:223
  (49 other events, 55.9 us)

commit v2 on v1

v2 whole, which is shorter than its diff:
```python
import functools

import jax
import jax.numpy as jnp
from jax import lax
from jax.experimental import pallas as pl
from jax.experimental.pallas import tpu as pltpu
from jax.sharding import Mesh
from jax.sharding import PartitionSpec as P

FACTOR = 4
BATCH = ("batch_0", "batch_1", "batch_2")
WORLD = ("depth",) + BATCH

EPSILON = 1e-05
STEP_SIZE = 0.25

ROWS = 32
COLS = 32
CHANNELS = 128
PAIRS = ROWS // 2
CELLS = ROWS * COLS
VMEM_LIMIT = 24 * 2**20


def split(x):
    high = x.astype(jnp.bfloat16)
    low = (x - high.astype(jnp.float32)).astype(jnp.bfloat16)
    return high, low


def place(row, value, high_ref, low_ref):
    at = (row + 1) // 2 * COLS
    lane = 0 if row % 2 else CHANNELS
    high, low = split(value)
    high_ref[at : at + COLS, lane : lane + CHANNELS] = high
    low_ref[at : at + COLS, lane : lane + CHANNELS] = low


def clear_edges(high_ref, low_ref):
    zeros = jnp.zeros((COLS, CHANNELS), jnp.bfloat16)
    for ref in (high_ref, low_ref):
        ref[0:COLS, 0:CHANNELS] = zeros
        ref[PAIRS * COLS : (PAIRS + 1) * COLS, CHANNELS:] = zeros


def convolve(high_ref, low_ref, weights):
    many = PAIRS * COLS
    high0, high1 = high_ref[0:many, :], high_ref[COLS : COLS + many, :]
    low0, low1 = low_ref[0:many, :], low_ref[COLS : COLS + many, :]
    left = jnp.concatenate([high0, high1, low0, low1, high0, high1], axis=1)
    zeros = jnp.zeros((CHANNELS, CHANNELS), jnp.bfloat16)

    def part(shift):
        rows = []
        for kind in range(2):
            w0, w1, w2 = (weights[kind, up, shift] for up in range(3))
            blocks = ((w0, zeros), (w1, w0), (w2, w1), (zeros, w2))
            rows.append([jnp.concatenate(b, axis=1) for b in blocks])
        right = jnp.concatenate(rows[0] + rows[0] + rows[1], axis=0)
        return jnp.dot(left, right, preferred_element_type=jnp.float32)

    column = lax.broadcasted_iota(jnp.int32, (many, 2 * CHANNELS), 0) % COLS
    out = part(1)
    out = out + jnp.where(column == 0, 0.0, pltpu.roll(part(0), 1, 0))
    return out + jnp.where(column == COLS - 1, 0.0, pltpu.roll(part(2), many - 1, 0))


def pair_rows(out, pair):
    block = out[pair * COLS : (pair + 1) * COLS, :]
    return block[:, :CHANNELS], block[:, CHANNELS:]


def fold(x):
    total = jnp.sum(x, axis=0, keepdims=True)
    return total[:, :CHANNELS] + total[:, CHANNELS:]


def statistics(out):
    total = fold(out)
    own = total * (1.0 / CELLS)
    away = out - jnp.concatenate([own, own], axis=1)
    return total, fold(away * away)


def emit_statistics(out, send_ref):
    both = jnp.concatenate(statistics(out), axis=0)
    send_ref[...] = jnp.broadcast_to(both[None], send_ref.shape)


def combined(received_ref, base):
    rows = received_ref[pl.ds(base, received_ref.shape[0] // 2)]
    samples = rows.shape[0]
    totals = rows[:, 0:1, :]
    average = jnp.sum(totals, axis=0) * (1.0 / (samples * CELLS))
    away = totals * (1.0 / CELLS) - average[None]
    square = jnp.sum(rows[:, 1:2, :], axis=0) + CELLS * jnp.sum(away * away, axis=0)
    return average, lax.rsqrt(square * (1.0 / (samples * CELLS)) + EPSILON)


def normalise(received_ref, base, z_ref, held):
    average, factor = combined(received_ref, base)
    clear_edges(*held)
    for row in range(ROWS):
        place(row, jnp.maximum((z_ref[row] - average) * factor, 0.0), *held)


def into_conv(held, weights, z_ref, send_ref):
    out = convolve(*held, weights)
    for pair in range(PAIRS):
        z_ref[2 * pair], z_ref[2 * pair + 1] = pair_rows(out, pair)
    emit_statistics(out, send_ref)


def branch_blocks(held, weights):
    out = convolve(*held, weights)
    for pair in range(PAIRS):
        for half, block in enumerate(pair_rows(out, pair)):
            yield 2 * pair + half, block


def add_branch(held, weights, scale, u_ref, unew_ref, again=True):
    for row, block in branch_blocks(held, weights):
        after = u_ref[row] + scale * block
        unew_ref[row] = after
        if again:
            place(row, after, *held)


def load_kernel(layers, flags_ref, in_hbm, out_hbm, in_ref, out_ref, packed_ref, raw_ref, sem):
    jobs = [(which, layer) for layer in range(layers) for which in range(2)]
    sources, targets = (in_hbm, out_hbm), (in_ref, out_ref)
    copies = [
        pltpu.make_async_copy(sources[which].at[layer], raw_ref.at[at], sem.at[at])
        for at, (which, layer) in enumerate(jobs)
    ]
    for copy in copies:
        copy.start()
    for at, (which, layer) in enumerate(jobs):
        copies[at].wait()
        for up in range(3):
            for across in range(3):
                value = raw_ref[at, up, across]
                high, low = split(value)
                targets[which][layer, 0, up, across] = high
                targets[which][layer, 1, up, across] = low
                if layer == 0:
                    packed_ref[which, up, across] = value


def split_weights(raw_ref, which, weights_ref):
    for up in range(3):
        for across in range(3):
            high, low = split(raw_ref[which, up, across])
            weights_ref[0, up, across] = high
            weights_ref[1, up, across] = low


def open_kernel(flags_ref, initial_ref, before_ref, win_ref, z_ref, u_ref, send_ref, *held):
    @pl.when(flags_ref[1] == 1)
    def _():
        u_ref[...] = initial_ref[...]

    @pl.when(flags_ref[1] == 0)
    def _():
        u_ref[...] = before_ref[...]

    clear_edges(*held)
    for row in range(ROWS):
        place(row, u_ref[row], *held)
    into_conv(held, win_ref.at[0], z_ref, send_ref)


def step_kernel(
    layer, flags_ref, received_ref, z_ref, u_ref, wout_ref, win_ref, unew_ref, znew_ref, send_ref, *refs
):
    *rest_ref, high_ref, low_ref = refs
    held = (high_ref, low_ref)
    normalise(received_ref, flags_ref[0], z_ref, held)
    if layer == 0:
        (rest_ref,) = rest_ref
        for row, block in branch_blocks(held, wout_ref.at[layer]):
            before = u_ref[row]
            after = before + STEP_SIZE * block
            unew_ref[row] = after
            place(row, after, *held)
            coarse = before + FACTOR * STEP_SIZE * block
            rest_ref[row] = coarse - (before + FACTOR * (after - before))
    else:
        add_branch(held, wout_ref.at[layer], STEP_SIZE, u_ref, unew_ref)
    into_conv(held, win_ref.at[layer + 1], znew_ref, send_ref)


def turn_kernel(
    flags_ref, received_ref, z_ref, u_ref, wout_ref, moved_ref, both_ref, ends_ref, send_ref, high_ref, low_ref, weights_ref
):
    held = (high_ref, low_ref)
    normalise(received_ref, flags_ref[0], z_ref, held)
    for row, block in branch_blocks(held, wout_ref.at[FACTOR - 1]):
        after = u_ref[row] + STEP_SIZE * block
        both_ref[0, row] = after
        ends_ref[row] = after
        place(row, after, *held)

    @pl.when(flags_ref[1] == 1)
    def _():
        split_weights(moved_ref, 0, weights_ref)
        into_conv(held, weights_ref, both_ref.at[1], send_ref)


def fork_kernel(
    flags_ref, received_ref, arrived_ref, both_ref, rest_ref, wout_ref, win_ref, moved_ref,
    unew_ref, znew_ref, send_ref, high_ref, low_ref, weights_ref,
):
    held = (high_ref, low_ref)

    @pl.when(flags_ref[1] == 1)
    def _():
        clear_edges(*held)
        for row in range(ROWS):
            value = both_ref[0, row] + rest_ref[row]
            unew_ref[row] = value
            place(row, value, *held)
        split_weights(moved_ref, 0, weights_ref)
        into_conv(held, weights_ref, znew_ref, send_ref)

    @pl.when(flags_ref[1] == 0)
    def _():
        normalise(received_ref, 0, arrived_ref.at[1], held)
        add_branch(held, wout_ref.at[0], STEP_SIZE, arrived_ref.at[0], unew_ref)
        into_conv(held, win_ref.at[1], znew_ref, send_ref)


def coarse_kernel(
    flags_ref, received_ref, z_ref, u_ref, wout_ref, win_ref, moved_ref,
    unew_ref, znew_ref, send_ref, high_ref, low_ref, weights_ref,
):
    held = (high_ref, low_ref)
    normalise(received_ref, flags_ref[0], z_ref, held)

    @pl.when(flags_ref[1] == 1)
    def _():
        split_weights(moved_ref, 1, weights_ref)
        add_branch(held, weights_ref, FACTOR * STEP_SIZE, u_ref, unew_ref, again=False)

    @pl.when(flags_ref[1] == 0)
    def _():
        add_branch(held, wout_ref.at[1], STEP_SIZE, u_ref, unew_ref)
        into_conv(held, win_ref.at[2], znew_ref, send_ref)


def second_kernel(flags_ref, *refs):
    @pl.when(flags_ref[1] == 0)
    def _():
        step_kernel(2, flags_ref, *refs)


def close_kernel(
    flags_ref, received_ref, z_ref, u_ref, wout_ref, arrived_ref, first_ref, coarse_ref, out_ref, *held
):
    @pl.when(flags_ref[1] == 1)
    def _():
        out_ref[...] = first_ref[...]

    @pl.when(flags_ref[1] == 0)
    def _():
        normalise(received_ref, flags_ref[0], z_ref, held)
        for row, block in branch_blocks(held, wout_ref.at[FACTOR - 1]):
            fine = u_ref[row] + STEP_SIZE * block
            begun, first = arrived_ref[0, row], first_ref[row]
            tau = fine - (begun + FACTOR * (first - begun))
            out_ref[row] = coarse_ref[row] + tau


STATE = jax.ShapeDtypeStruct((ROWS, COLS, CHANNELS), jnp.float32)
BOTH = jax.ShapeDtypeStruct((2, ROWS, COLS, CHANNELS), jnp.float32)
SMEM = pl.BlockSpec(memory_space=pltpu.SMEM)
VMEM = pl.BlockSpec(memory_space=pltpu.VMEM)
HELD = [pltpu.VMEM(((PAIRS + 1) * COLS, 2 * CHANNELS), jnp.bfloat16)] * 2
WEIGHTS = [pltpu.VMEM((2, 3, 3, CHANNELS, CHANNELS), jnp.bfloat16)]
CONV_FLOPS = 2 * 3 * 512 * 1536 * 256


def call(kernel, name, outs, convs, scratch, *args):
    touched = sum(a.size * a.dtype.itemsize for a in (*args, *outs))
    return pl.pallas_call(
        kernel,
        name=name,
        out_shape=tuple(outs),
        in_specs=[SMEM] + [VMEM] * (len(args) - 1),
        out_specs=(VMEM,) * len(outs),
        scratch_shapes=scratch,
        compiler_params=pltpu.CompilerParams(vmem_limit_bytes=VMEM_LIMIT),
        cost_estimate=pl.CostEstimate(
            flops=convs * CONV_FLOPS, bytes_accessed=touched, transcendentals=0
        ),
    )(*args)


def load(flags, conv_in, conv_out):
    layers = conv_in.shape[0]
    shape = conv_in.shape[1:]
    ready = jax.ShapeDtypeStruct((layers, 2) + shape, jnp.bfloat16)
    packed = jax.ShapeDtypeStruct((2,) + shape, jnp.float32)
    return pl.pallas_call(
        functools.partial(load_kernel, layers),
        name="load",
        out_shape=(ready, ready, packed),
        in_specs=[SMEM] + [pl.BlockSpec(memory_space=pltpu.HBM)] * 2,
        out_specs=(VMEM,) * 3,
        scratch_shapes=[
            pltpu.VMEM((2 * layers,) + shape, jnp.float32),
            pltpu.SemaphoreType.DMA((2 * layers,)),
        ],
        compiler_params=pltpu.CompilerParams(vmem_limit_bytes=VMEM_LIMIT),
        cost_estimate=pl.CostEstimate(
            flops=1000, bytes_accessed=4 * conv_in.size * 4, transcendentals=0
        ),
    )(flags, conv_in, conv_out)


def handed(x, pairs):
    return lax.ppermute(x, "depth", pairs)


def exchange(send):
    return lax.all_to_all(send, WORLD, 0, 0)


def body(initial, guess, conv_in, conv_out):
    devices = lax.axis_size(WORLD)
    sent = jax.ShapeDtypeStruct((devices, 2, CHANNELS), jnp.float32)
    position = lax.axis_index("depth")
    flags = jnp.stack([position * (devices // 2), 1 - position]).astype(jnp.int32)
    outs = (STATE, STATE, sent)

    before = handed(guess[0, 0], [(0, 1)])
    ready_in, ready_out, packed = load(flags, conv_in, conv_out)
    moved = handed(packed, [(1, 0)])
    z, u, send = call(open_kernel, "open", outs, 1, HELD, flags, initial[0], before, ready_in)
    send, moved = lax.optimization_barrier((send, moved))
    received = exchange(send)
    u, z, send, rest = call(
        functools.partial(step_kernel, 0), "step", outs + (STATE,), 2, HELD,
        flags, received, z, u, ready_out, ready_in,
    )
    received = exchange(send)
    for layer in (1, 2):
        u, z, send = call(
            functools.partial(step_kernel, layer), "step", outs, 2, HELD,
            flags, received, z, u, ready_out, ready_in,
        )
        received = exchange(send)
    both, ends, send = call(
        turn_kernel, "turn", (BOTH, STATE, sent), 2, HELD + WEIGHTS,
        flags, received, z, u, ready_out, moved,
    )
    arrived = handed(both, [(0, 1)])
    received = exchange(send)
    first, z, send = call(
        fork_kernel, "fork", outs, 2, HELD + WEIGHTS,
        flags, received, arrived, both, rest, ready_out, ready_in, moved,
    )
    received = exchange(send)
    u, z, send = call(
        coarse_kernel, "coarse", outs, 2, HELD + WEIGHTS,
        flags, received, z, first, ready_out, ready_in, moved,
    )
    coarse = handed(u, [(0, 1)])
    received = exchange(send)
    u, z, send = call(
        second_kernel, "second", outs, 2, HELD, flags, received, z, u, ready_out, ready_in
    )
    received = exchange(send)
    (result,) = call(
        close_kernel, "close", (STATE,), 1, HELD,
        flags, received, z, u, ready_out, arrived, first, coarse,
    )
    return (result[None, None], ends[None, None])


def solution(mesh):
    split_mesh = Mesh(
        mesh.devices.reshape(mesh.shape["depth"], 4, 4, 4),
        ("depth", "batch_0", "batch_1", "batch_2"),
    )
    placed = (
        P(BATCH, None, None, None),
        P("depth", BATCH, None, None, None),
        P("depth", None, None, None, None),
        P("depth", None, None, None, None),
    )
    return jax.shard_map(
        body,
        mesh=split_mesh,
        in_specs=placed,
        out_specs=(P("depth", BATCH, None, None, None), P("depth", BATCH, None, None, None)),
        check_vma=False,
    )
```

time: 216 us -> 169 us (0.78)
  blocking collectives: 15.1 us -> 117 us
  starting transfers between devices: 59.8 us -> 7.26 us
  local copies, waits for them, and re-layouts: 53.5 us -> 3.34 us
  waiting for transfers between devices: 34.3 us -> 2.51 us
  Pallas kernels: 44.7 us -> 36.8 us
  other arithmetic: 5.84 us -> 0.08 us
    all_to_all x1 -> x8, blocking collectives: 15.1 us -> 117 us  [exchange(): return lax.all_to_all(send, WORLD, 0, 0)]
    all_to_all x7 -> x0, starting transfers between devices: 46.9 us -> none  [exchange(): return lax.all_to_all(send, WORLD, 0, 0)]
    unnamed x120 -> x8, local copies, waits for them, and re-layouts: 48.2 us -> 3.34 us
    all_to_all x7 -> x0, waiting for transfers between devices: 34.3 us -> none  [exchange(): return lax.all_to_all(send, WORLD, 0, 0)]
    pallas_call x20 -> x9, Pallas kernels: 44.7 us -> 34.7 us  [call(): pl.pallas_call(kernel, name=name, out_shape=tuple(outs), in_specs=[SMEM]...]
    ppermute x6 -> x4, starting transfers between devices: 13 us -> 7.26 us  [handed(): return lax.ppermute(x, 'depth', pairs)]
    select_n x4 -> x0, other arithmetic: 5.69 us -> none  [the longest x1 2.35 us: body(): u = jnp.where(is_first, v1, a1)]
    squeeze x2 -> x0, local copies, waits for them, and re-layouts: 5.23 us -> none  [the longest x1 2.63 us: body(): conv_out[3]]
  transfers between devices with their start and end apart: 13 -> 4, of which waited for: 7 -> 1; matrix products, arithmetic and copies ran while one was open for 5% -> 0% of each run, Pallas kernels for 12% -> 4%
where the time goes in v2:
time: 169 us; the launch traced here: 168 us
  blocking collectives  117 us (69%)
  Pallas kernels  36.8 us (22%)
  starting transfers between devices  7.26 us (4%)
  local copies, waits for them, and re-layouts  3.34 us (2%)
  waiting for transfers between devices  2.51 us (1%)
    all_to_all x8, blocking collectives, exchange(): return lax.all_to_all(send, WORLD, 0, 0)  117 us
    pallas_call x9, Pallas kernels, call(): pl.pallas_call(kernel, name=name, out_shape=tuple(outs), in_specs=[SMEM]...  34.7 us
    ppermute x4, starting transfers between devices, handed(): return lax.ppermute(x, 'depth', pairs)  7.26 us
  transfers between devices with their start and end apart: 4, of which 1 were waited for; matrix products, arithmetic and copies ran while one was open for 0% of the time, Pallas kernels for 4%

profile of v2, /device:TPU:1, one launch (start us, length us, event | category | flops | bytes accessed | tf_op | source)
XLA Modules:
  0.0 168.1 jit_solution(7207772014944880576)
XLA Ops:
  0.7 1.7 copy-done
  2.4 1.7 copy-done.1
  4.0 2.1 %load.1 = (bf16[4,2,3,3,128,128]{5,4,3,2,1,0:T(8,128)(2,1)S(1)}, bf16[4,2,3,3,128,128]{5,4,3,2,1,0:T(8,128)(2,1)S(1)}, f32[2,3,3,128,128]{4,3,2,1,0:T(8,128)S(1)}) custom-call(s32[2]{0:T(128)S(1)} %pad_add_fusion.flags_ref, f32[4,3,3,128,128]{4,3,2,1,0:T(8,128)S(1)} %copy-done, f32[4,3,3,128,128]{4,3,2,1,0:T(8,128)S(1)} %copy-done.1), custom_call_target="tpu_custom_call" | custom-call | flops 1000 | bytes 9437184 | tf_op jit(solution)/shard_map/load/pallas_call | solution.py:305
  6.2 3.4 %collective-permute-start.1 = (f32[2,3,3,128,128]{4,3,2,1,0:T(8,128)S(1)}, f32[2,3,3,128,128]{4,3,2,1,0:T(8,128)S(1)}, u32[]{:S(2)}, u32[]{:S(2)}) collective-permute-start(f32[2,3,3,128,128]{4,3,2,1,0:T(8,128)S(1)} %get-tuple-element.34), channel_id=1, source_target_pairs={{64,0},{65,1},{66,2},{67,3},{68,4},{69,5},{70,6},{71,7},{72,8},{73... | collective-permute-start | bytes 3538952 | tf_op jit(solution)/shard_map/ppermute | solution.py:323
  9.6 1.3 collective-permute-start
  10.9 2.5 %collective-permute-done.before_ref = f32[32,32,128]{2,1,0:T(8,128)S(1)} collective-permute-done((f32[32,32,128]{2,1,0:T(8,128)S(1)}, f32[32,32,128]{2,1,0:T(8,128)S(1)}, u32[]{:S(2)}, u32[]{:S(2)}) %collective-permute-start) | collective-permute-done | bytes 524320 | tf_op jit(solution)/shard_map/ppermute | solution.py:323
  13.4 2.1 %open.1 = (f32[32,32,128]{2,1,0:T(8,128)S(1)}, f32[32,32,128]{2,1,0:T(8,128)S(1)}, f32[128,2,128]{2,1,0:T(2,128)S(1)}) custom-call(s32[2]{0:T(128)S(1)} %pad_add_fusion.flags_ref, f32[32,32,128]{2,1,0:T(8,128)S(1)} %bitcast.6, f32[32,32,128]{2,1,0:T(8,128)S(1)} %collective-permute-done.before_ref, ...), custom_call_target="tpu_custom_call" | custom-call | flops 1207959552 | bytes 4587528 | tf_op jit(solution)/shard_map/open/pallas_call | solution.py:286
  15.5 20.0 %all_to_all.40.received_ref = f32[128,2,128]{2,1,0:T(2,128)S(1)} all-to-all(f32[128,2,128]{2,1,0:T(2,128)S(1)} %get-tuple-element.35), channel_id=1, replica_groups=mesh['depth'=2,'batch_0'=4,'batch_1'=4,'batch_2'=4] {'depth','batch_0','..., dimensions={0} | all-to-all | bytes 262144 | tf_op jit(solution)/shard_map/all_to_all | solution.py:327
  35.6 4.5 %step.3 = (f32[32,32,128]{2,1,0:T(8,128)S(1)}, f32[32,32,128]{2,1,0:T(8,128)S(1)}, f32[128,2,128]{2,1,0:T(2,128)S(1)}, f32[32,32,128]{2,1,0:T(8,128)S(1)}) custom-call(s32[2]{0:T(128)S(1)} %pad_add_fusion.flags_ref, f32[128,2,128]{2,1,0:T(2,128)S(1)} %all_to_all.40.received_ref, f32[32,32,128]{2,1,0:T(8,128)S(1)} %get-tuple-element.36.z_ref, ...), custom_call_target="tpu_custom_call" | custom-call | flops 2415919104 | bytes 7602184 | tf_op jit(solution)/shard_map/step/pallas_call | solution.py:286
  40.1 13.7 %all_to_all.41.received_ref = f32[128,2,128]{2,1,0:T(2,128)S(1)} all-to-all(f32[128,2,128]{2,1,0:T(2,128)S(1)} %get-tuple-element.39), channel_id=1, replica_groups=mesh['depth'=2,'batch_0'=4,'batch_1'=4,'batch_2'=4] {'depth','batch_0','..., dimensions={0} | all-to-all | bytes 262144 | tf_op jit(solution)/shard_map/all_to_all | solution.py:327
  53.7 4.4 %step.4 = (f32[32,32,128]{2,1,0:T(8,128)S(1)}, f32[32,32,128]{2,1,0:T(8,128)S(1)}, f32[128,2,128]{2,1,0:T(2,128)S(1)}) custom-call(s32[2]{0:T(128)S(1)} %pad_add_fusion.flags_ref, f32[128,2,128]{2,1,0:T(2,128)S(1)} %all_to_all.41.received_ref, f32[32,32,128]{2,1,0:T(8,128)S(1)} %get-tuple-element.40.z_ref, f32[32,32,128]{2,1,0:T(8,128)S(1)} %get-tuple-element.41.u_ref, ...), custom_call_target="tpu_custom_call" | custom-call | flops 2415919104 | bytes 7077896 | tf_op jit(solution)/shard_map/step/pallas_call | solution.py:286
  58.1 13.7 %all_to_all.42.received_ref = f32[128,2,128]{2,1,0:T(2,128)S(1)} all-to-all(f32[128,2,128]{2,1,0:T(2,128)S(1)} %get-tuple-element.42), channel_id=1, replica_groups=mesh['depth'=2,'batch_0'=4,'batch_1'=4,'batch_2'=4] {'depth','batch_0','..., dimensions={0} | all-to-all | bytes 262144 | tf_op jit(solution)/shard_map/all_to_all | solution.py:327
  71.8 4.4 %step.5 = (f32[32,32,128]{2,1,0:T(8,128)S(1)}, f32[32,32,128]{2,1,0:T(8,128)S(1)}, f32[128,2,128]{2,1,0:T(2,128)S(1)}) custom-call(s32[2]{0:T(128)S(1)} %pad_add_fusion.flags_ref, f32[128,2,128]{2,1,0:T(2,128)S(1)} %all_to_all.42.received_ref, f32[32,32,128]{2,1,0:T(8,128)S(1)} %get-tuple-element.43.z_ref, f32[32,32,128]{2,1,0:T(8,128)S(1)} %get-tuple-element.44.u_ref, ...), custom_call_target="tpu_custom_call" | custom-call | flops 2415919104 | bytes 7077896 | tf_op jit(solution)/shard_map/step/pallas_call | solution.py:286
  76.1 13.7 %all_to_all.43.received_ref = f32[128,2,128]{2,1,0:T(2,128)S(1)} all-to-all(f32[128,2,128]{2,1,0:T(2,128)S(1)} %get-tuple-element.45), channel_id=1, replica_groups=mesh['depth'=2,'batch_0'=4,'batch_1'=4,'batch_2'=4] {'depth','batch_0','..., dimensions={0} | all-to-all | bytes 262144 | tf_op jit(solution)/shard_map/all_to_all | solution.py:327
  89.8 3.0 %turn.1 = (f32[2,32,32,128]{3,2,1,0:T(8,128)S(1)}, f32[32,32,128]{2,1,0:T(8,128)}, f32[128,2,128]{2,1,0:T(2,128)S(1)}) custom-call(s32[2]{0:T(128)S(1)} %pad_add_fusion.flags_ref, f32[128,2,128]{2,1,0:T(2,128)S(1)} %all_to_all.43.received_ref, f32[32,32,128]{2,1,0:T(8,128)S(1)} %get-tuple-element.46.z_ref, f32[32,32,128]{2,1,0:T(8,128)S(1)} %get-tuple-element.47.u_ref, ...), custom_call_target="tpu_custom_call" | custom-call | flops 2415919104 | bytes 6422536 | tf_op jit(solution)/shard_map/turn/pallas_call | solution.py:286
  94.1 15.3 %all_to_all.44.received_ref = f32[128,2,128]{2,1,0:T(2,128)S(1)} all-to-all(f32[128,2,128]{2,1,0:T(2,128)S(1)} %get-tuple-element.49), channel_id=1, replica_groups=mesh['depth'=2,'batch_0'=4,'batch_1'=4,'batch_2'=4] {'depth','batch_0','..., dimensions={0} | all-to-all | bytes 262144 | tf_op jit(solution)/shard_map/all_to_all | solution.py:327
  109.4 4.3 %fork.1 = (f32[32,32,128]{2,1,0:T(8,128)S(1)}, f32[32,32,128]{2,1,0:T(8,128)S(1)}, f32[128,2,128]{2,1,0:T(2,128)S(1)}) custom-call(s32[2]{0:T(128)S(1)} %pad_add_fusion.flags_ref, f32[128,2,128]{2,1,0:T(2,128)S(1)} %all_to_all.44.received_ref, f32[2,32,32,128]{3,2,1,0:T(8,128)S(1)} %collective-permute-done.2.arrived_ref, ...), custom_call_target="tpu_custom_call" | custom-call | flops 2415919104 | bytes 9830408 | tf_op jit(solution)/shard_map/fork/pallas_call | solution.py:286
  113.8 13.3 %all_to_all.45.received_ref = f32[128,2,128]{2,1,0:T(2,128)S(1)} all-to-all(f32[128,2,128]{2,1,0:T(2,128)S(1)} %get-tuple-element.52), channel_id=1, replica_groups=mesh['depth'=2,'batch_0'=4,'batch_1'=4,'batch_2'=4] {'depth','batch_0','..., dimensions={0} | all-to-all | bytes 262144 | tf_op jit(solution)/shard_map/all_to_all | solution.py:327
  127.1 4.5 %coarse.1 = (f32[32,32,128]{2,1,0:T(8,128)S(1)}, f32[32,32,128]{2,1,0:T(8,128)S(1)}, f32[128,2,128]{2,1,0:T(2,128)S(1)}) custom-call(s32[2]{0:T(128)S(1)} %pad_add_fusion.flags_ref, f32[128,2,128]{2,1,0:T(2,128)S(1)} %all_to_all.45.received_ref, f32[32,32,128]{2,1,0:T(8,128)S(1)} %get-tuple-element.53.z_ref, ...), custom_call_target="tpu_custom_call" | custom-call | flops 2415919104 | bytes 8257544 | tf_op jit(solution)/shard_map/coarse/pallas_call | solution.py:286
  131.6 1.3 collective-permute-start.3
  132.9 14.3 %all_to_all.46.refs_0_ = f32[128,2,128]{2,1,0:T(2,128)S(1)} all-to-all(f32[128,2,128]{2,1,0:T(2,128)S(1)} %get-tuple-element.55), channel_id=1, replica_groups=mesh['depth'=2,'batch_0'=4,'batch_1'=4,'batch_2'=4] {'depth','batch_0','..., dimensions={0} | all-to-all | bytes 262144 | tf_op jit(solution)/shard_map/all_to_all | solution.py:327
  147.2 4.6 %second.1 = (f32[32,32,128]{2,1,0:T(8,128)S(1)}, f32[32,32,128]{2,1,0:T(8,128)S(1)}, f32[128,2,128]{2,1,0:T(2,128)S(1)}) custom-call(s32[2]{0:T(128)S(1)} %pad_add_fusion.flags_ref, f32[128,2,128]{2,1,0:T(2,128)S(1)} %all_to_all.46.refs_0_, f32[32,32,128]{2,1,0:T(8,128)S(1)} %get-tuple-element.56.refs_1_, f32[32,32,128]{2,1,0:T(8,128)S(1)} %get-tuple-element.57.refs_2_, ...), custom_call_target="tpu_custom_call" | custom-call | flops 2415919104 | bytes 7077896 | tf_op jit(solution)/shard_map/second/pallas_call | solution.py:286
  151.8 13.3 %all_to_all.47.received_ref = f32[128,2,128]{2,1,0:T(2,128)S(1)} all-to-all(f32[128,2,128]{2,1,0:T(2,128)S(1)} %get-tuple-element.58), channel_id=1, replica_groups=mesh['depth'=2,'batch_0'=4,'batch_1'=4,'batch_2'=4] {'depth','batch_0','..., dimensions={0} | all-to-all | bytes 262144 | tf_op jit(solution)/shard_map/all_to_all | solution.py:327
  165.1 3.0 %close.1 = f32[32,32,128]{2,1,0:T(8,128)} custom-call(s32[2]{0:T(128)S(1)} %pad_add_fusion.flags_ref, f32[128,2,128]{2,1,0:T(2,128)S(1)} %all_to_all.47.received_ref, f32[32,32,128]{2,1,0:T(8,128)S(1)} %get-tuple-element.59.z_ref, f32[32,32,128]{2,1,0:T(8,128)S(1)} %get-tuple-element.60.u_ref, ...), custom_call_target="tpu_custom_call" | custom-call | flops 1207959552 | bytes 6160392 | tf_op jit(solution)/shard_map/close/pallas_call | solution.py:286
  (11 shorter events, 1.4 us)
Async XLA Ops:
  0.7 1.7 copy-start
  2.4 1.7 copy-start.1
  4.0 5.6 %copy-start.3 = (f32[1,1,32,32,128]{4,3,2,1,0:T(8,128)S(1)}, f32[1,1,32,32,128]{4,3,2,1,0:T(8,128)}, u32[]{:S(2)}) copy-start(f32[1,1,32,32,128]{4,3,2,1,0:T(8,128)} %param.5) | copy-start | bytes 1572868
  4.0 9.4 %copy-start.2 = (f32[1,32,32,128]{3,2,1,0:T(8,128)S(1)}, f32[1,32,32,128]{3,2,1,0:T(8,128)}, u32[]{:S(2)}) copy-start(f32[1,32,32,128]{3,2,1,0:T(8,128)} %param.4) | copy-start | bytes 1572868
  6.2 9.3 %collective-permute-start.1 = (f32[2,3,3,128,128]{4,3,2,1,0:T(8,128)S(1)}, f32[2,3,3,128,128]{4,3,2,1,0:T(8,128)S(1)}, u32[]{:S(2)}, u32[]{:S(2)}) collective-permute-start(f32[2,3,3,128,128]{4,3,2,1,0:T(8,128)S(1)} %get-tuple-element.34), channel_id=1, source_target_pairs={{64,0},{65,1},{66,2},{67,3},{68,4},{69,5},{70,6},{71,7},{72,8},{73... | collective-permute-start | bytes 3538952 | tf_op jit(solution)/shard_map/ppermute | solution.py:323
  9.6 3.8 %collective-permute-start = (f32[32,32,128]{2,1,0:T(8,128)S(1)}, f32[32,32,128]{2,1,0:T(8,128)S(1)}, u32[]{:S(2)}, u32[]{:S(2)}) collective-permute-start(f32[32,32,128]{2,1,0:T(8,128)S(1)} %bitcast.8), channel_id=1, source_target_pairs={{0,64},{1,65},{2,66},{3,67},{4,68},{5,69},{6,70},{7,71},{8,72},{9,... | collective-permute-start | bytes 1572872 | tf_op jit(solution)/shard_map/ppermute | solution.py:323
  92.8 16.6 %collective-permute-start.2 = (f32[2,32,32,128]{3,2,1,0:T(8,128)S(1)}, f32[2,32,32,128]{3,2,1,0:T(8,128)S(1)}, u32[]{:S(2)}, u32[]{:S(2)}) collective-permute-start(f32[2,32,32,128]{3,2,1,0:T(8,128)S(1)} %get-tuple-element.50.both_ref), channel_id=1, source_target_pairs={{0,64},{1,65},{2,66},{3,67},{4,68},{5,69},{6,70},{7,71},{8,72},{9,... | collective-permute-start | bytes 3145736 | tf_op jit(solution)/shard_map/ppermute | solution.py:323
  131.6 33.5 %collective-permute-start.3 = (f32[32,32,128]{2,1,0:T(8,128)S(1)}, f32[32,32,128]{2,1,0:T(8,128)S(1)}, u32[]{:S(2)}, u32[]{:S(2)}) collective-permute-start(f32[32,32,128]{2,1,0:T(8,128)S(1)} %get-tuple-element.57.refs_2_), channel_id=1, source_target_pairs={{0,64},{1,65},{2,66},{3,67},{4,68},{5,69},{6,70},{7,71},{8,72},{9,... | collective-permute-start | bytes 1572872 | tf_op jit(solution)/shard_map/ppermute | solution.py:323

commit v3 on v2

--- a/solution.py
+++ b/solution.py
@@ -21,6 +21,7 @@
 PAIRS = ROWS // 2
 CELLS = ROWS * COLS
 VMEM_LIMIT = 24 * 2**20
+READY_LIMIT = 24 * 2**20
 
 
 def split(x):
@@ -127,36 +128,25 @@
             place(row, after, *held)
 
 
-def load_kernel(layers, flags_ref, in_hbm, out_hbm, in_ref, out_ref, packed_ref, raw_ref, sem):
-    jobs = [(which, layer) for layer in range(layers) for which in range(2)]
-    sources, targets = (in_hbm, out_hbm), (in_ref, out_ref)
-    copies = [
-        pltpu.make_async_copy(sources[which].at[layer], raw_ref.at[at], sem.at[at])
-        for at, (which, layer) in enumerate(jobs)
-    ]
-    for copy in copies:
-        copy.start()
-    for at, (which, layer) in enumerate(jobs):
-        copies[at].wait()
-        for up in range(3):
-            for across in range(3):
-                value = raw_ref[at, up, across]
-                high, low = split(value)
-                targets[which][layer, 0, up, across] = high
-                targets[which][layer, 1, up, across] = low
-                if layer == 0:
-                    packed_ref[which, up, across] = value
-
-
-def split_weights(raw_ref, which, weights_ref):
+def split_weights(raw_ref, at, weights_ref):
     for up in range(3):
         for across in range(3):
-            high, low = split(raw_ref[which, up, across])
+            high, low = split(raw_ref[at, up, across])
             weights_ref[0, up, across] = high
             weights_ref[1, up, across] = low
 
 
-def open_kernel(flags_ref, initial_ref, before_ref, win_ref, z_ref, u_ref, send_ref, *held):
+def ready_kernel(flags_ref, initial_hbm, win_hbm, initial_ref, weights_ref, raw_ref, sem):
+    weights = pltpu.make_async_copy(win_hbm.at[pl.ds(0, 1)], raw_ref, sem.at[0])
+    state = pltpu.make_async_copy(initial_hbm, initial_ref, sem.at[1])
+    weights.start()
+    state.start()
+    weights.wait()
+    split_weights(raw_ref, 0, weights_ref)
+    state.wait()
+
+
+def open_kernel(flags_ref, initial_ref, before_ref, weights_ref, z_ref, u_ref, send_ref, *held):
     @pl.when(flags_ref[1] == 1)
     def _():
         u_ref[...] = initial_ref[...]
@@ -168,18 +158,21 @@
     clear_edges(*held)
     for row in range(ROWS):
         place(row, u_ref[row], *held)
-    into_conv(held, win_ref.at[0], z_ref, send_ref)
+    into_conv(held, weights_ref, z_ref, send_ref)
 
 
 def step_kernel(
     layer, flags_ref, received_ref, z_ref, u_ref, wout_ref, win_ref, unew_ref, znew_ref, send_ref, *refs
 ):
-    *rest_ref, high_ref, low_ref = refs
+    *more, high_ref, low_ref, ending_ref, begun_ref = refs
     held = (high_ref, low_ref)
+    split_weights(wout_ref, layer, ending_ref)
     normalise(received_ref, flags_ref[0], z_ref, held)
     if layer == 0:
-        (rest_ref,) = rest_ref
-        for row, block in branch_blocks(held, wout_ref.at[layer]):
+        rest_ref, packed_ref = more
+        packed_ref[0] = win_ref[0]
+        packed_ref[1] = wout_ref[0]
+        for row, block in branch_blocks(held, ending_ref):
             before = u_ref[row]
             after = before + STEP_SIZE * block
             unew_ref[row] = after
@@ -187,16 +180,18 @@
             coarse = before + FACTOR * STEP_SIZE * block
             rest_ref[row] = coarse - (before + FACTOR * (after - before))
     else:
-        add_branch(held, wout_ref.at[layer], STEP_SIZE, u_ref, unew_ref)
-    into_conv(held, win_ref.at[layer + 1], znew_ref, send_ref)
+        add_branch(held, ending_ref, STEP_SIZE, u_ref, unew_ref)
+    split_weights(win_ref, layer + 1, begun_ref)
+    into_conv(held, begun_ref, znew_ref, send_ref)
 
 
 def turn_kernel(
-    flags_ref, received_ref, z_ref, u_ref, wout_ref, moved_ref, both_ref, ends_ref, send_ref, high_ref, low_ref, weights_ref
+    flags_ref, received_ref, z_ref, u_ref, wout_ref, moved_ref, both_ref, ends_ref, send_ref, high_ref, low_ref, ending_ref, weights_ref
 ):
     held = (high_ref, low_ref)
+    split_weights(wout_ref, FACTOR - 1, ending_ref)
     normalise(received_ref, flags_ref[0], z_ref, held)
-    for row, block in branch_blocks(held, wout_ref.at[FACTOR - 1]):
+    for row, block in branch_blocks(held, ending_ref):
         after = u_ref[row] + STEP_SIZE * block
         both_ref[0, row] = after
         ends_ref[row] = after
@@ -210,7 +205,7 @@
 
 def fork_kernel(
     flags_ref, received_ref, arrived_ref, both_ref, rest_ref, wout_ref, win_ref, moved_ref,
-    unew_ref, znew_ref, send_ref, high_ref, low_ref, weights_ref,
+    unew_ref, znew_ref, send_ref, high_ref, low_ref, ending_ref, weights_ref,
 ):
     held = (high_ref, low_ref)
 
@@ -226,14 +221,16 @@
 
     @pl.when(flags_ref[1] == 0)
     def _():
+        split_weights(wout_ref, 0, ending_ref)
         normalise(received_ref, 0, arrived_ref.at[1], held)
-        add_branch(held, wout_ref.at[0], STEP_SIZE, arrived_ref.at[0], unew_ref)
-        into_conv(held, win_ref.at[1], znew_ref, send_ref)
+        add_branch(held, ending_ref, STEP_SIZE, arrived_ref.at[0], unew_ref)
+        split_weights(win_ref, 1, weights_ref)
+        into_conv(held, weights_ref, znew_ref, send_ref)
 
 
 def coarse_kernel(
     flags_ref, received_ref, z_ref, u_ref, wout_ref, win_ref, moved_ref,
-    unew_ref, znew_ref, send_ref, high_ref, low_ref, weights_ref,
+    unew_ref, znew_ref, send_ref, high_ref, low_ref, ending_ref, weights_ref,
 ):
     held = (high_ref, low_ref)
     normalise(received_ref, flags_ref[0], z_ref, held)
@@ -245,8 +242,10 @@
 
     @pl.when(flags_ref[1] == 0)
     def _():
-        add_branch(held, wout_ref.at[1], STEP_SIZE, u_ref, unew_ref)
-        into_conv(held, win_ref.at[2], znew_ref, send_ref)
+        split_weights(wout_ref, 1, ending_ref)
+        add_branch(held, ending_ref, STEP_SIZE, u_ref, unew_ref)
+        split_weights(win_ref, 2, weights_ref)
+        into_conv(held, weights_ref, znew_ref, send_ref)
 
 
 def second_kernel(flags_ref, *refs):
@@ -264,8 +263,10 @@
 
     @pl.when(flags_ref[1] == 0)
     def _():
-        normalise(received_ref, flags_ref[0], z_ref, held)
-        for row, block in branch_blocks(held, wout_ref.at[FACTOR - 1]):
+        *states, weights_ref = held
+        split_weights(wout_ref, FACTOR - 1, weights_ref)
+        normalise(received_ref, flags_ref[0], z_ref, states)
+        for row, block in branch_blocks(states, weights_ref):
             fine = u_ref[row] + STEP_SIZE * block
             begun, first = arrived_ref[0, row], first_ref[row]
             tau = fine - (begun + FACTOR * (first - begun))
@@ -278,6 +279,8 @@
 VMEM = pl.BlockSpec(memory_space=pltpu.VMEM)
 HELD = [pltpu.VMEM(((PAIRS + 1) * COLS, 2 * CHANNELS), jnp.bfloat16)] * 2
 WEIGHTS = [pltpu.VMEM((2, 3, 3, CHANNELS, CHANNELS), jnp.bfloat16)]
+ONE = HELD + WEIGHTS
+TWO = HELD + WEIGHTS * 2
 CONV_FLOPS = 2 * 3 * 512 * 1536 * 256
 
 
@@ -297,30 +300,25 @@
     )(*args)
 
 
-def load(flags, conv_in, conv_out):
-    layers = conv_in.shape[0]
+def ready(flags, initial, conv_in):
     shape = conv_in.shape[1:]
-    ready = jax.ShapeDtypeStruct((layers, 2) + shape, jnp.bfloat16)
-    packed = jax.ShapeDtypeStruct((2,) + shape, jnp.float32)
     return pl.pallas_call(
-        functools.partial(load_kernel, layers),
-        name="load",
-        out_shape=(ready, ready, packed),
+        ready_kernel,
+        name="ready",
+        out_shape=(STATE, jax.ShapeDtypeStruct((2,) + shape, jnp.bfloat16)),
         in_specs=[SMEM] + [pl.BlockSpec(memory_space=pltpu.HBM)] * 2,
-        out_specs=(VMEM,) * 3,
+        out_specs=(VMEM,) * 2,
         scratch_shapes=[
-            pltpu.VMEM((2 * layers,) + shape, jnp.float32),
-            pltpu.SemaphoreType.DMA((2 * layers,)),
+            pltpu.VMEM((1,) + shape, jnp.float32),
+            pltpu.SemaphoreType.DMA((2,)),
         ],
-        compiler_params=pltpu.CompilerParams(vmem_limit_bytes=VMEM_LIMIT),
-        cost_estimate=pl.CostEstimate(
-            flops=1000, bytes_accessed=4 * conv_in.size * 4, transcendentals=0
-        ),
-    )(flags, conv_in, conv_out)
-
-
-def handed(x, pairs):
-    return lax.ppermute(x, "depth", pairs)
+        compiler_params=pltpu.CompilerParams(vmem_limit_bytes=READY_LIMIT),
+        cost_estimate=pl.CostEstimate(flops=1000, bytes_accessed=3000000, transcendentals=0),
+    )(flags, *(pltpu.with_memory_space_constraint(x, pltpu.HBM) for x in (initial, conv_in)))
+
+
+def swapped(x):
+    return lax.ppermute(x, "depth", [(0, 1), (1, 0)])
 
 
 def exchange(send):
@@ -334,47 +332,47 @@
     flags = jnp.stack([position * (devices // 2), 1 - position]).astype(jnp.int32)
     outs = (STATE, STATE, sent)
 
-    before = handed(guess[0, 0], [(0, 1)])
-    ready_in, ready_out, packed = load(flags, conv_in, conv_out)
-    moved = handed(packed, [(1, 0)])
-    z, u, send = call(open_kernel, "open", outs, 1, HELD, flags, initial[0], before, ready_in)
-    send, moved = lax.optimization_barrier((send, moved))
-    received = exchange(send)
-    u, z, send, rest = call(
-        functools.partial(step_kernel, 0), "step", outs + (STATE,), 2, HELD,
-        flags, received, z, u, ready_out, ready_in,
-    )
+    before = swapped(guess[0, 0])
+    held, weights = ready(flags, initial[0], conv_in)
+    z, u, send = call(open_kernel, "open", outs, 1, HELD, flags, held, before, weights)
+    received = exchange(send)
+    packed = jax.ShapeDtypeStruct((2,) + conv_in.shape[1:], jnp.float32)
+    u, z, send, rest, packed = call(
+        functools.partial(step_kernel, 0), "step", outs + (STATE, packed), 2, TWO,
+        flags, received, z, u, conv_out, conv_in,
+    )
+    moved = swapped(packed)
     received = exchange(send)
     for layer in (1, 2):
         u, z, send = call(
-            functools.partial(step_kernel, layer), "step", outs, 2, HELD,
-            flags, received, z, u, ready_out, ready_in,
+            functools.partial(step_kernel, layer), "step", outs, 2, TWO,
+            flags, received, z, u, conv_out, conv_in,
         )
         received = exchange(send)
     both, ends, send = call(
-        turn_kernel, "turn", (BOTH, STATE, sent), 2, HELD + WEIGHTS,
-        flags, received, z, u, ready_out, moved,
-    )
-    arrived = handed(both, [(0, 1)])
+        turn_kernel, "turn", (BOTH, STATE, sent), 2, TWO,
+        flags, received, z, u, conv_out, moved,
+    )
+    arrived = swapped(both)
     received = exchange(send)
     first, z, send = call(
-        fork_kernel, "fork", outs, 2, HELD + WEIGHTS,
-        flags, received, arrived, both, rest, ready_out, ready_in, moved,
+        fork_kernel, "fork", outs, 2, TWO,
+        flags, received, arrived, both, rest, conv_out, conv_in, moved,
     )
     received = exchange(send)
     u, z, send = call(
-        coarse_kernel, "coarse", outs, 2, HELD + WEIGHTS,
-        flags, received, z, first, ready_out, ready_in, moved,
-    )
-    coarse = handed(u, [(0, 1)])
+        coarse_kernel, "coarse", outs, 2, TWO,
+        flags, received, z, first, conv_out, conv_in, moved,
+    )
+    coarse = swapped(u)
     received = exchange(send)
     u, z, send = call(
-        second_kernel, "second", outs, 2, HELD, flags, received, z, u, ready_out, ready_in
+        second_kernel, "second", outs, 2, TWO, flags, received, z, u, conv_out, conv_in
     )
     received = exchange(send)
     (result,) = call(
-        close_kernel, "close", (STATE,), 1, HELD,
-        flags, received, z, u, ready_out, arrived, first, coarse,
+        close_kernel, "close", (STATE,), 1, ONE,
+        flags, received, z, u, conv_out, arrived, first, coarse,
     )
     return (result[None, None], ends[None, None])
 

time: 169 us -> 157 us (0.929)
  local copies, waits for them, and re-layouts: 3.34 us -> 0.01 us
  blocking collectives: 117 us -> 114 us
  starting transfers between devices: 7.26 us -> 4.36 us
  waiting for transfers between devices: 2.51 us -> 0.01 us
    unnamed x8 -> x4, local copies, waits for them, and re-layouts: 3.34 us -> 0.01 us
    all_to_all x8, blocking collectives: 117 us -> 114 us  [exchange(): return lax.all_to_all(send, WORLD, 0, 0)]
    ppermute x4, starting transfers between devices: 7.26 us -> 4.36 us  [swapped(): return lax.ppermute(x, 'depth', [(0, 1), (1, 0)])]
    ppermute x4, waiting for transfers between devices: 2.51 us -> 0.01 us  [swapped(): return lax.ppermute(x, 'depth', [(0, 1), (1, 0)])]
  transfers between devices with their start and end apart: 4 -> 4, of which waited for: 1 -> 0; matrix products, arithmetic and copies ran while one was open for 0% -> 0% of each run, Pallas kernels for 4% -> 10%
where the time goes in v3:
time: 157 us
  blocking collectives  114 us (73%)
  Pallas kernels  37.4 us (24%)
  starting transfers between devices  4.36 us (3%)
    all_to_all x8, blocking collectives, exchange(): return lax.all_to_all(send, WORLD, 0, 0)  114 us
    pallas_call x9, Pallas kernels, call(): pl.pallas_call(kernel, name=name, out_shape=tuple(outs), in_specs=[SMEM]...  35.6 us
    ppermute x4, starting transfers between devices, swapped(): return lax.ppermute(x, 'depth', [(0, 1), (1, 0)])  4.36 us
  transfers between devices with their start and end apart: 4, of which 0 were waited for; matrix products, arithmetic and copies ran while one was open for 0% of the time, Pallas kernels for 10%

profile of v3, /device:TPU:1, one launch (start us, length us, event | category | flops | bytes accessed | tf_op | source)
XLA Modules:
  0.0 156.8 jit_solution(1481201377279440162)
XLA Ops:
  0.6 1.5 collective-permute-start
  2.1 0.1 pad_add_fusion.flags_ref
  2.2 1.8 %ready.1 = (f32[32,32,128]{2,1,0:T(8,128)S(1)}, bf16[2,3,3,128,128]{4,3,2,1,0:T(8,128)(2,1)S(1)}) custom-call(s32[2]{0:T(128)S(1)} %pad_add_fusion.flags_ref, f32[32,32,128]{2,1,0:T(8,128)} %bitcast.7, f32[4,3,3,128,128]{4,3,2,1,0:T(8,128)} %refs_4_.1), custom_call_target="tpu_custom_call" | custom-call | flops 1000 | bytes 3000000 | tf_op jit(solution)/shard_map/ready/pallas_call | solution.py:305
  4.0 0.0 copy-start
  4.0 2.1 %open.1 = (f32[32,32,128]{2,1,0:T(8,128)S(1)}, f32[32,32,128]{2,1,0:T(8,128)S(1)}, f32[128,2,128]{2,1,0:T(2,128)S(1)}) custom-call(s32[2]{0:T(128)S(1)} %pad_add_fusion.flags_ref, f32[32,32,128]{2,1,0:T(8,128)S(1)} %get-tuple-element.30.initial_ref, f32[32,32,128]{2,1,0:T(8,128)S(1)} %collective-permute-done.before_ref, ...), custom_call_target="tpu_custom_call" | custom-call | flops 1207959552 | bytes 2818056 | tf_op jit(solution)/shard_map/open/pallas_call | solution.py:289
  6.1 20.1 %all_to_all.40.received_ref = f32[128,2,128]{2,1,0:T(2,128)S(1)} all-to-all(f32[128,2,128]{2,1,0:T(2,128)S(1)} %get-tuple-element.32), channel_id=1, replica_groups=mesh['depth'=2,'batch_0'=4,'batch_1'=4,'batch_2'=4] {'depth','batch_0','..., dimensions={0} | all-to-all | bytes 262144 | tf_op jit(solution)/shard_map/all_to_all | solution.py:325
  26.3 4.6 %step.3 = (f32[32,32,128]{2,1,0:T(8,128)S(1)}, f32[32,32,128]{2,1,0:T(8,128)S(1)}, f32[128,2,128]{2,1,0:T(2,128)S(1)}, f32[32,32,128]{2,1,0:T(8,128)S(1)}, f32[2,3,3,128,128]{4,3,2,1,0:T(8,128)S(1)}) custom-call(s32[2]{0:T(128)S(1)} %pad_add_fusion.flags_ref, f32[128,2,128]{2,1,0:T(2,128)S(1)} %all_to_all.40.received_ref, ...), custom_call_target="tpu_custom_call" | custom-call | flops 2415919104 | bytes 8781832 | tf_op jit(solution)/shard_map/step/pallas_call | solution.py:289
  30.9 0.6 collective-permute-start.1
  31.6 13.2 %all_to_all.41.received_ref = f32[128,2,128]{2,1,0:T(2,128)S(1)} all-to-all(f32[128,2,128]{2,1,0:T(2,128)S(1)} %get-tuple-element.35), channel_id=1, replica_groups=mesh['depth'=2,'batch_0'=4,'batch_1'=4,'batch_2'=4] {'depth','batch_0','..., dimensions={0} | all-to-all | bytes 262144 | tf_op jit(solution)/shard_map/all_to_all | solution.py:325
  44.8 4.5 %step.4 = (f32[32,32,128]{2,1,0:T(8,128)S(1)}, f32[32,32,128]{2,1,0:T(8,128)S(1)}, f32[128,2,128]{2,1,0:T(2,128)S(1)}) custom-call(s32[2]{0:T(128)S(1)} %pad_add_fusion.flags_ref, f32[128,2,128]{2,1,0:T(2,128)S(1)} %all_to_all.41.received_ref, f32[32,32,128]{2,1,0:T(8,128)S(1)} %get-tuple-element.36.z_ref, f32[32,32,128]{2,1,0:T(8,128)S(1)} %get-tuple-element.37.u_ref, ...), custom_call_target="tpu_custom_call" | custom-call | flops 2415919104 | bytes 7077896 | tf_op jit(solution)/shard_map/step/pallas_call | solution.py:289
  49.3 13.7 %all_to_all.42.received_ref = f32[128,2,128]{2,1,0:T(2,128)S(1)} all-to-all(f32[128,2,128]{2,1,0:T(2,128)S(1)} %get-tuple-element.38), channel_id=1, replica_groups=mesh['depth'=2,'batch_0'=4,'batch_1'=4,'batch_2'=4] {'depth','batch_0','..., dimensions={0} | all-to-all | bytes 262144 | tf_op jit(solution)/shard_map/all_to_all | solution.py:325
  62.9 4.5 %step.5 = (f32[32,32,128]{2,1,0:T(8,128)S(1)}, f32[32,32,128]{2,1,0:T(8,128)S(1)}, f32[128,2,128]{2,1,0:T(2,128)S(1)}) custom-call(s32[2]{0:T(128)S(1)} %pad_add_fusion.flags_ref, f32[128,2,128]{2,1,0:T(2,128)S(1)} %all_to_all.42.received_ref, f32[32,32,128]{2,1,0:T(8,128)S(1)} %get-tuple-element.39.z_ref, f32[32,32,128]{2,1,0:T(8,128)S(1)} %get-tuple-element.40.u_ref, ...), custom_call_target="tpu_custom_call" | custom-call | flops 2415919104 | bytes 7077896 | tf_op jit(solution)/shard_map/step/pallas_call | solution.py:289
  67.4 13.7 %all_to_all.43.received_ref = f32[128,2,128]{2,1,0:T(2,128)S(1)} all-to-all(f32[128,2,128]{2,1,0:T(2,128)S(1)} %get-tuple-element.41), channel_id=1, replica_groups=mesh['depth'=2,'batch_0'=4,'batch_1'=4,'batch_2'=4] {'depth','batch_0','..., dimensions={0} | all-to-all | bytes 262144 | tf_op jit(solution)/shard_map/all_to_all | solution.py:325
  81.1 3.0 %turn.1 = (f32[2,32,32,128]{3,2,1,0:T(8,128)S(1)}, f32[32,32,128]{2,1,0:T(8,128)}, f32[128,2,128]{2,1,0:T(2,128)S(1)}) custom-call(s32[2]{0:T(128)S(1)} %pad_add_fusion.flags_ref, f32[128,2,128]{2,1,0:T(2,128)S(1)} %all_to_all.43.received_ref, f32[32,32,128]{2,1,0:T(8,128)S(1)} %get-tuple-element.42.z_ref, f32[32,32,128]{2,1,0:T(8,128)S(1)} %get-tuple-element.43.u_ref, ...), custom_call_target="tpu_custom_call" | custom-call | flops 2415919104 | bytes 6422536 | tf_op jit(solution)/shard_map/turn/pallas_call | solution.py:289
  84.1 2.1 %collective-permute-start.2 = (f32[2,32,32,128]{3,2,1,0:T(8,128)S(1)}, f32[2,32,32,128]{3,2,1,0:T(8,128)S(1)}, u32[]{:S(2)}, u32[]{:S(2)}) collective-permute-start(f32[2,32,32,128]{3,2,1,0:T(8,128)S(1)} %get-tuple-element.46.both_ref), channel_id=1, source_target_pairs={{0,64},{64,0},{1,65},{65,1},{2,66},{66,2},{3,67},{67,3},{4,68},{68... | collective-permute-start | bytes 3145736 | tf_op jit(solution)/shard_map/ppermute | solution.py:321
  86.3 13.2 %all_to_all.44.received_ref = f32[128,2,128]{2,1,0:T(2,128)S(1)} all-to-all(f32[128,2,128]{2,1,0:T(2,128)S(1)} %get-tuple-element.45), channel_id=1, replica_groups=mesh['depth'=2,'batch_0'=4,'batch_1'=4,'batch_2'=4] {'depth','batch_0','..., dimensions={0} | all-to-all | bytes 262144 | tf_op jit(solution)/shard_map/all_to_all | solution.py:325
  99.5 4.5 %fork.1 = (f32[32,32,128]{2,1,0:T(8,128)S(1)}, f32[32,32,128]{2,1,0:T(8,128)S(1)}, f32[128,2,128]{2,1,0:T(2,128)S(1)}) custom-call(s32[2]{0:T(128)S(1)} %pad_add_fusion.flags_ref, f32[128,2,128]{2,1,0:T(2,128)S(1)} %all_to_all.44.received_ref, f32[2,32,32,128]{3,2,1,0:T(8,128)S(1)} %collective-permute-done.2.arrived_ref, ...), custom_call_target="tpu_custom_call" | custom-call | flops 2415919104 | bytes 9830408 | tf_op jit(solution)/shard_map/fork/pallas_call | solution.py:289
  104.0 13.3 %all_to_all.45.received_ref = f32[128,2,128]{2,1,0:T(2,128)S(1)} all-to-all(f32[128,2,128]{2,1,0:T(2,128)S(1)} %get-tuple-element.48), channel_id=1, replica_groups=mesh['depth'=2,'batch_0'=4,'batch_1'=4,'batch_2'=4] {'depth','batch_0','..., dimensions={0} | all-to-all | bytes 262144 | tf_op jit(solution)/shard_map/all_to_all | solution.py:325
  117.3 4.8 %coarse.1 = (f32[32,32,128]{2,1,0:T(8,128)S(1)}, f32[32,32,128]{2,1,0:T(8,128)S(1)}, f32[128,2,128]{2,1,0:T(2,128)S(1)}) custom-call(s32[2]{0:T(128)S(1)} %pad_add_fusion.flags_ref, f32[128,2,128]{2,1,0:T(2,128)S(1)} %all_to_all.45.received_ref, f32[32,32,128]{2,1,0:T(8,128)S(1)} %get-tuple-element.49.z_ref, ...), custom_call_target="tpu_custom_call" | custom-call | flops 2415919104 | bytes 8257544 | tf_op jit(solution)/shard_map/coarse/pallas_call | solution.py:289
  122.1 0.1 collective-permute-start.3
  122.2 13.7 %all_to_all.46.refs_0_ = f32[128,2,128]{2,1,0:T(2,128)S(1)} all-to-all(f32[128,2,128]{2,1,0:T(2,128)S(1)} %get-tuple-element.51), channel_id=1, replica_groups=mesh['depth'=2,'batch_0'=4,'batch_1'=4,'batch_2'=4] {'depth','batch_0','..., dimensions={0} | all-to-all | bytes 262144 | tf_op jit(solution)/shard_map/all_to_all | solution.py:325
  135.9 4.5 %second.1 = (f32[32,32,128]{2,1,0:T(8,128)S(1)}, f32[32,32,128]{2,1,0:T(8,128)S(1)}, f32[128,2,128]{2,1,0:T(2,128)S(1)}) custom-call(s32[2]{0:T(128)S(1)} %pad_add_fusion.flags_ref, f32[128,2,128]{2,1,0:T(2,128)S(1)} %all_to_all.46.refs_0_, f32[32,32,128]{2,1,0:T(8,128)S(1)} %get-tuple-element.52.refs_1_, f32[32,32,128]{2,1,0:T(8,128)S(1)} %get-tuple-element.53.refs_2_, ...), custom_call_target="tpu_custom_call" | custom-call | flops 2415919104 | bytes 7077896 | tf_op jit(solution)/shard_map/second/pallas_call | solution.py:289
  140.4 13.3 %all_to_all.47.received_ref = f32[128,2,128]{2,1,0:T(2,128)S(1)} all-to-all(f32[128,2,128]{2,1,0:T(2,128)S(1)} %get-tuple-element.54), channel_id=1, replica_groups=mesh['depth'=2,'batch_0'=4,'batch_1'=4,'batch_2'=4] {'depth','batch_0','..., dimensions={0} | all-to-all | bytes 262144 | tf_op jit(solution)/shard_map/all_to_all | solution.py:325
  153.7 3.0 %close.1 = f32[32,32,128]{2,1,0:T(8,128)} custom-call(s32[2]{0:T(128)S(1)} %pad_add_fusion.flags_ref, f32[128,2,128]{2,1,0:T(2,128)S(1)} %all_to_all.47.received_ref, f32[32,32,128]{2,1,0:T(8,128)S(1)} %get-tuple-element.55.z_ref, f32[32,32,128]{2,1,0:T(8,128)S(1)} %get-tuple-element.56.u_ref, f32[4,3,3,128,128]{4,3,2,1,0:T(8,128)S(1)} %copy-done, ...), custom_call_target="tpu_custom_call" | custom-call | flops 1207959552 | bytes 6160392 | tf_op jit(solution)/shard_map/close/pallas_call | solution.py:289
  (7 shorter events, 0.0 us)
Async XLA Ops:
  0.6 3.4 %collective-permute-start = (f32[32,32,128]{2,1,0:T(8,128)}, f32[32,32,128]{2,1,0:T(8,128)S(1)}, u32[]{:S(2)}, u32[]{:S(2)}) collective-permute-start(f32[32,32,128]{2,1,0:T(8,128)} %bitcast.8), channel_id=1, source_target_pairs={{0,64},{64,0},{1,65},{65,1},{2,66},{66,2},{3,67},{67,3},{4,68},{68... | collective-permute-start | bytes 1572872 | tf_op jit(solution)/shard_map/ppermute | solution.py:321
  4.0 22.3 %copy-start = (f32[4,3,3,128,128]{4,3,2,1,0:T(8,128)S(1)}, f32[4,3,3,128,128]{4,3,2,1,0:T(8,128)}, u32[]{:S(2)}) copy-start(f32[4,3,3,128,128]{4,3,2,1,0:T(8,128)} %wout_ref.13) | copy-start | bytes 7077892
  4.0 22.3 %copy-start.1 = (f32[4,3,3,128,128]{4,3,2,1,0:T(8,128)S(1)}, f32[4,3,3,128,128]{4,3,2,1,0:T(8,128)}, u32[]{:S(2)}) copy-start(f32[4,3,3,128,128]{4,3,2,1,0:T(8,128)} %refs_4_.1) | copy-start | bytes 7077892
  30.9 50.2 %collective-permute-start.1 = (f32[2,3,3,128,128]{4,3,2,1,0:T(8,128)S(1)}, f32[2,3,3,128,128]{4,3,2,1,0:T(8,128)S(1)}, u32[]{:S(2)}, u32[]{:S(2)}) collective-permute-start(f32[2,3,3,128,128]{4,3,2,1,0:T(8,128)S(1)} %get-tuple-element.44), channel_id=1, source_target_pairs={{0,64},{64,0},{1,65},{65,1},{2,66},{66,2},{3,67},{67,3},{4,68},{68... | collective-permute-start | bytes 3538952 | tf_op jit(solution)/shard_map/ppermute | solution.py:321
  84.1 15.4 %collective-permute-start.2 = (f32[2,32,32,128]{3,2,1,0:T(8,128)S(1)}, f32[2,32,32,128]{3,2,1,0:T(8,128)S(1)}, u32[]{:S(2)}, u32[]{:S(2)}) collective-permute-start(f32[2,32,32,128]{3,2,1,0:T(8,128)S(1)} %get-tuple-element.46.both_ref), channel_id=1, source_target_pairs={{0,64},{64,0},{1,65},{65,1},{2,66},{66,2},{3,67},{67,3},{4,68},{68... | collective-permute-start | bytes 3145736 | tf_op jit(solution)/shard_map/ppermute | solution.py:321
  122.1 31.6 %collective-permute-start.3 = (f32[32,32,128]{2,1,0:T(8,128)S(1)}, f32[32,32,128]{2,1,0:T(8,128)S(1)}, u32[]{:S(2)}, u32[]{:S(2)}) collective-permute-start(f32[32,32,128]{2,1,0:T(8,128)S(1)} %get-tuple-element.53.refs_2_), channel_id=1, source_target_pairs={{0,64},{64,0},{1,65},{65,1},{2,66},{66,2},{3,67},{67,3},{4,68},{68... | collective-permute-start | bytes 1572872 | tf_op jit(solution)/shard_map/ppermute | solution.py:321

commit v4 on v3

--- a/solution.py
+++ b/solution.py
@@ -20,6 +20,8 @@
 CHANNELS = 128
 PAIRS = ROWS // 2
 CELLS = ROWS * COLS
+CHUNKS = 2
+PART = PAIRS // CHUNKS
 VMEM_LIMIT = 24 * 2**20
 READY_LIMIT = 24 * 2**20
 
@@ -45,10 +47,11 @@
         ref[PAIRS * COLS : (PAIRS + 1) * COLS, CHANNELS:] = zeros
 
 
-def convolve(high_ref, low_ref, weights):
-    many = PAIRS * COLS
-    high0, high1 = high_ref[0:many, :], high_ref[COLS : COLS + many, :]
-    low0, low1 = low_ref[0:many, :], low_ref[COLS : COLS + many, :]
+def convolve(high_ref, low_ref, weights, chunk):
+    many = PART * COLS
+    at = chunk * many
+    high0, high1 = high_ref[at : at + many, :], high_ref[at + COLS : at + COLS + many, :]
+    low0, low1 = low_ref[at : at + many, :], low_ref[at + COLS : at + COLS + many, :]
     left = jnp.concatenate([high0, high1, low0, low1, high0, high1], axis=1)
     zeros = jnp.zeros((CHANNELS, CHANNELS), jnp.bfloat16)
 
@@ -67,25 +70,36 @@
     return out + jnp.where(column == COLS - 1, 0.0, pltpu.roll(part(2), many - 1, 0))
 
 
-def pair_rows(out, pair):
-    block = out[pair * COLS : (pair + 1) * COLS, :]
-    return block[:, :CHANNELS], block[:, CHANNELS:]
-
-
-def fold(x):
-    total = jnp.sum(x, axis=0, keepdims=True)
-    return total[:, :CHANNELS] + total[:, CHANNELS:]
-
-
-def statistics(out):
-    total = fold(out)
-    own = total * (1.0 / CELLS)
-    away = out - jnp.concatenate([own, own], axis=1)
-    return total, fold(away * away)
-
-
-def emit_statistics(out, send_ref):
-    both = jnp.concatenate(statistics(out), axis=0)
+def branch_blocks(held, weights):
+    for chunk in range(CHUNKS):
+        out = convolve(*held, weights, chunk)
+        for pair in range(PART):
+            block = out[pair * COLS : (pair + 1) * COLS, :]
+            row = 2 * (chunk * PART + pair)
+            yield row, block[:, :CHANNELS]
+            yield row + 1, block[:, CHANNELS:]
+
+
+def into_conv(held, weights, z_ref, send_ref):
+    totals, squares = [], []
+    for chunk in range(CHUNKS):
+        out = convolve(*held, weights, chunk)
+        for pair in range(PART):
+            block = out[pair * COLS : (pair + 1) * COLS, :]
+            row = 2 * (chunk * PART + pair)
+            z_ref[row], z_ref[row + 1] = block[:, :CHANNELS], block[:, CHANNELS:]
+        total = jnp.sum(out, axis=0, keepdims=True)
+        away = out - total * (1.0 / (PART * COLS))
+        square = jnp.sum(away * away, axis=0, keepdims=True)
+        for half in range(2):
+            totals.append(total[:, half * CHANNELS : (half + 1) * CHANNELS])
+            squares.append(square[:, half * CHANNELS : (half + 1) * CHANNELS])
+    total = functools.reduce(jnp.add, totals)
+    square = functools.reduce(jnp.add, squares)
+    for part in totals:
+        away = part * (1.0 / (PART * COLS)) - total * (1.0 / CELLS)
+        square = square + (PART * COLS) * (away * away)
+    both = jnp.concatenate([total, square], axis=0)
     send_ref[...] = jnp.broadcast_to(both[None], send_ref.shape)
 
 
@@ -106,26 +120,14 @@
         place(row, jnp.maximum((z_ref[row] - average) * factor, 0.0), *held)
 
 
-def into_conv(held, weights, z_ref, send_ref):
-    out = convolve(*held, weights)
-    for pair in range(PAIRS):
-        z_ref[2 * pair], z_ref[2 * pair + 1] = pair_rows(out, pair)
-    emit_statistics(out, send_ref)
-
-
-def branch_blocks(held, weights):
-    out = convolve(*held, weights)
-    for pair in range(PAIRS):
-        for half, block in enumerate(pair_rows(out, pair)):
-            yield 2 * pair + half, block
-
-
-def add_branch(held, weights, scale, u_ref, unew_ref, again=True):
+def add_branch(held, weights, scale, u_ref, unew_ref, onto=None):
+    if onto is not None:
+        clear_edges(*onto)
     for row, block in branch_blocks(held, weights):
         after = u_ref[row] + scale * block
         unew_ref[row] = after
-        if again:
-            place(row, after, *held)
+        if onto is not None:
+            place(row, after, *onto)
 
 
 def split_weights(raw_ref, at, weights_ref):
@@ -164,50 +166,52 @@
 def step_kernel(
     layer, flags_ref, received_ref, z_ref, u_ref, wout_ref, win_ref, unew_ref, znew_ref, send_ref, *refs
 ):
-    *more, high_ref, low_ref, ending_ref, begun_ref = refs
-    held = (high_ref, low_ref)
+    *more, high_ref, low_ref, high2_ref, low2_ref, ending_ref, begun_ref = refs
+    held, onto = (high_ref, low_ref), (high2_ref, low2_ref)
     split_weights(wout_ref, layer, ending_ref)
     normalise(received_ref, flags_ref[0], z_ref, held)
     if layer == 0:
         rest_ref, packed_ref = more
         packed_ref[0] = win_ref[0]
         packed_ref[1] = wout_ref[0]
+        clear_edges(*onto)
         for row, block in branch_blocks(held, ending_ref):
             before = u_ref[row]
             after = before + STEP_SIZE * block
             unew_ref[row] = after
-            place(row, after, *held)
+            place(row, after, *onto)
             coarse = before + FACTOR * STEP_SIZE * block
             rest_ref[row] = coarse - (before + FACTOR * (after - before))
     else:
-        add_branch(held, ending_ref, STEP_SIZE, u_ref, unew_ref)
+        add_branch(held, ending_ref, STEP_SIZE, u_ref, unew_ref, onto)
     split_weights(win_ref, layer + 1, begun_ref)
-    into_conv(held, begun_ref, znew_ref, send_ref)
+    into_conv(onto, begun_ref, znew_ref, send_ref)
 
 
 def turn_kernel(
-    flags_ref, received_ref, z_ref, u_ref, wout_ref, moved_ref, both_ref, ends_ref, send_ref, high_ref, low_ref, ending_ref, weights_ref
+    flags_ref, received_ref, z_ref, u_ref, wout_ref, moved_ref, both_ref, ends_ref, send_ref, high_ref, low_ref, high2_ref, low2_ref, ending_ref, weights_ref
 ):
-    held = (high_ref, low_ref)
+    held, onto = (high_ref, low_ref), (high2_ref, low2_ref)
+    clear_edges(*onto)
     split_weights(wout_ref, FACTOR - 1, ending_ref)
     normalise(received_ref, flags_ref[0], z_ref, held)
     for row, block in branch_blocks(held, ending_ref):
         after = u_ref[row] + STEP_SIZE * block
         both_ref[0, row] = after
         ends_ref[row] = after
-        place(row, after, *held)
+        place(row, after, *onto)
 
     @pl.when(flags_ref[1] == 1)
     def _():
         split_weights(moved_ref, 0, weights_ref)
-        into_conv(held, weights_ref, both_ref.at[1], send_ref)
+        into_conv(onto, weights_ref, both_ref.at[1], send_ref)
 
 
 def fork_kernel(
     flags_ref, received_ref, arrived_ref, both_ref, rest_ref, wout_ref, win_ref, moved_ref,
-    unew_ref, znew_ref, send_ref, high_ref, low_ref, ending_ref, weights_ref,
+    unew_ref, znew_ref, send_ref, high_ref, low_ref, high2_ref, low2_ref, ending_ref, weights_ref,
 ):
-    held = (high_ref, low_ref)
+    held, onto = (high_ref, low_ref), (high2_ref, low2_ref)
 
     @pl.when(flags_ref[1] == 1)
     def _():
@@ -223,29 +227,29 @@
     def _():
         split_weights(wout_ref, 0, ending_ref)
         normalise(received_ref, 0, arrived_ref.at[1], held)
-        add_branch(held, ending_ref, STEP_SIZE, arrived_ref.at[0], unew_ref)
+        add_branch(held, ending_ref, STEP_SIZE, arrived_ref.at[0], unew_ref, onto)
         split_weights(win_ref, 1, weights_ref)
-        into_conv(held, weights_ref, znew_ref, send_ref)
+        into_conv(onto, weights_ref, znew_ref, send_ref)
 
 
 def coarse_kernel(
     flags_ref, received_ref, z_ref, u_ref, wout_ref, win_ref, moved_ref,
-    unew_ref, znew_ref, send_ref, high_ref, low_ref, ending_ref, weights_ref,
+    unew_ref, znew_ref, send_ref, high_ref, low_ref, high2_ref, low2_ref, ending_ref, weights_ref,
 ):
-    held = (high_ref, low_ref)
+    held, onto = (high_ref, low_ref), (high2_ref, low2_ref)
     normalise(received_ref, flags_ref[0], z_ref, held)
 
     @pl.when(flags_ref[1] == 1)
     def _():
         split_weights(moved_ref, 1, weights_ref)
-        add_branch(held, weights_ref, FACTOR * STEP_SIZE, u_ref, unew_ref, again=False)
+        add_branch(held, weights_ref, FACTOR * STEP_SIZE, u_ref, unew_ref)
 
     @pl.when(flags_ref[1] == 0)
     def _():
         split_weights(wout_ref, 1, ending_ref)
-        add_branch(held, ending_ref, STEP_SIZE, u_ref, unew_ref)
+        add_branch(held, ending_ref, STEP_SIZE, u_ref, unew_ref, onto)
         split_weights(win_ref, 2, weights_ref)
-        into_conv(held, weights_ref, znew_ref, send_ref)
+        into_conv(onto, weights_ref, znew_ref, send_ref)
 
 
 def second_kernel(flags_ref, *refs):
@@ -280,7 +284,7 @@
 HELD = [pltpu.VMEM(((PAIRS + 1) * COLS, 2 * CHANNELS), jnp.bfloat16)] * 2
 WEIGHTS = [pltpu.VMEM((2, 3, 3, CHANNELS, CHANNELS), jnp.bfloat16)]
 ONE = HELD + WEIGHTS
-TWO = HELD + WEIGHTS * 2
+TWO = HELD * 2 + WEIGHTS * 2
 CONV_FLOPS = 2 * 3 * 512 * 1536 * 256
 
 

time: 157 us -> 151 us (0.962)
  Pallas kernels: 37.4 us -> 31.8 us
    pallas_call x9, Pallas kernels: 35.6 us -> 30 us  [call(): pl.pallas_call(kernel, name=name, out_shape=tuple(outs), in_specs=[SMEM]...]
  transfers between devices with their start and end apart: 4 -> 4, of which waited for: 0 -> 0; matrix products, arithmetic and copies ran while one was open for 0% -> 0% of each run, Pallas kernels for 10% -> 8%
where the time goes in v4:
time: 151 us
  blocking collectives  114 us (75%)
  Pallas kernels  31.8 us (21%)
  starting transfers between devices  4.33 us (3%)
    all_to_all x8, blocking collectives, exchange(): return lax.all_to_all(send, WORLD, 0, 0)  114 us
    pallas_call x9, Pallas kernels, call(): pl.pallas_call(kernel, name=name, out_shape=tuple(outs), in_specs=[SMEM]...  30 us
    ppermute x4, starting transfers between devices, swapped(): return lax.ppermute(x, 'depth', [(0, 1), (1, 0)])  4.33 us
  transfers between devices with their start and end apart: 4, of which 0 were waited for; matrix products, arithmetic and copies ran while one was open for 0% of the time, Pallas kernels for 8%

profile of v4, /device:TPU:1, one launch (start us, length us, event | category | flops | bytes accessed | tf_op | source)
XLA Modules:
  0.0 151.1 jit_solution(4138469643695068783)
XLA Ops:
  0.6 1.5 collective-permute-start
  2.1 0.1 pad_add_fusion.flags_ref
  2.2 1.8 %ready.1 = (f32[32,32,128]{2,1,0:T(8,128)S(1)}, bf16[2,3,3,128,128]{4,3,2,1,0:T(8,128)(2,1)S(1)}) custom-call(s32[2]{0:T(128)S(1)} %pad_add_fusion.flags_ref, f32[32,32,128]{2,1,0:T(8,128)} %bitcast.7, f32[4,3,3,128,128]{4,3,2,1,0:T(8,128)} %refs_4_.1), custom_call_target="tpu_custom_call" | custom-call | flops 1000 | bytes 3000000 | tf_op jit(solution)/shard_map/ready/pallas_call | solution.py:309
  4.0 0.0 copy-start
  4.0 2.1 %open.1 = (f32[32,32,128]{2,1,0:T(8,128)S(1)}, f32[32,32,128]{2,1,0:T(8,128)S(1)}, f32[128,2,128]{2,1,0:T(2,128)S(1)}) custom-call(s32[2]{0:T(128)S(1)} %pad_add_fusion.flags_ref, f32[32,32,128]{2,1,0:T(8,128)S(1)} %get-tuple-element.30.initial_ref, f32[32,32,128]{2,1,0:T(8,128)S(1)} %collective-permute-done.before_ref, ...), custom_call_target="tpu_custom_call" | custom-call | flops 1207959552 | bytes 2818056 | tf_op jit(solution)/shard_map/open/pallas_call | solution.py:293
  6.1 20.1 %all_to_all.40.received_ref = f32[128,2,128]{2,1,0:T(2,128)S(1)} all-to-all(f32[128,2,128]{2,1,0:T(2,128)S(1)} %get-tuple-element.32), channel_id=1, replica_groups=mesh['depth'=2,'batch_0'=4,'batch_1'=4,'batch_2'=4] {'depth','batch_0','..., dimensions={0} | all-to-all | bytes 262144 | tf_op jit(solution)/shard_map/all_to_all | solution.py:329
  26.3 3.6 %step.3 = (f32[32,32,128]{2,1,0:T(8,128)S(1)}, f32[32,32,128]{2,1,0:T(8,128)S(1)}, f32[128,2,128]{2,1,0:T(2,128)S(1)}, f32[32,32,128]{2,1,0:T(8,128)S(1)}, f32[2,3,3,128,128]{4,3,2,1,0:T(8,128)S(1)}) custom-call(s32[2]{0:T(128)S(1)} %pad_add_fusion.flags_ref, f32[128,2,128]{2,1,0:T(2,128)S(1)} %all_to_all.40.received_ref, ...), custom_call_target="tpu_custom_call" | custom-call | flops 2415919104 | bytes 8781832 | tf_op jit(solution)/shard_map/step/pallas_call | solution.py:293
  29.9 0.6 collective-permute-start.1
  30.5 13.2 %all_to_all.41.received_ref = f32[128,2,128]{2,1,0:T(2,128)S(1)} all-to-all(f32[128,2,128]{2,1,0:T(2,128)S(1)} %get-tuple-element.35), channel_id=1, replica_groups=mesh['depth'=2,'batch_0'=4,'batch_1'=4,'batch_2'=4] {'depth','batch_0','..., dimensions={0} | all-to-all | bytes 262144 | tf_op jit(solution)/shard_map/all_to_all | solution.py:329
  43.8 3.6 %step.4 = (f32[32,32,128]{2,1,0:T(8,128)S(1)}, f32[32,32,128]{2,1,0:T(8,128)S(1)}, f32[128,2,128]{2,1,0:T(2,128)S(1)}) custom-call(s32[2]{0:T(128)S(1)} %pad_add_fusion.flags_ref, f32[128,2,128]{2,1,0:T(2,128)S(1)} %all_to_all.41.received_ref, f32[32,32,128]{2,1,0:T(8,128)S(1)} %get-tuple-element.36.z_ref, f32[32,32,128]{2,1,0:T(8,128)S(1)} %get-tuple-element.37.u_ref, ...), custom_call_target="tpu_custom_call" | custom-call | flops 2415919104 | bytes 7077896 | tf_op jit(solution)/shard_map/step/pallas_call | solution.py:293
  47.3 13.7 %all_to_all.42.received_ref = f32[128,2,128]{2,1,0:T(2,128)S(1)} all-to-all(f32[128,2,128]{2,1,0:T(2,128)S(1)} %get-tuple-element.38), channel_id=1, replica_groups=mesh['depth'=2,'batch_0'=4,'batch_1'=4,'batch_2'=4] {'depth','batch_0','..., dimensions={0} | all-to-all | bytes 262144 | tf_op jit(solution)/shard_map/all_to_all | solution.py:329
  61.0 3.6 %step.5 = (f32[32,32,128]{2,1,0:T(8,128)S(1)}, f32[32,32,128]{2,1,0:T(8,128)S(1)}, f32[128,2,128]{2,1,0:T(2,128)S(1)}) custom-call(s32[2]{0:T(128)S(1)} %pad_add_fusion.flags_ref, f32[128,2,128]{2,1,0:T(2,128)S(1)} %all_to_all.42.received_ref, f32[32,32,128]{2,1,0:T(8,128)S(1)} %get-tuple-element.39.z_ref, f32[32,32,128]{2,1,0:T(8,128)S(1)} %get-tuple-element.40.u_ref, ...), custom_call_target="tpu_custom_call" | custom-call | flops 2415919104 | bytes 7077896 | tf_op jit(solution)/shard_map/step/pallas_call | solution.py:293
  64.6 13.7 %all_to_all.43.received_ref = f32[128,2,128]{2,1,0:T(2,128)S(1)} all-to-all(f32[128,2,128]{2,1,0:T(2,128)S(1)} %get-tuple-element.41), channel_id=1, replica_groups=mesh['depth'=2,'batch_0'=4,'batch_1'=4,'batch_2'=4] {'depth','batch_0','..., dimensions={0} | all-to-all | bytes 262144 | tf_op jit(solution)/shard_map/all_to_all | solution.py:329
  78.2 3.0 %turn.1 = (f32[2,32,32,128]{3,2,1,0:T(8,128)S(1)}, f32[32,32,128]{2,1,0:T(8,128)}, f32[128,2,128]{2,1,0:T(2,128)S(1)}) custom-call(s32[2]{0:T(128)S(1)} %pad_add_fusion.flags_ref, f32[128,2,128]{2,1,0:T(2,128)S(1)} %all_to_all.43.received_ref, f32[32,32,128]{2,1,0:T(8,128)S(1)} %get-tuple-element.42.z_ref, f32[32,32,128]{2,1,0:T(8,128)S(1)} %get-tuple-element.43.u_ref, ...), custom_call_target="tpu_custom_call" | custom-call | flops 2415919104 | bytes 6422536 | tf_op jit(solution)/shard_map/turn/pallas_call | solution.py:293
  81.3 2.1 %collective-permute-start.2 = (f32[2,32,32,128]{3,2,1,0:T(8,128)S(1)}, f32[2,32,32,128]{3,2,1,0:T(8,128)S(1)}, u32[]{:S(2)}, u32[]{:S(2)}) collective-permute-start(f32[2,32,32,128]{3,2,1,0:T(8,128)S(1)} %get-tuple-element.46.both_ref), channel_id=1, source_target_pairs={{0,64},{64,0},{1,65},{65,1},{2,66},{66,2},{3,67},{67,3},{4,68},{68... | collective-permute-start | bytes 3145736 | tf_op jit(solution)/shard_map/ppermute | solution.py:325
  83.4 13.2 %all_to_all.44.received_ref = f32[128,2,128]{2,1,0:T(2,128)S(1)} all-to-all(f32[128,2,128]{2,1,0:T(2,128)S(1)} %get-tuple-element.45), channel_id=1, replica_groups=mesh['depth'=2,'batch_0'=4,'batch_1'=4,'batch_2'=4] {'depth','batch_0','..., dimensions={0} | all-to-all | bytes 262144 | tf_op jit(solution)/shard_map/all_to_all | solution.py:329
  96.6 3.6 %fork.1 = (f32[32,32,128]{2,1,0:T(8,128)S(1)}, f32[32,32,128]{2,1,0:T(8,128)S(1)}, f32[128,2,128]{2,1,0:T(2,128)S(1)}) custom-call(s32[2]{0:T(128)S(1)} %pad_add_fusion.flags_ref, f32[128,2,128]{2,1,0:T(2,128)S(1)} %all_to_all.44.received_ref, f32[2,32,32,128]{3,2,1,0:T(8,128)S(1)} %collective-permute-done.2.arrived_ref, ...), custom_call_target="tpu_custom_call" | custom-call | flops 2415919104 | bytes 9830408 | tf_op jit(solution)/shard_map/fork/pallas_call | solution.py:293
  100.2 13.3 %all_to_all.45.received_ref = f32[128,2,128]{2,1,0:T(2,128)S(1)} all-to-all(f32[128,2,128]{2,1,0:T(2,128)S(1)} %get-tuple-element.48), channel_id=1, replica_groups=mesh['depth'=2,'batch_0'=4,'batch_1'=4,'batch_2'=4] {'depth','batch_0','..., dimensions={0} | all-to-all | bytes 262144 | tf_op jit(solution)/shard_map/all_to_all | solution.py:329
  113.5 3.7 %coarse.1 = (f32[32,32,128]{2,1,0:T(8,128)S(1)}, f32[32,32,128]{2,1,0:T(8,128)S(1)}, f32[128,2,128]{2,1,0:T(2,128)S(1)}) custom-call(s32[2]{0:T(128)S(1)} %pad_add_fusion.flags_ref, f32[128,2,128]{2,1,0:T(2,128)S(1)} %all_to_all.45.received_ref, f32[32,32,128]{2,1,0:T(8,128)S(1)} %get-tuple-element.49.z_ref, ...), custom_call_target="tpu_custom_call" | custom-call | flops 2415919104 | bytes 8257544 | tf_op jit(solution)/shard_map/coarse/pallas_call | solution.py:293
  117.2 0.1 collective-permute-start.3
  117.3 13.7 %all_to_all.46.refs_0_ = f32[128,2,128]{2,1,0:T(2,128)S(1)} all-to-all(f32[128,2,128]{2,1,0:T(2,128)S(1)} %get-tuple-element.51), channel_id=1, replica_groups=mesh['depth'=2,'batch_0'=4,'batch_1'=4,'batch_2'=4] {'depth','batch_0','..., dimensions={0} | all-to-all | bytes 262144 | tf_op jit(solution)/shard_map/all_to_all | solution.py:329
  131.0 3.8 %second.1 = (f32[32,32,128]{2,1,0:T(8,128)S(1)}, f32[32,32,128]{2,1,0:T(8,128)S(1)}, f32[128,2,128]{2,1,0:T(2,128)S(1)}) custom-call(s32[2]{0:T(128)S(1)} %pad_add_fusion.flags_ref, f32[128,2,128]{2,1,0:T(2,128)S(1)} %all_to_all.46.refs_0_, f32[32,32,128]{2,1,0:T(8,128)S(1)} %get-tuple-element.52.refs_1_, f32[32,32,128]{2,1,0:T(8,128)S(1)} %get-tuple-element.53.refs_2_, ...), custom_call_target="tpu_custom_call" | custom-call | flops 2415919104 | bytes 7077896 | tf_op jit(solution)/shard_map/second/pallas_call | solution.py:293
  134.8 13.3 %all_to_all.47.received_ref = f32[128,2,128]{2,1,0:T(2,128)S(1)} all-to-all(f32[128,2,128]{2,1,0:T(2,128)S(1)} %get-tuple-element.54), channel_id=1, replica_groups=mesh['depth'=2,'batch_0'=4,'batch_1'=4,'batch_2'=4] {'depth','batch_0','..., dimensions={0} | all-to-all | bytes 262144 | tf_op jit(solution)/shard_map/all_to_all | solution.py:329
  148.1 3.0 %close.1 = f32[32,32,128]{2,1,0:T(8,128)} custom-call(s32[2]{0:T(128)S(1)} %pad_add_fusion.flags_ref, f32[128,2,128]{2,1,0:T(2,128)S(1)} %all_to_all.47.received_ref, f32[32,32,128]{2,1,0:T(8,128)S(1)} %get-tuple-element.55.z_ref, f32[32,32,128]{2,1,0:T(8,128)S(1)} %get-tuple-element.56.u_ref, f32[4,3,3,128,128]{4,3,2,1,0:T(8,128)S(1)} %copy-done, ...), custom_call_target="tpu_custom_call" | custom-call | flops 1207959552 | bytes 6160392 | tf_op jit(solution)/shard_map/close/pallas_call | solution.py:293
  (7 shorter events, 0.0 us)
Async XLA Ops:
  0.6 3.4 %collective-permute-start = (f32[32,32,128]{2,1,0:T(8,128)}, f32[32,32,128]{2,1,0:T(8,128)S(1)}, u32[]{:S(2)}, u32[]{:S(2)}) collective-permute-start(f32[32,32,128]{2,1,0:T(8,128)} %bitcast.8), channel_id=1, source_target_pairs={{0,64},{64,0},{1,65},{65,1},{2,66},{66,2},{3,67},{67,3},{4,68},{68... | collective-permute-start | bytes 1572872 | tf_op jit(solution)/shard_map/ppermute | solution.py:325
  4.0 22.3 %copy-start = (f32[4,3,3,128,128]{4,3,2,1,0:T(8,128)S(1)}, f32[4,3,3,128,128]{4,3,2,1,0:T(8,128)}, u32[]{:S(2)}) copy-start(f32[4,3,3,128,128]{4,3,2,1,0:T(8,128)} %wout_ref.13) | copy-start | bytes 7077892
  4.0 22.3 %copy-start.1 = (f32[4,3,3,128,128]{4,3,2,1,0:T(8,128)S(1)}, f32[4,3,3,128,128]{4,3,2,1,0:T(8,128)}, u32[]{:S(2)}) copy-start(f32[4,3,3,128,128]{4,3,2,1,0:T(8,128)} %refs_4_.1) | copy-start | bytes 7077892
  29.9 48.3 %collective-permute-start.1 = (f32[2,3,3,128,128]{4,3,2,1,0:T(8,128)S(1)}, f32[2,3,3,128,128]{4,3,2,1,0:T(8,128)S(1)}, u32[]{:S(2)}, u32[]{:S(2)}) collective-permute-start(f32[2,3,3,128,128]{4,3,2,1,0:T(8,128)S(1)} %get-tuple-element.44), channel_id=1, source_target_pairs={{0,64},{64,0},{1,65},{65,1},{2,66},{66,2},{3,67},{67,3},{4,68},{68... | collective-permute-start | bytes 3538952 | tf_op jit(solution)/shard_map/ppermute | solution.py:325
  81.3 15.3 %collective-permute-start.2 = (f32[2,32,32,128]{3,2,1,0:T(8,128)S(1)}, f32[2,32,32,128]{3,2,1,0:T(8,128)S(1)}, u32[]{:S(2)}, u32[]{:S(2)}) collective-permute-start(f32[2,32,32,128]{3,2,1,0:T(8,128)S(1)} %get-tuple-element.46.both_ref), channel_id=1, source_target_pairs={{0,64},{64,0},{1,65},{65,1},{2,66},{66,2},{3,67},{67,3},{4,68},{68... | collective-permute-start | bytes 3145736 | tf_op jit(solution)/shard_map/ppermute | solution.py:325
  117.2 30.9 %collective-permute-start.3 = (f32[32,32,128]{2,1,0:T(8,128)S(1)}, f32[32,32,128]{2,1,0:T(8,128)S(1)}, u32[]{:S(2)}, u32[]{:S(2)}) collective-permute-start(f32[32,32,128]{2,1,0:T(8,128)S(1)} %get-tuple-element.53.refs_2_), channel_id=1, source_target_pairs={{0,64},{64,0},{1,65},{65,1},{2,66},{66,2},{3,67},{67,3},{4,68},{68... | collective-permute-start | bytes 1572872 | tf_op jit(solution)/shard_map/ppermute | solution.py:325

commit v5 on v4

v5 whole, which is shorter than its diff:
```python
import functools

import jax
import jax.numpy as jnp
from jax import lax
from jax.experimental import pallas as pl
from jax.experimental.pallas import tpu as pltpu
from jax.sharding import Mesh
from jax.sharding import PartitionSpec as P

FACTOR = 4
BATCH = ("batch_0", "batch_1", "batch_2")
WORLD = ("depth",) + BATCH

EPSILON = 1e-05
STEP_SIZE = 0.25

ROWS = 32
COLS = 32
CHANNELS = 128
PAIRS = ROWS // 2
CELLS = ROWS * COLS
CHUNKS = 2
PART = PAIRS // CHUNKS
VMEM_LIMIT = 24 * 2**20
READY_LIMIT = 24 * 2**20


def split(x):
    high = x.astype(jnp.bfloat16)
    low = (x - high.astype(jnp.float32)).astype(jnp.bfloat16)
    return high, low


def placer(held_ref):
    rows = {-1: jnp.zeros((COLS, CHANNELS), jnp.float32)}

    def put(pair):
        d0, d1, d2, d3 = (rows[2 * pair + i] for i in range(-1, 3))
        del rows[2 * pair - 1], rows[2 * pair]
        at = slice(pair * COLS, (pair + 1) * COLS)
        for kind, value in enumerate((d0 - d2, d1 + d2, d2 - d1, d1 - d3)):
            high, low = split(value)
            held_ref[kind, at, :CHANNELS] = high
            held_ref[kind, at, CHANNELS:] = low

    def add(row, value):
        rows[row] = value
        if row and row % 2 == 0:
            put(row // 2 - 1)
        if row == ROWS - 1:
            rows[ROWS] = rows_end
            put(PAIRS - 1)

    rows_end = rows[-1]
    return add


def convolve(held_ref, weights_ref, chunk):
    many = PART * COLS
    at = slice(chunk * many, (chunk + 1) * many)
    wide = 3 * CHANNELS

    def product(kind):
        right = weights_ref[kind]
        out = jnp.dot(
            held_ref[kind, at, :],
            jnp.concatenate([right, right], axis=0),
            preferred_element_type=jnp.float32,
        )
        return out[:, :wide] + out[:, wide:]

    m0, m1, m2, m3 = (product(kind) for kind in range(4))
    column = lax.broadcasted_iota(jnp.int32, (many, CHANNELS), 0) % COLS

    def across(x):
        left, middle, right = (x[:, i * CHANNELS : (i + 1) * CHANNELS] for i in range(3))
        out = middle + jnp.where(column == 0, 0.0, pltpu.roll(left, 1, 0))
        return out + jnp.where(column == COLS - 1, 0.0, pltpu.roll(right, many - 1, 0))

    return across(m0 + (m1 + m2)), across((m1 - m2) - m3)


def branch_blocks(held_ref, weights_ref):
    for chunk in range(CHUNKS):
        halves = convolve(held_ref, weights_ref, chunk)
        for pair in range(PART):
            for half in range(2):
                yield 2 * (chunk * PART + pair) + half, halves[half][pair * COLS : (pair + 1) * COLS]


def into_conv(held_ref, weights_ref, z_ref, send_ref):
    totals, squares = [], []
    for chunk in range(CHUNKS):
        halves = convolve(held_ref, weights_ref, chunk)
        for half, out in enumerate(halves):
            for pair in range(PART):
                z_ref[2 * (chunk * PART + pair) + half] = out[pair * COLS : (pair + 1) * COLS]
            total = jnp.sum(out, axis=0, keepdims=True)
            away = out - total * (1.0 / (PART * COLS))
            totals.append(total)
            squares.append(jnp.sum(away * away, axis=0, keepdims=True))
    total = functools.reduce(jnp.add, totals)
    square = functools.reduce(jnp.add, squares)
    for part in totals:
        away = part * (1.0 / (PART * COLS)) - total * (1.0 / CELLS)
        square = square + (PART * COLS) * (away * away)
    both = jnp.concatenate([total, square], axis=0)
    send_ref[...] = jnp.broadcast_to(both[None], send_ref.shape)


def combined(received_ref, base):
    rows = received_ref[pl.ds(base, received_ref.shape[0] // 2)]
    samples = rows.shape[0]
    totals = rows[:, 0:1, :]
    average = jnp.sum(totals, axis=0) * (1.0 / (samples * CELLS))
    away = totals * (1.0 / CELLS) - average[None]
    square = jnp.sum(rows[:, 1:2, :], axis=0) + CELLS * jnp.sum(away * away, axis=0)
    return average, lax.rsqrt(square * (1.0 / (samples * CELLS)) + EPSILON)


def normalise(received_ref, base, z_ref, held_ref):
    average, factor = combined(received_ref, base)
    put = placer(held_ref)
    for row in range(ROWS):
        put(row, jnp.maximum((z_ref[row] - average) * factor, 0.0))


def add_branch(held_ref, weights_ref, scale, u_ref, unew_ref, onto_ref=None):
    put = placer(onto_ref) if onto_ref is not None else None
    for row, block in branch_blocks(held_ref, weights_ref):
        after = u_ref[row] + scale * block
        unew_ref[row] = after
        if put:
            put(row, after)


def split_weights(raw_ref, at, weights_ref):
    for across in range(3):
        first, middle, last = (raw_ref[at, up, across] for up in range(3))
        outer, inner = 0.5 * (first + last), 0.5 * middle
        for kind, value in enumerate((first, outer + inner, outer - inner, last)):
            high, low = split(value)
            weights_ref[kind, :, across * CHANNELS : (across + 1) * CHANNELS] = high
            weights_ref[kind, :, (3 + across) * CHANNELS : (4 + across) * CHANNELS] = low


def ready_kernel(flags_ref, initial_hbm, win_hbm, initial_ref, weights_ref, raw_ref, sem):
    weights = pltpu.make_async_copy(win_hbm.at[pl.ds(0, 1)], raw_ref, sem.at[0])
    state = pltpu.make_async_copy(initial_hbm, initial_ref, sem.at[1])
    weights.start()
    state.start()
    weights.wait()
    split_weights(raw_ref, 0, weights_ref)
    state.wait()


def open_kernel(flags_ref, initial_ref, before_ref, weights_ref, z_ref, u_ref, send_ref, held_ref):
    first = flags_ref[1] == 1
    put = placer(held_ref)
    for row in range(ROWS):
        value = jnp.where(first, initial_ref[row], before_ref[row])
        u_ref[row] = value
        put(row, value)
    into_conv(held_ref, weights_ref, z_ref, send_ref)


def step_kernel(
    layer, flags_ref, received_ref, z_ref, u_ref, wout_ref, win_ref, unew_ref, znew_ref, send_ref, *refs
):
    *more, held_ref, onto_ref, ending_ref, begun_ref = refs
    split_weights(wout_ref, layer, ending_ref)
    normalise(received_ref, flags_ref[0], z_ref, held_ref)
    if layer == 0:
        rest_ref, packed_ref = more
        packed_ref[0] = win_ref[0]
        packed_ref[1] = wout_ref[0]
        put = placer(onto_ref)
        for row, block in branch_blocks(held_ref, ending_ref):
            before = u_ref[row]
            after = before + STEP_SIZE * block
            unew_ref[row] = after
            put(row, after)
            coarse = before + FACTOR * STEP_SIZE * block
            rest_ref[row] = coarse - (before + FACTOR * (after - before))
    else:
        add_branch(held_ref, ending_ref, STEP_SIZE, u_ref, unew_ref, onto_ref)
    split_weights(win_ref, layer + 1, begun_ref)
    into_conv(onto_ref, begun_ref, znew_ref, send_ref)


def turn_kernel(
    flags_ref, received_ref, z_ref, u_ref, wout_ref, moved_ref, both_ref, ends_ref, send_ref,
    held_ref, onto_ref, ending_ref, begun_ref,
):
    split_weights(wout_ref, FACTOR - 1, ending_ref)
    normalise(received_ref, flags_ref[0], z_ref, held_ref)
    put = placer(onto_ref)
    for row, block in branch_blocks(held_ref, ending_ref):
        after = u_ref[row] + STEP_SIZE * block
        both_ref[0, row] = after
        ends_ref[row] = after
        put(row, after)
    split_weights(moved_ref, 0, begun_ref)
    into_conv(onto_ref, begun_ref, both_ref.at[1], send_ref)


def fork_kernel(
    flags_ref, received_ref, arrived_ref, both_ref, rest_ref, wout_ref, win_ref, moved_ref,
    unew_ref, znew_ref, send_ref, held_ref, onto_ref, ending_ref, begun_ref,
):
    @pl.when(flags_ref[1] == 1)
    def _():
        put = placer(held_ref)
        for row in range(ROWS):
            value = both_ref[0, row] + rest_ref[row]
            unew_ref[row] = value
            put(row, value)
        split_weights(moved_ref, 0, begun_ref)
        into_conv(held_ref, begun_ref, znew_ref, send_ref)

    @pl.when(flags_ref[1] == 0)
    def _():
        split_weights(wout_ref, 0, ending_ref)
        normalise(received_ref, 0, arrived_ref.at[1], held_ref)
        add_branch(held_ref, ending_ref, STEP_SIZE, arrived_ref.at[0], unew_ref, onto_ref)
        split_weights(win_ref, 1, begun_ref)
        into_conv(onto_ref, begun_ref, znew_ref, send_ref)


def coarse_kernel(
    flags_ref, received_ref, z_ref, u_ref, wout_ref, win_ref, moved_ref,
    unew_ref, znew_ref, send_ref, held_ref, onto_ref, ending_ref, begun_ref,
):
    @pl.when(flags_ref[1] == 1)
    def _():
        split_weights(moved_ref, 1, ending_ref)
        normalise(received_ref, flags_ref[0], z_ref, held_ref)
        add_branch(held_ref, ending_ref, FACTOR * STEP_SIZE, u_ref, unew_ref)

    @pl.when(flags_ref[1] == 0)
    def _():
        split_weights(wout_ref, 1, ending_ref)
        normalise(received_ref, flags_ref[0], z_ref, held_ref)
        add_branch(held_ref, ending_ref, STEP_SIZE, u_ref, unew_ref, onto_ref)
        split_weights(win_ref, 2, begun_ref)
        into_conv(onto_ref, begun_ref, znew_ref, send_ref)


def second_kernel(flags_ref, *refs):
    @pl.when(flags_ref[1] == 0)
    def _():
        step_kernel(2, flags_ref, *refs)


def close_kernel(
    flags_ref, received_ref, z_ref, u_ref, wout_ref, arrived_ref, first_ref, coarse_ref, out_hbm,
    held_ref, ending_ref, out_ref, sem,
):
    @pl.when(flags_ref[1] == 1)
    def _():
        copy = pltpu.make_async_copy(first_ref, out_hbm, sem.at[0])
        copy.start()
        copy.wait()

    @pl.when(flags_ref[1] == 0)
    def _():
        split_weights(wout_ref, FACTOR - 1, ending_ref)
        normalise(received_ref, flags_ref[0], z_ref, held_ref)
        copies = []
        for row, block in branch_blocks(held_ref, ending_ref):
            fine = u_ref[row] + STEP_SIZE * block
            begun, first = arrived_ref[0, row], first_ref[row]
            tau = fine - (begun + FACTOR * (first - begun))
            out_ref[row] = coarse_ref[row] + tau
            if (row + 1) % (2 * PART) == 0:
                rows = pl.ds(row + 1 - 2 * PART, 2 * PART)
                copies.append(
                    pltpu.make_async_copy(out_ref.at[rows], out_hbm.at[rows], sem.at[len(copies)])
                )
                copies[-1].start()
        for copy in copies:
            copy.wait()


STATE = jax.ShapeDtypeStruct((ROWS, COLS, CHANNELS), jnp.float32)
BOTH = jax.ShapeDtypeStruct((2, ROWS, COLS, CHANNELS), jnp.float32)
SMEM = pl.BlockSpec(memory_space=pltpu.SMEM)
VMEM = pl.BlockSpec(memory_space=pltpu.VMEM)
HELD = [pltpu.VMEM((4, PAIRS * COLS, 2 * CHANNELS), jnp.bfloat16)]
WEIGHTS = [pltpu.VMEM((4, CHANNELS, 6 * CHANNELS), jnp.bfloat16)]
ONE = HELD + WEIGHTS
TWO = HELD * 2 + WEIGHTS * 2
CLOSE = ONE + [
    pltpu.VMEM((ROWS, COLS, CHANNELS), jnp.float32),
    pltpu.SemaphoreType.DMA((CHUNKS,)),
]
CONV_FLOPS = 2 * 4 * 512 * 256 * 768


def call(kernel, name, outs, convs, scratch, *args, out_space=VMEM):
    touched = sum(a.size * a.dtype.itemsize for a in (*args, *outs))
    return pl.pallas_call(
        kernel,
        name=name,
        out_shape=tuple(outs),
        in_specs=[SMEM] + [VMEM] * (len(args) - 1),
        out_specs=(out_space,) * len(outs),
        scratch_shapes=scratch,
        compiler_params=pltpu.CompilerParams(vmem_limit_bytes=VMEM_LIMIT),
        cost_estimate=pl.CostEstimate(
            flops=convs * CONV_FLOPS, bytes_accessed=touched, transcendentals=0
        ),
    )(*args)


def ready(flags, initial, conv_in):
    shape = conv_in.shape[1:]
    return pl.pallas_call(
        ready_kernel,
        name="ready",
        out_shape=(STATE, jax.ShapeDtypeStruct(WEIGHTS[0].shape, jnp.bfloat16)),
        in_specs=[SMEM] + [pl.BlockSpec(memory_space=pltpu.HBM)] * 2,
        out_specs=(VMEM,) * 2,
        scratch_shapes=[
            pltpu.VMEM((1,) + shape, jnp.float32),
            pltpu.SemaphoreType.DMA((2,)),
        ],
        compiler_params=pltpu.CompilerParams(vmem_limit_bytes=READY_LIMIT),
        cost_estimate=pl.CostEstimate(flops=1000, bytes_accessed=3000000, transcendentals=0),
    )(flags, *(pltpu.with_memory_space_constraint(x, pltpu.HBM) for x in (initial, conv_in)))


def swapped(x):
    return lax.ppermute(x, "depth", [(0, 1), (1, 0)])


def exchange(send):
    return lax.all_to_all(send, WORLD, 0, 0)


def body(initial, guess, conv_in, conv_out):
    devices = lax.axis_size(WORLD)
    sent = jax.ShapeDtypeStruct((devices, 2, CHANNELS), jnp.float32)
    position = lax.axis_index("depth")
    flags = jnp.stack([position * (devices // 2), 1 - position]).astype(jnp.int32)
    outs = (STATE, STATE, sent)

    before = swapped(guess[0, 0])
    held, weights = ready(flags, initial[0], conv_in)
    z, u, send = call(open_kernel, "open", outs, 1, HELD, flags, held, before, weights)
    received = exchange(send)
    packed = jax.ShapeDtypeStruct((2,) + conv_in.shape[1:], jnp.float32)
    u, z, send, rest, packed = call(
        functools.partial(step_kernel, 0), "step", outs + (STATE, packed), 2, TWO,
        flags, received, z, u, conv_out, conv_in,
    )
    moved = swapped(packed)
    received = exchange(send)
    for layer in (1, 2):
        u, z, send = call(
            functools.partial(step_kernel, layer), "step", outs, 2, TWO,
            flags, received, z, u, conv_out, conv_in,
        )
        received = exchange(send)
    both, ends, send = call(
        turn_kernel, "turn", (BOTH, STATE, sent), 2, TWO,
        flags, received, z, u, conv_out, moved,
    )
    arrived = swapped(both)
    received = exchange(send)
    first, z, send = call(
        fork_kernel, "fork", outs, 2, TWO,
        flags, received, arrived, both, rest, conv_out, conv_in, moved,
    )
    received = exchange(send)
    u, z, send = call(
        coarse_kernel, "coarse", outs, 2, TWO,
        flags, received, z, first, conv_out, conv_in, moved,
    )
    coarse = swapped(u)
    received = exchange(send)
    u, z, send = call(
        second_kernel, "second", outs, 2, TWO, flags, received, z, u, conv_out, conv_in
    )
    received = exchange(send)
    (result,) = call(
        close_kernel, "close", (STATE,), 1, CLOSE,
        flags, received, z, u, conv_out, arrived, first, coarse, out_space=pl.BlockSpec(memory_space=pltpu.HBM),
    )
    return (result[None, None], ends[None, None])


def solution(mesh):
    split_mesh = Mesh(
        mesh.devices.reshape(mesh.shape["depth"], 4, 4, 4),
        ("depth", "batch_0", "batch_1", "batch_2"),
    )
    placed = (
        P(BATCH, None, None, None),
        P("depth", BATCH, None, None, None),
        P("depth", None, None, None, None),
        P("depth", None, None, None, None),
    )
    return jax.shard_map(
        body,
        mesh=split_mesh,
        in_specs=placed,
        out_specs=(P("depth", BATCH, None, None, None), P("depth", BATCH, None, None, None)),
        check_vma=False,
    )
```

time: 151 us -> 148 us (0.980)
  Pallas kernels: 31.8 us -> 30 us
    pallas_call x9, Pallas kernels: 30 us -> 28 us  [call(): pl.pallas_call(kernel, name=name, out_shape=tuple(outs), in_specs=[SMEM]...]
where the time goes in v5:
time: 148 us
  blocking collectives  114 us (77%)
  Pallas kernels  30 us (20%)
  starting transfers between devices  2.87 us (2%)
    all_to_all x8, blocking collectives, exchange(): return lax.all_to_all(send, WORLD, 0, 0)  114 us
    pallas_call x9, Pallas kernels, call(): pl.pallas_call(kernel, name=name, out_shape=tuple(outs), in_specs=[SMEM]...  28 us
  transfers between devices with their start and end apart: 4, of which 0 were waited for; matrix products, arithmetic and copies ran while one was open for 0% of the time, Pallas kernels for 8%

profile of v5, /device:TPU:1, one launch (start us, length us, event | category | flops | bytes accessed | tf_op | source)
XLA Modules:
  0.0 148.0 jit_solution(2454076567064460596)
XLA Ops:
  0.6 1.5 %collective-permute-start = (f32[32,32,128]{2,1,0:T(8,128)}, f32[32,32,128]{2,1,0:T(8,128)S(1)}, u32[]{:S(2)}, u32[]{:S(2)}) collective-permute-start(f32[32,32,128]{2,1,0:T(8,128)} %bitcast.8), channel_id=1, source_target_pairs={{0,64},{64,0},{1,65},{65,1},{2,66},{66,2},{3,67},{67,3},{4,68},{68... | collective-permute-start | bytes 1572872 | tf_op jit(solution)/shard_map/ppermute | solution.py:335
  2.1 0.1 pad_add_fusion.flags_ref
  2.2 2.1 %ready.1 = (f32[32,32,128]{2,1,0:T(8,128)S(1)}, bf16[4,128,768]{2,1,0:T(8,128)(2,1)S(1)}) custom-call(s32[2]{0:T(128)S(1)} %pad_add_fusion.flags_ref, f32[32,32,128]{2,1,0:T(8,128)} %bitcast.7, f32[4,3,3,128,128]{4,3,2,1,0:T(8,128)} %refs_4_.1), custom_call_target="tpu_custom_call" | custom-call | flops 1000 | bytes 3000000 | tf_op jit(solution)/shard_map/ready/pallas_call | solution.py:319
  4.3 1.8 %open.1 = (f32[32,32,128]{2,1,0:T(8,128)S(1)}, f32[32,32,128]{2,1,0:T(8,128)S(1)}, f32[128,2,128]{2,1,0:T(2,128)S(1)}) custom-call(s32[2]{0:T(128)S(1)} %pad_add_fusion.flags_ref, f32[32,32,128]{2,1,0:T(8,128)S(1)} %get-tuple-element.30.initial_ref, f32[32,32,128]{2,1,0:T(8,128)S(1)} %collective-permute-done.before_ref, ...), custom_call_target="tpu_custom_call" | custom-call | flops 805306368 | bytes 3014664 | tf_op jit(solution)/shard_map/open/pallas_call | solution.py:303
  6.1 20.0 %all_to_all.40.received_ref = f32[128,2,128]{2,1,0:T(2,128)S(1)} all-to-all(f32[128,2,128]{2,1,0:T(2,128)S(1)} %get-tuple-element.32), channel_id=1, replica_groups=mesh['depth'=2,'batch_0'=4,'batch_1'=4,'batch_2'=4] {'depth','batch_0','..., dimensions={0} | all-to-all | bytes 262144 | tf_op jit(solution)/shard_map/all_to_all | solution.py:339
  26.1 3.4 %step.3 = (f32[32,32,128]{2,1,0:T(8,128)S(1)}, f32[32,32,128]{2,1,0:T(8,128)S(1)}, f32[128,2,128]{2,1,0:T(2,128)S(1)}, f32[32,32,128]{2,1,0:T(8,128)S(1)}, f32[2,3,3,128,128]{4,3,2,1,0:T(8,128)S(1)}) custom-call(s32[2]{0:T(128)S(1)} %pad_add_fusion.flags_ref, f32[128,2,128]{2,1,0:T(2,128)S(1)} %all_to_all.40.received_ref, ...), custom_call_target="tpu_custom_call" | custom-call | flops 1610612736 | bytes 8781832 | tf_op jit(solution)/shard_map/step/pallas_call | solution.py:303
  29.5 0.6 collective-permute-start.1
  30.1 13.2 %all_to_all.41.received_ref = f32[128,2,128]{2,1,0:T(2,128)S(1)} all-to-all(f32[128,2,128]{2,1,0:T(2,128)S(1)} %get-tuple-element.35), channel_id=1, replica_groups=mesh['depth'=2,'batch_0'=4,'batch_1'=4,'batch_2'=4] {'depth','batch_0','..., dimensions={0} | all-to-all | bytes 262144 | tf_op jit(solution)/shard_map/all_to_all | solution.py:339
  43.3 3.3 %step.4 = (f32[32,32,128]{2,1,0:T(8,128)S(1)}, f32[32,32,128]{2,1,0:T(8,128)S(1)}, f32[128,2,128]{2,1,0:T(2,128)S(1)}) custom-call(s32[2]{0:T(128)S(1)} %pad_add_fusion.flags_ref, f32[128,2,128]{2,1,0:T(2,128)S(1)} %all_to_all.41.received_ref, f32[32,32,128]{2,1,0:T(8,128)S(1)} %get-tuple-element.36.z_ref, f32[32,32,128]{2,1,0:T(8,128)S(1)} %get-tuple-element.37.u_ref, ...), custom_call_target="tpu_custom_call" | custom-call | flops 1610612736 | bytes 7077896 | tf_op jit(solution)/shard_map/step/pallas_call | solution.py:303
  46.6 13.7 %all_to_all.42.received_ref = f32[128,2,128]{2,1,0:T(2,128)S(1)} all-to-all(f32[128,2,128]{2,1,0:T(2,128)S(1)} %get-tuple-element.38), channel_id=1, replica_groups=mesh['depth'=2,'batch_0'=4,'batch_1'=4,'batch_2'=4] {'depth','batch_0','..., dimensions={0} | all-to-all | bytes 262144 | tf_op jit(solution)/shard_map/all_to_all | solution.py:339
  60.3 3.3 %step.5 = (f32[32,32,128]{2,1,0:T(8,128)S(1)}, f32[32,32,128]{2,1,0:T(8,128)S(1)}, f32[128,2,128]{2,1,0:T(2,128)S(1)}) custom-call(s32[2]{0:T(128)S(1)} %pad_add_fusion.flags_ref, f32[128,2,128]{2,1,0:T(2,128)S(1)} %all_to_all.42.received_ref, f32[32,32,128]{2,1,0:T(8,128)S(1)} %get-tuple-element.39.z_ref, f32[32,32,128]{2,1,0:T(8,128)S(1)} %get-tuple-element.40.u_ref, ...), custom_call_target="tpu_custom_call" | custom-call | flops 1610612736 | bytes 7077896 | tf_op jit(solution)/shard_map/step/pallas_call | solution.py:303
  63.6 13.7 %all_to_all.43.received_ref = f32[128,2,128]{2,1,0:T(2,128)S(1)} all-to-all(f32[128,2,128]{2,1,0:T(2,128)S(1)} %get-tuple-element.41), channel_id=1, replica_groups=mesh['depth'=2,'batch_0'=4,'batch_1'=4,'batch_2'=4] {'depth','batch_0','..., dimensions={0} | all-to-all | bytes 262144 | tf_op jit(solution)/shard_map/all_to_all | solution.py:339
  77.3 3.3 %turn.1 = (f32[2,32,32,128]{3,2,1,0:T(8,128)S(1)}, f32[32,32,128]{2,1,0:T(8,128)}, f32[128,2,128]{2,1,0:T(2,128)S(1)}) custom-call(s32[2]{0:T(128)S(1)} %pad_add_fusion.flags_ref, f32[128,2,128]{2,1,0:T(2,128)S(1)} %all_to_all.43.received_ref, f32[32,32,128]{2,1,0:T(8,128)S(1)} %get-tuple-element.42.z_ref, f32[32,32,128]{2,1,0:T(8,128)S(1)} %get-tuple-element.43.u_ref, ...), custom_call_target="tpu_custom_call" | custom-call | flops 1610612736 | bytes 6422536 | tf_op jit(solution)/shard_map/turn/pallas_call | solution.py:303
  80.6 0.6 collective-permute-start.2
  81.2 13.2 %all_to_all.44.received_ref = f32[128,2,128]{2,1,0:T(2,128)S(1)} all-to-all(f32[128,2,128]{2,1,0:T(2,128)S(1)} %get-tuple-element.45), channel_id=1, replica_groups=mesh['depth'=2,'batch_0'=4,'batch_1'=4,'batch_2'=4] {'depth','batch_0','..., dimensions={0} | all-to-all | bytes 262144 | tf_op jit(solution)/shard_map/all_to_all | solution.py:339
  94.4 0.0 collective-permute-done.2.arrived_ref
  94.4 3.3 %fork.1 = (f32[32,32,128]{2,1,0:T(8,128)S(1)}, f32[32,32,128]{2,1,0:T(8,128)S(1)}, f32[128,2,128]{2,1,0:T(2,128)S(1)}) custom-call(s32[2]{0:T(128)S(1)} %pad_add_fusion.flags_ref, f32[128,2,128]{2,1,0:T(2,128)S(1)} %all_to_all.44.received_ref, f32[2,32,32,128]{3,2,1,0:T(8,128)S(1)} %collective-permute-done.2.arrived_ref, ...), custom_call_target="tpu_custom_call" | custom-call | flops 1610612736 | bytes 9830408 | tf_op jit(solution)/shard_map/fork/pallas_call | solution.py:303
  97.8 13.3 %all_to_all.45.received_ref = f32[128,2,128]{2,1,0:T(2,128)S(1)} all-to-all(f32[128,2,128]{2,1,0:T(2,128)S(1)} %get-tuple-element.48), channel_id=1, replica_groups=mesh['depth'=2,'batch_0'=4,'batch_1'=4,'batch_2'=4] {'depth','batch_0','..., dimensions={0} | all-to-all | bytes 262144 | tf_op jit(solution)/shard_map/all_to_all | solution.py:339
  111.1 3.5 %coarse.1 = (f32[32,32,128]{2,1,0:T(8,128)S(1)}, f32[32,32,128]{2,1,0:T(8,128)S(1)}, f32[128,2,128]{2,1,0:T(2,128)S(1)}) custom-call(s32[2]{0:T(128)S(1)} %pad_add_fusion.flags_ref, f32[128,2,128]{2,1,0:T(2,128)S(1)} %all_to_all.45.received_ref, f32[32,32,128]{2,1,0:T(8,128)S(1)} %get-tuple-element.49.z_ref, ...), custom_call_target="tpu_custom_call" | custom-call | flops 1610612736 | bytes 8257544 | tf_op jit(solution)/shard_map/coarse/pallas_call | solution.py:303
  114.6 0.1 collective-permute-start.3
  114.7 13.7 %all_to_all.46.refs_0_ = f32[128,2,128]{2,1,0:T(2,128)S(1)} all-to-all(f32[128,2,128]{2,1,0:T(2,128)S(1)} %get-tuple-element.51), channel_id=1, replica_groups=mesh['depth'=2,'batch_0'=4,'batch_1'=4,'batch_2'=4] {'depth','batch_0','..., dimensions={0} | all-to-all | bytes 262144 | tf_op jit(solution)/shard_map/all_to_all | solution.py:339
  128.4 3.3 %second.1 = (f32[32,32,128]{2,1,0:T(8,128)S(1)}, f32[32,32,128]{2,1,0:T(8,128)S(1)}, f32[128,2,128]{2,1,0:T(2,128)S(1)}) custom-call(s32[2]{0:T(128)S(1)} %pad_add_fusion.flags_ref, f32[128,2,128]{2,1,0:T(2,128)S(1)} %all_to_all.46.refs_0_, f32[32,32,128]{2,1,0:T(8,128)S(1)} %get-tuple-element.52.refs_1_, f32[32,32,128]{2,1,0:T(8,128)S(1)} %get-tuple-element.53.refs_2_, ...), custom_call_target="tpu_custom_call" | custom-call | flops 1610612736 | bytes 7077896 | tf_op jit(solution)/shard_map/second/pallas_call | solution.py:303
  131.7 13.3 %all_to_all.47.received_ref = f32[128,2,128]{2,1,0:T(2,128)S(1)} all-to-all(f32[128,2,128]{2,1,0:T(2,128)S(1)} %get-tuple-element.54), channel_id=1, replica_groups=mesh['depth'=2,'batch_0'=4,'batch_1'=4,'batch_2'=4] {'depth','batch_0','..., dimensions={0} | all-to-all | bytes 262144 | tf_op jit(solution)/shard_map/all_to_all | solution.py:339
  145.0 2.8 %close.1 = f32[32,32,128]{2,1,0:T(8,128)} custom-call(s32[2]{0:T(128)S(1)} %pad_add_fusion.flags_ref, f32[128,2,128]{2,1,0:T(2,128)S(1)} %all_to_all.47.received_ref, f32[32,32,128]{2,1,0:T(8,128)S(1)} %get-tuple-element.55.z_ref, f32[32,32,128]{2,1,0:T(8,128)S(1)} %get-tuple-element.56.u_ref, f32[4,3,3,128,128]{4,3,2,1,0:T(8,128)S(1)} %copy-done, ...), custom_call_target="tpu_custom_call" | custom-call | flops 805306368 | bytes 6160392 | tf_op jit(solution)/shard_map/close/pallas_call | solution.py:303
  (7 shorter events, 0.0 us)
Async XLA Ops:
  0.6 3.6 %collective-permute-start = (f32[32,32,128]{2,1,0:T(8,128)}, f32[32,32,128]{2,1,0:T(8,128)S(1)}, u32[]{:S(2)}, u32[]{:S(2)}) collective-permute-start(f32[32,32,128]{2,1,0:T(8,128)} %bitcast.8), channel_id=1, source_target_pairs={{0,64},{64,0},{1,65},{65,1},{2,66},{66,2},{3,67},{67,3},{4,68},{68... | collective-permute-start | bytes 1572872 | tf_op jit(solution)/shard_map/ppermute | solution.py:335
  2.2 23.9 %copy-start = (f32[4,3,3,128,128]{4,3,2,1,0:T(8,128)S(1)}, f32[4,3,3,128,128]{4,3,2,1,0:T(8,128)}, u32[]{:S(2)}) copy-start(f32[4,3,3,128,128]{4,3,2,1,0:T(8,128)} %wout_ref.13) | copy-start | bytes 7077892
  2.2 23.9 %copy-start.1 = (f32[4,3,3,128,128]{4,3,2,1,0:T(8,128)S(1)}, f32[4,3,3,128,128]{4,3,2,1,0:T(8,128)}, u32[]{:S(2)}) copy-start(f32[4,3,3,128,128]{4,3,2,1,0:T(8,128)} %refs_4_.1) | copy-start | bytes 7077892
  29.5 47.8 %collective-permute-start.1 = (f32[2,3,3,128,128]{4,3,2,1,0:T(8,128)S(1)}, f32[2,3,3,128,128]{4,3,2,1,0:T(8,128)S(1)}, u32[]{:S(2)}, u32[]{:S(2)}) collective-permute-start(f32[2,3,3,128,128]{4,3,2,1,0:T(8,128)S(1)} %get-tuple-element.44), channel_id=1, source_target_pairs={{0,64},{64,0},{1,65},{65,1},{2,66},{66,2},{3,67},{67,3},{4,68},{68... | collective-permute-start | bytes 3538952 | tf_op jit(solution)/shard_map/ppermute | solution.py:335
  80.6 13.9 %collective-permute-start.2 = (f32[2,32,32,128]{3,2,1,0:T(8,128)S(1)}, f32[2,32,32,128]{3,2,1,0:T(8,128)S(1)}, u32[]{:S(2)}, u32[]{:S(2)}) collective-permute-start(f32[2,32,32,128]{3,2,1,0:T(8,128)S(1)} %get-tuple-element.46.both_ref), channel_id=1, source_target_pairs={{0,64},{64,0},{1,65},{65,1},{2,66},{66,2},{3,67},{67,3},{4,68},{68... | collective-permute-start | bytes 3145736 | tf_op jit(solution)/shard_map/ppermute | solution.py:335
  114.6 30.4 %collective-permute-start.3 = (f32[32,32,128]{2,1,0:T(8,128)S(1)}, f32[32,32,128]{2,1,0:T(8,128)S(1)}, u32[]{:S(2)}, u32[]{:S(2)}) collective-permute-start(f32[32,32,128]{2,1,0:T(8,128)S(1)} %get-tuple-element.53.refs_2_), channel_id=1, source_target_pairs={{0,64},{64,0},{1,65},{65,1},{2,66},{66,2},{3,67},{67,3},{4,68},{68... | collective-permute-start | bytes 1572872 | tf_op jit(solution)/shard_map/ppermute | solution.py:335

commit v6 on v5

--- a/solution.py
+++ b/solution.py
@@ -105,17 +105,17 @@
     for part in totals:
         away = part * (1.0 / (PART * COLS)) - total * (1.0 / CELLS)
         square = square + (PART * COLS) * (away * away)
-    both = jnp.concatenate([total, square], axis=0)
-    send_ref[...] = jnp.broadcast_to(both[None], send_ref.shape)
+    is_sum = lax.broadcasted_iota(jnp.int32, send_ref.shape, 0) % 2 == 0
+    send_ref[...] = jnp.where(is_sum, total, square)
 
 
 def combined(received_ref, base):
-    rows = received_ref[pl.ds(base, received_ref.shape[0] // 2)]
-    samples = rows.shape[0]
-    totals = rows[:, 0:1, :]
-    average = jnp.sum(totals, axis=0) * (1.0 / (samples * CELLS))
-    away = totals * (1.0 / CELLS) - average[None]
-    square = jnp.sum(rows[:, 1:2, :], axis=0) + CELLS * jnp.sum(away * away, axis=0)
+    samples = received_ref.shape[0] // 4
+    rows = received_ref[pl.ds(pl.multiple_of(2 * base, 2 * samples), 2 * samples), :]
+    is_sum = lax.broadcasted_iota(jnp.int32, rows.shape, 0) % 2 == 0
+    average = jnp.sum(jnp.where(is_sum, rows, 0.0), axis=0, keepdims=True) * (1.0 / (samples * CELLS))
+    away = rows * (1.0 / CELLS) - average
+    square = jnp.sum(jnp.where(is_sum, CELLS * (away * away), rows), axis=0, keepdims=True)
     return average, lax.rsqrt(square * (1.0 / (samples * CELLS)) + EPSILON)
 
 
@@ -165,33 +165,46 @@
     into_conv(held_ref, weights_ref, z_ref, send_ref)
 
 
+def fine_step(flags_ref, received_ref, z_ref, u_ref, ending_ref, begun_ref, unew_ref, znew_ref, send_ref, held_ref, onto_ref):
+    normalise(received_ref, flags_ref[0], z_ref, held_ref)
+    add_branch(held_ref, ending_ref, STEP_SIZE, u_ref, unew_ref, onto_ref)
+    into_conv(onto_ref, begun_ref, znew_ref, send_ref)
+
+
+def begin_kernel(
+    flags_ref, received_ref, z_ref, u_ref, wout_ref, win_ref,
+    unew_ref, znew_ref, send_ref, ending_ref, begun_ref, rest_ref, packed_ref, held_ref, onto_ref,
+):
+    split_weights(wout_ref, 0, ending_ref)
+    normalise(received_ref, flags_ref[0], z_ref, held_ref)
+    put = placer(onto_ref)
+    for row, block in branch_blocks(held_ref, ending_ref):
+        before = u_ref[row]
+        after = before + STEP_SIZE * block
+        unew_ref[row] = after
+        put(row, after)
+        coarse = before + FACTOR * STEP_SIZE * block
+        rest_ref[row] = coarse - (before + FACTOR * (after - before))
+    packed_ref[0] = win_ref[0]
+    packed_ref[1] = wout_ref[0]
+    split_weights(win_ref, 1, begun_ref)
+    into_conv(onto_ref, begun_ref, znew_ref, send_ref)
+
+
 def step_kernel(
-    layer, flags_ref, received_ref, z_ref, u_ref, wout_ref, win_ref, unew_ref, znew_ref, send_ref, *refs
-):
-    *more, held_ref, onto_ref, ending_ref, begun_ref = refs
+    layer, flags_ref, received_ref, z_ref, u_ref, wout_ref, win_ref,
+    unew_ref, znew_ref, send_ref, ending_ref, begun_ref, held_ref, onto_ref,
+):
     split_weights(wout_ref, layer, ending_ref)
     normalise(received_ref, flags_ref[0], z_ref, held_ref)
-    if layer == 0:
-        rest_ref, packed_ref = more
-        packed_ref[0] = win_ref[0]
-        packed_ref[1] = wout_ref[0]
-        put = placer(onto_ref)
-        for row, block in branch_blocks(held_ref, ending_ref):
-            before = u_ref[row]
-            after = before + STEP_SIZE * block
-            unew_ref[row] = after
-            put(row, after)
-            coarse = before + FACTOR * STEP_SIZE * block
-            rest_ref[row] = coarse - (before + FACTOR * (after - before))
-    else:
-        add_branch(held_ref, ending_ref, STEP_SIZE, u_ref, unew_ref, onto_ref)
+    add_branch(held_ref, ending_ref, STEP_SIZE, u_ref, unew_ref, onto_ref)
     split_weights(win_ref, layer + 1, begun_ref)
     into_conv(onto_ref, begun_ref, znew_ref, send_ref)
 
 
 def turn_kernel(
-    flags_ref, received_ref, z_ref, u_ref, wout_ref, moved_ref, both_ref, ends_ref, send_ref,
-    held_ref, onto_ref, ending_ref, begun_ref,
+    flags_ref, received_ref, z_ref, u_ref, wout_ref, moved_ref,
+    both_ref, ends_ref, send_ref, ending_ref, begun_ref, held_ref, onto_ref,
 ):
     split_weights(wout_ref, FACTOR - 1, ending_ref)
     normalise(received_ref, flags_ref[0], z_ref, held_ref)
@@ -206,8 +219,8 @@
 
 
 def fork_kernel(
-    flags_ref, received_ref, arrived_ref, both_ref, rest_ref, wout_ref, win_ref, moved_ref,
-    unew_ref, znew_ref, send_ref, held_ref, onto_ref, ending_ref, begun_ref,
+    flags_ref, received_ref, arrived_ref, both_ref, rest_ref, moved_ref, ending_ref, begun_ref,
+    unew_ref, znew_ref, send_ref, held_ref, onto_ref,
 ):
     @pl.when(flags_ref[1] == 1)
     def _():
@@ -216,46 +229,42 @@
             value = both_ref[0, row] + rest_ref[row]
             unew_ref[row] = value
             put(row, value)
-        split_weights(moved_ref, 0, begun_ref)
-        into_conv(held_ref, begun_ref, znew_ref, send_ref)
+        into_conv(held_ref, moved_ref, znew_ref, send_ref)
 
     @pl.when(flags_ref[1] == 0)
     def _():
-        split_weights(wout_ref, 0, ending_ref)
         normalise(received_ref, 0, arrived_ref.at[1], held_ref)
         add_branch(held_ref, ending_ref, STEP_SIZE, arrived_ref.at[0], unew_ref, onto_ref)
-        split_weights(win_ref, 1, begun_ref)
         into_conv(onto_ref, begun_ref, znew_ref, send_ref)
 
 
 def coarse_kernel(
-    flags_ref, received_ref, z_ref, u_ref, wout_ref, win_ref, moved_ref,
-    unew_ref, znew_ref, send_ref, held_ref, onto_ref, ending_ref, begun_ref,
+    flags_ref, received_ref, z_ref, u_ref, moved_ref, ending_ref, begun_ref,
+    unew_ref, znew_ref, send_ref, held_ref, onto_ref, weights_ref,
 ):
     @pl.when(flags_ref[1] == 1)
     def _():
-        split_weights(moved_ref, 1, ending_ref)
+        split_weights(moved_ref, 1, weights_ref)
         normalise(received_ref, flags_ref[0], z_ref, held_ref)
-        add_branch(held_ref, ending_ref, FACTOR * STEP_SIZE, u_ref, unew_ref)
+        add_branch(held_ref, weights_ref, FACTOR * STEP_SIZE, u_ref, unew_ref)
 
     @pl.when(flags_ref[1] == 0)
     def _():
-        split_weights(wout_ref, 1, ending_ref)
-        normalise(received_ref, flags_ref[0], z_ref, held_ref)
-        add_branch(held_ref, ending_ref, STEP_SIZE, u_ref, unew_ref, onto_ref)
-        split_weights(win_ref, 2, begun_ref)
-        into_conv(onto_ref, begun_ref, znew_ref, send_ref)
+        fine_step(
+            flags_ref, received_ref, z_ref, u_ref, ending_ref, begun_ref,
+            unew_ref, znew_ref, send_ref, held_ref, onto_ref,
+        )
 
 
 def second_kernel(flags_ref, *refs):
     @pl.when(flags_ref[1] == 0)
     def _():
-        step_kernel(2, flags_ref, *refs)
+        fine_step(flags_ref, *refs)
 
 
 def close_kernel(
-    flags_ref, received_ref, z_ref, u_ref, wout_ref, arrived_ref, first_ref, coarse_ref, out_hbm,
-    held_ref, ending_ref, out_ref, sem,
+    flags_ref, received_ref, z_ref, u_ref, ending_ref, arrived_ref, first_ref, coarse_ref, out_hbm,
+    held_ref, out_ref, sem,
 ):
     @pl.when(flags_ref[1] == 1)
     def _():
@@ -265,7 +274,6 @@
 
     @pl.when(flags_ref[1] == 0)
     def _():
-        split_weights(wout_ref, FACTOR - 1, ending_ref)
         normalise(received_ref, flags_ref[0], z_ref, held_ref)
         copies = []
         for row, block in branch_blocks(held_ref, ending_ref):
@@ -289,9 +297,9 @@
 VMEM = pl.BlockSpec(memory_space=pltpu.VMEM)
 HELD = [pltpu.VMEM((4, PAIRS * COLS, 2 * CHANNELS), jnp.bfloat16)]
 WEIGHTS = [pltpu.VMEM((4, CHANNELS, 6 * CHANNELS), jnp.bfloat16)]
-ONE = HELD + WEIGHTS
-TWO = HELD * 2 + WEIGHTS * 2
-CLOSE = ONE + [
+READY = jax.ShapeDtypeStruct(WEIGHTS[0].shape, jnp.bfloat16)
+TWO = HELD * 2
+CLOSE = HELD + [
     pltpu.VMEM((ROWS, COLS, CHANNELS), jnp.float32),
     pltpu.SemaphoreType.DMA((CHUNKS,)),
 ]
@@ -319,7 +327,7 @@
     return pl.pallas_call(
         ready_kernel,
         name="ready",
-        out_shape=(STATE, jax.ShapeDtypeStruct(WEIGHTS[0].shape, jnp.bfloat16)),
+        out_shape=(STATE, READY),
         in_specs=[SMEM] + [pl.BlockSpec(memory_space=pltpu.HBM)] * 2,
         out_specs=(VMEM,) * 2,
         scratch_shapes=[
@@ -336,12 +344,13 @@
 
 
 def exchange(send):
-    return lax.all_to_all(send, WORLD, 0, 0)
+    apart = send.reshape(send.shape[0] // 2, 2, CHANNELS)
+    return lax.all_to_all(apart, WORLD, 0, 0).reshape(send.shape)
 
 
 def body(initial, guess, conv_in, conv_out):
     devices = lax.axis_size(WORLD)
-    sent = jax.ShapeDtypeStruct((devices, 2, CHANNELS), jnp.float32)
+    sent = jax.ShapeDtypeStruct((2 * devices, CHANNELS), jnp.float32)
     position = lax.axis_index("depth")
     flags = jnp.stack([position * (devices // 2), 1 - position]).astype(jnp.int32)
     outs = (STATE, STATE, sent)
@@ -351,42 +360,47 @@
     z, u, send = call(open_kernel, "open", outs, 1, HELD, flags, held, before, weights)
     received = exchange(send)
     packed = jax.ShapeDtypeStruct((2,) + conv_in.shape[1:], jnp.float32)
-    u, z, send, rest, packed = call(
-        functools.partial(step_kernel, 0), "step", outs + (STATE, packed), 2, TWO,
+    u, z, send, ending, begun, rest, packed = call(
+        begin_kernel, "begin", outs + (READY, READY, STATE, packed), 2, TWO,
         flags, received, z, u, conv_out, conv_in,
     )
+    endings, beginnings = [ending], [None, begun]
     moved = swapped(packed)
     received = exchange(send)
     for layer in (1, 2):
-        u, z, send = call(
-            functools.partial(step_kernel, layer), "step", outs, 2, TWO,
+        u, z, send, ending, begun = call(
+            functools.partial(step_kernel, layer), "step", outs + (READY, READY), 2, TWO,
             flags, received, z, u, conv_out, conv_in,
         )
+        endings.append(ending)
+        beginnings.append(begun)
         received = exchange(send)
-    both, ends, send = call(
-        turn_kernel, "turn", (BOTH, STATE, sent), 2, TWO,
+    both, ends, send, ending, coarse_in = call(
+        turn_kernel, "turn", (BOTH, STATE, sent, READY, READY), 2, TWO,
         flags, received, z, u, conv_out, moved,
     )
+    endings.append(ending)
     arrived = swapped(both)
     received = exchange(send)
     first, z, send = call(
         fork_kernel, "fork", outs, 2, TWO,
-        flags, received, arrived, both, rest, conv_out, conv_in, moved,
+        flags, received, arrived, both, rest, coarse_in, endings[0], beginnings[1],
     )
     received = exchange(send)
     u, z, send = call(
-        coarse_kernel, "coarse", outs, 2, TWO,
-        flags, received, z, first, conv_out, conv_in, moved,
+        coarse_kernel, "coarse", outs, 2, TWO + WEIGHTS,
+        flags, received, z, first, moved, endings[1], beginnings[2],
     )
     coarse = swapped(u)
     received = exchange(send)
     u, z, send = call(
-        second_kernel, "second", outs, 2, TWO, flags, received, z, u, conv_out, conv_in
+        second_kernel, "second", outs, 2, TWO, flags, received, z, u, endings[2], beginnings[3]
     )
     received = exchange(send)
     (result,) = call(
         close_kernel, "close", (STATE,), 1, CLOSE,
-        flags, received, z, u, conv_out, arrived, first, coarse, out_space=pl.BlockSpec(memory_space=pltpu.HBM),
+        flags, received, z, u, endings[3], arrived, first, coarse,
+        out_space=pl.BlockSpec(memory_space=pltpu.HBM),
     )
     return (result[None, None], ends[None, None])
 

time: 148 us -> 147 us (level)
  Pallas kernels: 30 us -> 28.4 us
    pallas_call x9, Pallas kernels: 28 us -> 26.3 us  [call(): pl.pallas_call(kernel, name=name, out_shape=tuple(outs), in_specs=[SMEM]...]
where the time goes in v6:
time: 147 us; the launch traced here: 146 us
  blocking collectives  114 us (78%)
  Pallas kernels  28.4 us (19%)
  starting transfers between devices  2.88 us (2%)
    all_to_all x8, blocking collectives, exchange(): return lax.all_to_all(apart, WORLD, 0, 0).reshape(send.shape)  114 us
    pallas_call x9, Pallas kernels, call(): pl.pallas_call(kernel, name=name, out_shape=tuple(outs), in_specs=[SMEM]...  26.3 us
  transfers between devices with their start and end apart: 4, of which 0 were waited for; matrix products, arithmetic and copies ran while one was open for 0% of the time, Pallas kernels for 8%

profile of v6, /device:TPU:1, one launch (start us, length us, event | category | flops | bytes accessed | tf_op | source)
XLA Modules:
  0.0 146.3 jit_solution(2941771796554026186)
XLA Ops:
  0.6 1.5 %collective-permute-start = (f32[32,32,128]{2,1,0:T(8,128)}, f32[32,32,128]{2,1,0:T(8,128)S(1)}, u32[]{:S(2)}, u32[]{:S(2)}) collective-permute-start(f32[32,32,128]{2,1,0:T(8,128)} %bitcast.40), channel_id=1, source_target_pairs={{0,64},{64,0},{1,65},{65,1},{2,66},{66,2},{3,67},{67,3},{4,68},{68... | collective-permute-start | bytes 1572872 | tf_op jit(solution)/shard_map/ppermute | solution.py:343
  2.1 0.1 pad_add_fusion.flags_ref
  2.2 2.1 %ready.1 = (f32[32,32,128]{2,1,0:T(8,128)S(1)}, bf16[4,128,768]{2,1,0:T(8,128)(2,1)S(1)}) custom-call(s32[2]{0:T(128)S(1)} %pad_add_fusion.flags_ref, f32[32,32,128]{2,1,0:T(8,128)} %bitcast.39, f32[4,3,3,128,128]{4,3,2,1,0:T(8,128)} %win_ref.5), custom_call_target="tpu_custom_call" | custom-call | flops 1000 | bytes 3000000 | tf_op jit(solution)/shard_map/ready/pallas_call | solution.py:327
  4.3 1.8 %open.1 = (f32[32,32,128]{2,1,0:T(8,128)S(1)}, f32[32,32,128]{2,1,0:T(8,128)S(1)}, f32[256,128]{1,0:T(8,128)S(1)}) custom-call(s32[2]{0:T(128)S(1)} %pad_add_fusion.flags_ref, f32[32,32,128]{2,1,0:T(8,128)S(1)} %get-tuple-element.38.initial_ref, f32[32,32,128]{2,1,0:T(8,128)S(1)} %collective-permute-done.before_ref, ...), custom_call_target="tpu_custom_call" | custom-call | flops 805306368 | bytes 3014664 | tf_op jit(solution)/shard_map/open/pallas_call | solution.py:311
  6.1 20.0 %all_to_all.40 = f32[128,2,128]{2,1,0:T(2,128)S(1)} all-to-all(f32[128,2,128]{2,1,0:T(2,128)S(1)} %bitcast.37), channel_id=1, replica_groups=mesh['depth'=2,'batch_0'=4,'batch_1'=4,'batch_2'=4] {'depth','batch_0','..., dimensions={0} | all-to-all | bytes 262144 | tf_op jit(solution)/shard_map/all_to_all | solution.py:348
  26.1 3.3 %begin.1 = (f32[32,32,128]{2,1,0:T(8,128)S(1)}, f32[32,32,128]{2,1,0:T(8,128)S(1)}, f32[256,128]{1,0:T(8,128)S(1)}, bf16[4,128,768]{2,1,0:T(8,128)(2,1)S(1)}, bf...) custom-call(s32[2]{0:T(128)S(1)} %pad_add_fusion.flags_ref, ...), custom_call_target="tpu_custom_call" | custom-call | flops 1610612736 | bytes 10354696 | tf_op jit(solution)/shard_map/begin/pallas_call | solution.py:311
  29.4 0.6 collective-permute-start.1
  30.0 13.2 %all_to_all.41 = f32[128,2,128]{2,1,0:T(2,128)S(1)} all-to-all(f32[128,2,128]{2,1,0:T(2,128)S(1)} %bitcast.23), channel_id=1, replica_groups=mesh['depth'=2,'batch_0'=4,'batch_1'=4,'batch_2'=4] {'depth','batch_0','..., dimensions={0} | all-to-all | bytes 262144 | tf_op jit(solution)/shard_map/all_to_all | solution.py:348
  43.2 3.3 %step.2 = (f32[32,32,128]{2,1,0:T(8,128)S(1)}, f32[32,32,128]{2,1,0:T(8,128)S(1)}, f32[256,128]{1,0:T(8,128)S(1)}, bf16[4,128,768]{2,1,0:T(8,128)(2,1)S(1)}, bf16[4,128,768]{2,1,0:T(8,128)(2,1)S(1)}) custom-call(s32[2]{0:T(128)S(1)} %pad_add_fusion.flags_ref, f32[256,128]{1,0:T(8,128)S(1)} %bitcast.32, f32[32,32,128]{2,1,0:T(8,128)S(1)} %get-tuple-element.44.z_ref, ...), custom_call_target="tpu_custom_call" | custom-call | flops 1610612736 | bytes 8650760 | tf_op jit(solution)/shard_map/step/pallas_call | solution.py:311
  46.5 13.7 %all_to_all.42 = f32[128,2,128]{2,1,0:T(2,128)S(1)} all-to-all(f32[128,2,128]{2,1,0:T(2,128)S(1)} %bitcast.33), channel_id=1, replica_groups=mesh['depth'=2,'batch_0'=4,'batch_1'=4,'batch_2'=4] {'depth','batch_0','..., dimensions={0} | all-to-all | bytes 262144 | tf_op jit(solution)/shard_map/all_to_all | solution.py:348
  60.2 3.3 %step.3 = (f32[32,32,128]{2,1,0:T(8,128)S(1)}, f32[32,32,128]{2,1,0:T(8,128)S(1)}, f32[256,128]{1,0:T(8,128)S(1)}, bf16[4,128,768]{2,1,0:T(8,128)(2,1)S(1)}, bf16[4,128,768]{2,1,0:T(8,128)(2,1)S(1)}) custom-call(s32[2]{0:T(128)S(1)} %pad_add_fusion.flags_ref, f32[256,128]{1,0:T(8,128)S(1)} %bitcast.34, f32[32,32,128]{2,1,0:T(8,128)S(1)} %get-tuple-element.47.z_ref, ...), custom_call_target="tpu_custom_call" | custom-call | flops 1610612736 | bytes 8650760 | tf_op jit(solution)/shard_map/step/pallas_call | solution.py:311
  63.5 13.7 %all_to_all.43 = f32[128,2,128]{2,1,0:T(2,128)S(1)} all-to-all(f32[128,2,128]{2,1,0:T(2,128)S(1)} %bitcast.35), channel_id=1, replica_groups=mesh['depth'=2,'batch_0'=4,'batch_1'=4,'batch_2'=4] {'depth','batch_0','..., dimensions={0} | all-to-all | bytes 262144 | tf_op jit(solution)/shard_map/all_to_all | solution.py:348
  77.2 3.2 %turn.1 = (f32[2,32,32,128]{3,2,1,0:T(8,128)S(1)}, f32[32,32,128]{2,1,0:T(8,128)}, f32[256,128]{1,0:T(8,128)S(1)}, bf16[4,128,768]{2,1,0:T(8,128)(2,1)S(1)}, bf16[4,128,768]{2,1,0:T(8,128)(2,1)S(1)}) custom-call(s32[2]{0:T(128)S(1)} %pad_add_fusion.flags_ref, f32[256,128]{1,0:T(8,128)S(1)} %bitcast.25, f32[32,32,128]{2,1,0:T(8,128)S(1)} %get-tuple-element.50.z_ref, ...), custom_call_target="tpu_custom_call" | custom-call | flops 1610612736 | bytes 7995400 | tf_op jit(solution)/shard_map/turn/pallas_call | solution.py:311
  80.4 0.6 collective-permute-start.2
  81.0 13.2 %all_to_all.44 = f32[128,2,128]{2,1,0:T(2,128)S(1)} all-to-all(f32[128,2,128]{2,1,0:T(2,128)S(1)} %bitcast.26), channel_id=1, replica_groups=mesh['depth'=2,'batch_0'=4,'batch_1'=4,'batch_2'=4] {'depth','batch_0','..., dimensions={0} | all-to-all | bytes 262144 | tf_op jit(solution)/shard_map/all_to_all | solution.py:348
  94.2 0.0 collective-permute-done.2.arrived_ref
  94.2 2.9 %fork.1 = (f32[32,32,128]{2,1,0:T(8,128)S(1)}, f32[32,32,128]{2,1,0:T(8,128)S(1)}, f32[256,128]{1,0:T(8,128)S(1)}) custom-call(s32[2]{0:T(128)S(1)} %pad_add_fusion.flags_ref, f32[256,128]{1,0:T(8,128)S(1)} %bitcast.24, f32[2,32,32,128]{3,2,1,0:T(8,128)S(1)} %collective-permute-done.2.arrived_ref, f32[2,32,32,128]{3,2,1,0:T(8,128)S(1)} %get-tuple-element.54.both_ref, ...), custom_call_target="tpu_custom_call" | custom-call | flops 1610612736 | bytes 6291464 | tf_op jit(solution)/shard_map/fork/pallas_call | solution.py:311
  97.1 13.3 %all_to_all.45 = f32[128,2,128]{2,1,0:T(2,128)S(1)} all-to-all(f32[128,2,128]{2,1,0:T(2,128)S(1)} %bitcast.30), channel_id=1, replica_groups=mesh['depth'=2,'batch_0'=4,'batch_1'=4,'batch_2'=4] {'depth','batch_0','..., dimensions={0} | all-to-all | bytes 262144 | tf_op jit(solution)/shard_map/all_to_all | solution.py:348
  110.4 3.0 %coarse.1 = (f32[32,32,128]{2,1,0:T(8,128)S(1)}, f32[32,32,128]{2,1,0:T(8,128)S(1)}, f32[256,128]{1,0:T(8,128)S(1)}) custom-call(s32[2]{0:T(128)S(1)} %pad_add_fusion.flags_ref, f32[256,128]{1,0:T(8,128)S(1)} %bitcast.29, f32[32,32,128]{2,1,0:T(8,128)S(1)} %get-tuple-element.60.z_ref, f32[32,32,128]{2,1,0:T(8,128)S(1)} %get-tuple-element.61.u_ref.first_ref, ...), custom_call_target="tpu_custom_call" | custom-call | flops 1610612736 | bytes 5111816 | tf_op jit(solution)/shard_map/coarse/pallas_call | solution.py:311
  113.4 0.1 collective-permute-start.3
  113.5 13.7 %all_to_all.46 = f32[128,2,128]{2,1,0:T(2,128)S(1)} all-to-all(f32[128,2,128]{2,1,0:T(2,128)S(1)} %bitcast.27), channel_id=1, replica_groups=mesh['depth'=2,'batch_0'=4,'batch_1'=4,'batch_2'=4] {'depth','batch_0','..., dimensions={0} | all-to-all | bytes 262144 | tf_op jit(solution)/shard_map/all_to_all | solution.py:348
  127.2 3.0 %second.1 = (f32[32,32,128]{2,1,0:T(8,128)S(1)}, f32[32,32,128]{2,1,0:T(8,128)S(1)}, f32[256,128]{1,0:T(8,128)S(1)}) custom-call(s32[2]{0:T(128)S(1)} %pad_add_fusion.flags_ref, f32[256,128]{1,0:T(8,128)S(1)} %bitcast.31, f32[32,32,128]{2,1,0:T(8,128)S(1)} %get-tuple-element.65.refs_1_, f32[32,32,128]{2,1,0:T(8,128)S(1)} %get-tuple-element.66.refs_2_, ...), custom_call_target="tpu_custom_call" | custom-call | flops 1610612736 | bytes 3932168 | tf_op jit(solution)/shard_map/second/pallas_call | solution.py:311
  130.2 13.3 %all_to_all.47 = f32[128,2,128]{2,1,0:T(2,128)S(1)} all-to-all(f32[128,2,128]{2,1,0:T(2,128)S(1)} %bitcast.36), channel_id=1, replica_groups=mesh['depth'=2,'batch_0'=4,'batch_1'=4,'batch_2'=4] {'depth','batch_0','..., dimensions={0} | all-to-all | bytes 262144 | tf_op jit(solution)/shard_map/all_to_all | solution.py:348
  143.5 2.6 %close.1 = f32[32,32,128]{2,1,0:T(8,128)} custom-call(s32[2]{0:T(128)S(1)} %pad_add_fusion.flags_ref, f32[256,128]{1,0:T(8,128)S(1)} %bitcast.22, f32[32,32,128]{2,1,0:T(8,128)S(1)} %get-tuple-element.70.z_ref, f32[32,32,128]{2,1,0:T(8,128)S(1)} %get-tuple-element.71.u_ref, bf16[4,128,768]{2,1,0:T(8,128)(2,1)S(1)} %get-tuple-element.72.ending_ref, ...), custom_call_target="tpu_custom_call" | custom-call | flops 805306368 | bytes 4587528 | tf_op jit(solution)/shard_map/close/pallas_call | solution.py:311
  (7 shorter events, 0.0 us)
Async XLA Ops:
  0.6 3.6 %collective-permute-start = (f32[32,32,128]{2,1,0:T(8,128)}, f32[32,32,128]{2,1,0:T(8,128)S(1)}, u32[]{:S(2)}, u32[]{:S(2)}) collective-permute-start(f32[32,32,128]{2,1,0:T(8,128)} %bitcast.40), channel_id=1, source_target_pairs={{0,64},{64,0},{1,65},{65,1},{2,66},{66,2},{3,67},{67,3},{4,68},{68... | collective-permute-start | bytes 1572872 | tf_op jit(solution)/shard_map/ppermute | solution.py:343
  2.2 23.9 %copy-start = (f32[4,3,3,128,128]{4,3,2,1,0:T(8,128)S(1)}, f32[4,3,3,128,128]{4,3,2,1,0:T(8,128)}, u32[]{:S(2)}) copy-start(f32[4,3,3,128,128]{4,3,2,1,0:T(8,128)} %win_ref.5) | copy-start | bytes 7077892
  2.2 23.9 %copy-start.1 = (f32[4,3,3,128,128]{4,3,2,1,0:T(8,128)S(1)}, f32[4,3,3,128,128]{4,3,2,1,0:T(8,128)}, u32[]{:S(2)}) copy-start(f32[4,3,3,128,128]{4,3,2,1,0:T(8,128)} %wout_ref.7) | copy-start | bytes 7077892
  29.4 47.8 %collective-permute-start.1 = (f32[2,3,3,128,128]{4,3,2,1,0:T(8,128)S(1)}, f32[2,3,3,128,128]{4,3,2,1,0:T(8,128)S(1)}, u32[]{:S(2)}, u32[]{:S(2)}) collective-permute-start(f32[2,3,3,128,128]{4,3,2,1,0:T(8,128)S(1)} %get-tuple-element.52), channel_id=1, source_target_pairs={{0,64},{64,0},{1,65},{65,1},{2,66},{66,2},{3,67},{67,3},{4,68},{68... | collective-permute-start | bytes 3538952 | tf_op jit(solution)/shard_map/ppermute | solution.py:343
  80.4 13.9 %collective-permute-start.2 = (f32[2,32,32,128]{3,2,1,0:T(8,128)S(1)}, f32[2,32,32,128]{3,2,1,0:T(8,128)S(1)}, u32[]{:S(2)}, u32[]{:S(2)}) collective-permute-start(f32[2,32,32,128]{3,2,1,0:T(8,128)S(1)} %get-tuple-element.54.both_ref), channel_id=1, source_target_pairs={{0,64},{64,0},{1,65},{65,1},{2,66},{66,2},{3,67},{67,3},{4,68},{68... | collective-permute-start | bytes 3145736 | tf_op jit(solution)/shard_map/ppermute | solution.py:343
  113.4 30.1 %collective-permute-start.3 = (f32[32,32,128]{2,1,0:T(8,128)S(1)}, f32[32,32,128]{2,1,0:T(8,128)S(1)}, u32[]{:S(2)}, u32[]{:S(2)}) collective-permute-start(f32[32,32,128]{2,1,0:T(8,128)S(1)} %get-tuple-element.66.refs_2_), channel_id=1, source_target_pairs={{0,64},{64,0},{1,65},{65,1},{2,66},{66,2},{3,67},{67,3},{4,68},{68... | collective-permute-start | bytes 1572872 | tf_op jit(solution)/shard_map/ppermute | solution.py:343

commit v7 on v6

--- a/solution.py
+++ b/solution.py
@@ -109,9 +109,17 @@
     send_ref[...] = jnp.where(is_sum, total, square)
 
 
+def core():
+    return lax.axis_index("depth")
+
+
+def own_rows(received_ref):
+    return core() * (received_ref.shape[0] // 2)
+
+
 def combined(received_ref, base):
     samples = received_ref.shape[0] // 4
-    rows = received_ref[pl.ds(pl.multiple_of(2 * base, 2 * samples), 2 * samples), :]
+    rows = received_ref[pl.ds(pl.multiple_of(base, 2 * samples), 2 * samples), :]
     is_sum = lax.broadcasted_iota(jnp.int32, rows.shape, 0) % 2 == 0
     average = jnp.sum(jnp.where(is_sum, rows, 0.0), axis=0, keepdims=True) * (1.0 / (samples * CELLS))
     away = rows * (1.0 / CELLS) - average
@@ -145,7 +153,7 @@
             weights_ref[kind, :, (3 + across) * CHANNELS : (4 + across) * CHANNELS] = low
 
 
-def ready_kernel(flags_ref, initial_hbm, win_hbm, initial_ref, weights_ref, raw_ref, sem):
+def ready_kernel(initial_hbm, win_hbm, initial_ref, weights_ref, raw_ref, sem):
     weights = pltpu.make_async_copy(win_hbm.at[pl.ds(0, 1)], raw_ref, sem.at[0])
     state = pltpu.make_async_copy(initial_hbm, initial_ref, sem.at[1])
     weights.start()
@@ -155,8 +163,8 @@
     state.wait()
 
 
-def open_kernel(flags_ref, initial_ref, before_ref, weights_ref, z_ref, u_ref, send_ref, held_ref):
-    first = flags_ref[1] == 1
+def open_kernel(initial_ref, before_ref, weights_ref, z_ref, u_ref, send_ref, held_ref):
+    first = core() == 0
     put = placer(held_ref)
     for row in range(ROWS):
         value = jnp.where(first, initial_ref[row], before_ref[row])
@@ -165,18 +173,18 @@
     into_conv(held_ref, weights_ref, z_ref, send_ref)
 
 
-def fine_step(flags_ref, received_ref, z_ref, u_ref, ending_ref, begun_ref, unew_ref, znew_ref, send_ref, held_ref, onto_ref):
-    normalise(received_ref, flags_ref[0], z_ref, held_ref)
+def fine_step(received_ref, z_ref, u_ref, ending_ref, begun_ref, unew_ref, znew_ref, send_ref, held_ref, onto_ref):
+    normalise(received_ref, own_rows(received_ref), z_ref, held_ref)
     add_branch(held_ref, ending_ref, STEP_SIZE, u_ref, unew_ref, onto_ref)
     into_conv(onto_ref, begun_ref, znew_ref, send_ref)
 
 
 def begin_kernel(
-    flags_ref, received_ref, z_ref, u_ref, wout_ref, win_ref,
+    received_ref, z_ref, u_ref, wout_ref, win_ref,
     unew_ref, znew_ref, send_ref, ending_ref, begun_ref, rest_ref, packed_ref, held_ref, onto_ref,
 ):
     split_weights(wout_ref, 0, ending_ref)
-    normalise(received_ref, flags_ref[0], z_ref, held_ref)
+    normalise(received_ref, own_rows(received_ref), z_ref, held_ref)
     put = placer(onto_ref)
     for row, block in branch_blocks(held_ref, ending_ref):
         before = u_ref[row]
@@ -192,22 +200,22 @@
 
 
 def step_kernel(
-    layer, flags_ref, received_ref, z_ref, u_ref, wout_ref, win_ref,
+    layer, received_ref, z_ref, u_ref, wout_ref, win_ref,
     unew_ref, znew_ref, send_ref, ending_ref, begun_ref, held_ref, onto_ref,
 ):
     split_weights(wout_ref, layer, ending_ref)
-    normalise(received_ref, flags_ref[0], z_ref, held_ref)
+    normalise(received_ref, own_rows(received_ref), z_ref, held_ref)
     add_branch(held_ref, ending_ref, STEP_SIZE, u_ref, unew_ref, onto_ref)
     split_weights(win_ref, layer + 1, begun_ref)
     into_conv(onto_ref, begun_ref, znew_ref, send_ref)
 
 
 def turn_kernel(
-    flags_ref, received_ref, z_ref, u_ref, wout_ref, moved_ref,
+    received_ref, z_ref, u_ref, wout_ref, moved_ref,
     both_ref, ends_ref, send_ref, ending_ref, begun_ref, held_ref, onto_ref,
 ):
     split_weights(wout_ref, FACTOR - 1, ending_ref)
-    normalise(received_ref, flags_ref[0], z_ref, held_ref)
+    normalise(received_ref, own_rows(received_ref), z_ref, held_ref)
     put = placer(onto_ref)
     for row, block in branch_blocks(held_ref, ending_ref):
         after = u_ref[row] + STEP_SIZE * block
@@ -219,10 +227,10 @@
 
 
 def fork_kernel(
-    flags_ref, received_ref, arrived_ref, both_ref, rest_ref, moved_ref, ending_ref, begun_ref,
+    received_ref, arrived_ref, both_ref, rest_ref, moved_ref, ending_ref, begun_ref,
     unew_ref, znew_ref, send_ref, held_ref, onto_ref,
 ):
-    @pl.when(flags_ref[1] == 1)
+    @pl.when(core() == 0)
     def _():
         put = placer(held_ref)
         for row in range(ROWS):
@@ -231,7 +239,7 @@
             put(row, value)
         into_conv(held_ref, moved_ref, znew_ref, send_ref)
 
-    @pl.when(flags_ref[1] == 0)
+    @pl.when(core() == 1)
     def _():
         normalise(received_ref, 0, arrived_ref.at[1], held_ref)
         add_branch(held_ref, ending_ref, STEP_SIZE, arrived_ref.at[0], unew_ref, onto_ref)
@@ -239,42 +247,42 @@
 
 
 def coarse_kernel(
-    flags_ref, received_ref, z_ref, u_ref, moved_ref, ending_ref, begun_ref,
+    received_ref, z_ref, u_ref, moved_ref, ending_ref, begun_ref,
     unew_ref, znew_ref, send_ref, held_ref, onto_ref, weights_ref,
 ):
-    @pl.when(flags_ref[1] == 1)
+    @pl.when(core() == 0)
     def _():
         split_weights(moved_ref, 1, weights_ref)
-        normalise(received_ref, flags_ref[0], z_ref, held_ref)
+        normalise(received_ref, own_rows(received_ref), z_ref, held_ref)
         add_branch(held_ref, weights_ref, FACTOR * STEP_SIZE, u_ref, unew_ref)
 
-    @pl.when(flags_ref[1] == 0)
+    @pl.when(core() == 1)
     def _():
         fine_step(
-            flags_ref, received_ref, z_ref, u_ref, ending_ref, begun_ref,
+            received_ref, z_ref, u_ref, ending_ref, begun_ref,
             unew_ref, znew_ref, send_ref, held_ref, onto_ref,
         )
 
 
-def second_kernel(flags_ref, *refs):
-    @pl.when(flags_ref[1] == 0)
-    def _():
-        fine_step(flags_ref, *refs)
+def second_kernel(*refs):
+    @pl.when(core() == 1)
+    def _():
+        fine_step(*refs)
 
 
 def close_kernel(
-    flags_ref, received_ref, z_ref, u_ref, ending_ref, arrived_ref, first_ref, coarse_ref, out_hbm,
+    received_ref, z_ref, u_ref, ending_ref, arrived_ref, first_ref, coarse_ref, out_hbm,
     held_ref, out_ref, sem,
 ):
-    @pl.when(flags_ref[1] == 1)
+    @pl.when(core() == 0)
     def _():
         copy = pltpu.make_async_copy(first_ref, out_hbm, sem.at[0])
         copy.start()
         copy.wait()
 
-    @pl.when(flags_ref[1] == 0)
-    def _():
-        normalise(received_ref, flags_ref[0], z_ref, held_ref)
+    @pl.when(core() == 1)
+    def _():
+        normalise(received_ref, own_rows(received_ref), z_ref, held_ref)
         copies = []
         for row, block in branch_blocks(held_ref, ending_ref):
             fine = u_ref[row] + STEP_SIZE * block
@@ -293,7 +301,6 @@
 
 STATE = jax.ShapeDtypeStruct((ROWS, COLS, CHANNELS), jnp.float32)
 BOTH = jax.ShapeDtypeStruct((2, ROWS, COLS, CHANNELS), jnp.float32)
-SMEM = pl.BlockSpec(memory_space=pltpu.SMEM)
 VMEM = pl.BlockSpec(memory_space=pltpu.VMEM)
 HELD = [pltpu.VMEM((4, PAIRS * COLS, 2 * CHANNELS), jnp.bfloat16)]
 WEIGHTS = [pltpu.VMEM((4, CHANNELS, 6 * CHANNELS), jnp.bfloat16)]
@@ -312,7 +319,7 @@
         kernel,
         name=name,
         out_shape=tuple(outs),
-        in_specs=[SMEM] + [VMEM] * (len(args) - 1),
+        in_specs=[VMEM] * len(args),
         out_specs=(out_space,) * len(outs),
         scratch_shapes=scratch,
         compiler_params=pltpu.CompilerParams(vmem_limit_bytes=VMEM_LIMIT),
@@ -322,13 +329,13 @@
     )(*args)
 
 
-def ready(flags, initial, conv_in):
+def ready(initial, conv_in):
     shape = conv_in.shape[1:]
     return pl.pallas_call(
         ready_kernel,
         name="ready",
         out_shape=(STATE, READY),
-        in_specs=[SMEM] + [pl.BlockSpec(memory_space=pltpu.HBM)] * 2,
+        in_specs=[pl.BlockSpec(memory_space=pltpu.HBM)] * 2,
         out_specs=(VMEM,) * 2,
         scratch_shapes=[
             pltpu.VMEM((1,) + shape, jnp.float32),
@@ -336,7 +343,7 @@
         ],
         compiler_params=pltpu.CompilerParams(vmem_limit_bytes=READY_LIMIT),
         cost_estimate=pl.CostEstimate(flops=1000, bytes_accessed=3000000, transcendentals=0),
-    )(flags, *(pltpu.with_memory_space_constraint(x, pltpu.HBM) for x in (initial, conv_in)))
+    )(*(pltpu.with_memory_space_constraint(x, pltpu.HBM) for x in (initial, conv_in)))
 
 
 def swapped(x):
@@ -351,18 +358,16 @@
 def body(initial, guess, conv_in, conv_out):
     devices = lax.axis_size(WORLD)
     sent = jax.ShapeDtypeStruct((2 * devices, CHANNELS), jnp.float32)
-    position = lax.axis_index("depth")
-    flags = jnp.stack([position * (devices // 2), 1 - position]).astype(jnp.int32)
     outs = (STATE, STATE, sent)
 
     before = swapped(guess[0, 0])
-    held, weights = ready(flags, initial[0], conv_in)
-    z, u, send = call(open_kernel, "open", outs, 1, HELD, flags, held, before, weights)
+    held, weights = ready(initial[0], conv_in)
+    z, u, send = call(open_kernel, "open", outs, 1, HELD, held, before, weights)
     received = exchange(send)
     packed = jax.ShapeDtypeStruct((2,) + conv_in.shape[1:], jnp.float32)
     u, z, send, ending, begun, rest, packed = call(
         begin_kernel, "begin", outs + (READY, READY, STATE, packed), 2, TWO,
-        flags, received, z, u, conv_out, conv_in,
+        received, z, u, conv_out, conv_in,
     )
     endings, beginnings = [ending], [None, begun]
     moved = swapped(packed)
@@ -370,36 +375,36 @@
     for layer in (1, 2):
         u, z, send, ending, begun = call(
             functools.partial(step_kernel, layer), "step", outs + (READY, READY), 2, TWO,
-            flags, received, z, u, conv_out, conv_in,
+            received, z, u, conv_out, conv_in,
         )
         endings.append(ending)
         beginnings.append(begun)
         received = exchange(send)
     both, ends, send, ending, coarse_in = call(
         turn_kernel, "turn", (BOTH, STATE, sent, READY, READY), 2, TWO,
-        flags, received, z, u, conv_out, moved,
+        received, z, u, conv_out, moved,
     )
     endings.append(ending)
     arrived = swapped(both)
     received = exchange(send)
     first, z, send = call(
         fork_kernel, "fork", outs, 2, TWO,
-        flags, received, arrived, both, rest, coarse_in, endings[0], beginnings[1],
+        received, arrived, both, rest, coarse_in, endings[0], beginnings[1],
     )
     received = exchange(send)
     u, z, send = call(
         coarse_kernel, "coarse", outs, 2, TWO + WEIGHTS,
-        flags, received, z, first, moved, endings[1], beginnings[2],
+        received, z, first, moved, endings[1], beginnings[2],
     )
     coarse = swapped(u)
     received = exchange(send)
     u, z, send = call(
-        second_kernel, "second", outs, 2, TWO, flags, received, z, u, endings[2], beginnings[3]
+        second_kernel, "second", outs, 2, TWO, received, z, u, endings[2], beginnings[3]
     )
     received = exchange(send)
     (result,) = call(
         close_kernel, "close", (STATE,), 1, CLOSE,
-        flags, received, z, u, endings[3], arrived, first, coarse,
+        received, z, u, endings[3], arrived, first, coarse,
         out_space=pl.BlockSpec(memory_space=pltpu.HBM),
     )
     return (result[None, None], ends[None, None])

time: 147 us -> 140 us (0.952)
  Pallas kernels: 28.4 us -> 21.8 us
    pallas_call x9, Pallas kernels: 26.3 us -> 20.4 us  [call(): pl.pallas_call(kernel, name=name, out_shape=tuple(outs), in_specs=[VMEM]...]
  transfers between devices with their start and end apart: 4 -> 4, of which waited for: 0 -> 1; matrix products, arithmetic and copies ran while one was open for 0% -> 0% of each run, Pallas kernels for 8% -> 6%
where the time goes in v7:
time: 140 us
  blocking collectives  114 us (81%)
  Pallas kernels  21.8 us (16%)
  starting transfers between devices  2.87 us (2%)
    all_to_all x8, blocking collectives, exchange(): return lax.all_to_all(apart, WORLD, 0, 0).reshape(send.shape)  114 us
    pallas_call x9, Pallas kernels, call(): pl.pallas_call(kernel, name=name, out_shape=tuple(outs), in_specs=[VMEM]...  20.4 us
    ppermute x4, starting transfers between devices, swapped(): return lax.ppermute(x, 'depth', [(0, 1), (1, 0)])  2.87 us
  transfers between devices with their start and end apart: 4, of which 1 were waited for; matrix products, arithmetic and copies ran while one was open for 0% of the time, Pallas kernels for 6%

profile of v7, /device:TPU:1, one launch (start us, length us, event | category | flops | bytes accessed | tf_op | source)
XLA Modules:
  0.0 140.2 jit_solution(7206789816043558678)
XLA Ops:
  0.6 1.5 %collective-permute-start = (f32[32,32,128]{2,1,0:T(8,128)}, f32[32,32,128]{2,1,0:T(8,128)S(1)}, u32[]{:S(2)}, u32[]{:S(2)}) collective-permute-start(f32[32,32,128]{2,1,0:T(8,128)} %bitcast.38), channel_id=1, source_target_pairs={{0,64},{64,0},{1,65},{65,1},{2,66},{66,2},{3,67},{67,3},{4,68},{68... | collective-permute-start | bytes 1572872 | tf_op jit(solution)/shard_map/ppermute | solution.py:350
  2.1 1.4 ready.1
  3.5 0.3 collective-permute-done.before_ref
  3.9 1.2 open.1
  5.0 20.3 %all_to_all.40 = f32[128,2,128]{2,1,0:T(2,128)S(1)} all-to-all(f32[128,2,128]{2,1,0:T(2,128)S(1)} %bitcast.35), channel_id=1, replica_groups=mesh['depth'=2,'batch_0'=4,'batch_1'=4,'batch_2'=4] {'depth','batch_0','..., dimensions={0} | all-to-all | bytes 262144 | tf_op jit(solution)/shard_map/all_to_all | solution.py:355
  25.3 2.6 %begin.1 = (f32[32,32,128]{2,1,0:T(8,128)S(1)}, f32[32,32,128]{2,1,0:T(8,128)S(1)}, f32[256,128]{1,0:T(8,128)S(1)}, bf16[4,128,768]{2,1,0:T(8,128)(2,1)S(1)}, bf...) custom-call(f32[256,128]{1,0:T(8,128)S(1)} %bitcast.26, ...), custom_call_target="tpu_custom_call" | custom-call | flops 1610612736 | bytes 10354688 | tf_op jit(solution)/shard_map/begin/pallas_call | solution.py:318
  28.0 0.6 collective-permute-start.1
  28.6 13.2 %all_to_all.41 = f32[128,2,128]{2,1,0:T(2,128)S(1)} all-to-all(f32[128,2,128]{2,1,0:T(2,128)S(1)} %bitcast.21), channel_id=1, replica_groups=mesh['depth'=2,'batch_0'=4,'batch_1'=4,'batch_2'=4] {'depth','batch_0','..., dimensions={0} | all-to-all | bytes 262144 | tf_op jit(solution)/shard_map/all_to_all | solution.py:355
  41.8 2.6 %step.2 = (f32[32,32,128]{2,1,0:T(8,128)S(1)}, f32[32,32,128]{2,1,0:T(8,128)S(1)}, f32[256,128]{1,0:T(8,128)S(1)}, bf16[4,128,768]{2,1,0:T(8,128)(2,1)S(1)}, bf16[4,128,768]{2,1,0:T(8,128)(2,1)S(1)}) custom-call(f32[256,128]{1,0:T(8,128)S(1)} %bitcast.30, f32[32,32,128]{2,1,0:T(8,128)S(1)} %get-tuple-element.44.z_ref, ...), custom_call_target="tpu_custom_call" | custom-call | flops 1610612736 | bytes 8650752 | tf_op jit(solution)/shard_map/step/pallas_call | solution.py:318
  44.4 13.7 %all_to_all.42 = f32[128,2,128]{2,1,0:T(2,128)S(1)} all-to-all(f32[128,2,128]{2,1,0:T(2,128)S(1)} %bitcast.31), channel_id=1, replica_groups=mesh['depth'=2,'batch_0'=4,'batch_1'=4,'batch_2'=4] {'depth','batch_0','..., dimensions={0} | all-to-all | bytes 262144 | tf_op jit(solution)/shard_map/all_to_all | solution.py:355
  58.1 2.6 %step.3 = (f32[32,32,128]{2,1,0:T(8,128)S(1)}, f32[32,32,128]{2,1,0:T(8,128)S(1)}, f32[256,128]{1,0:T(8,128)S(1)}, bf16[4,128,768]{2,1,0:T(8,128)(2,1)S(1)}, bf16[4,128,768]{2,1,0:T(8,128)(2,1)S(1)}) custom-call(f32[256,128]{1,0:T(8,128)S(1)} %bitcast.32, f32[32,32,128]{2,1,0:T(8,128)S(1)} %get-tuple-element.47.z_ref, ...), custom_call_target="tpu_custom_call" | custom-call | flops 1610612736 | bytes 8650752 | tf_op jit(solution)/shard_map/step/pallas_call | solution.py:318
  60.6 13.7 %all_to_all.43 = f32[128,2,128]{2,1,0:T(2,128)S(1)} all-to-all(f32[128,2,128]{2,1,0:T(2,128)S(1)} %bitcast.33), channel_id=1, replica_groups=mesh['depth'=2,'batch_0'=4,'batch_1'=4,'batch_2'=4] {'depth','batch_0','..., dimensions={0} | all-to-all | bytes 262144 | tf_op jit(solution)/shard_map/all_to_all | solution.py:355
  74.3 2.6 %turn.1 = (f32[2,32,32,128]{3,2,1,0:T(8,128)S(1)}, f32[32,32,128]{2,1,0:T(8,128)}, f32[256,128]{1,0:T(8,128)S(1)}, bf16[4,128,768]{2,1,0:T(8,128)(2,1)S(1)}, bf16[4,128,768]{2,1,0:T(8,128)(2,1)S(1)}) custom-call(f32[256,128]{1,0:T(8,128)S(1)} %bitcast.23, f32[32,32,128]{2,1,0:T(8,128)S(1)} %get-tuple-element.50.z_ref, ...), custom_call_target="tpu_custom_call" | custom-call | flops 1610612736 | bytes 7995392 | tf_op jit(solution)/shard_map/turn/pallas_call | solution.py:318
  76.9 0.6 collective-permute-start.2
  77.5 13.2 %all_to_all.44 = f32[128,2,128]{2,1,0:T(2,128)S(1)} all-to-all(f32[128,2,128]{2,1,0:T(2,128)S(1)} %bitcast.24), channel_id=1, replica_groups=mesh['depth'=2,'batch_0'=4,'batch_1'=4,'batch_2'=4] {'depth','batch_0','..., dimensions={0} | all-to-all | bytes 262144 | tf_op jit(solution)/shard_map/all_to_all | solution.py:355
  90.8 0.0 collective-permute-done.2.arrived_ref
  90.8 2.3 %fork.1 = (f32[32,32,128]{2,1,0:T(8,128)S(1)}, f32[32,32,128]{2,1,0:T(8,128)S(1)}, f32[256,128]{1,0:T(8,128)S(1)}) custom-call(f32[256,128]{1,0:T(8,128)S(1)} %bitcast.22, f32[2,32,32,128]{3,2,1,0:T(8,128)S(1)} %collective-permute-done.2.arrived_ref, f32[2,32,32,128]{3,2,1,0:T(8,128)S(1)} %get-tuple-element.54.both_ref, ...), custom_call_target="tpu_custom_call" | custom-call | flops 1610612736 | bytes 6291456 | tf_op jit(solution)/shard_map/fork/pallas_call | solution.py:318
  93.1 13.3 %all_to_all.45 = f32[128,2,128]{2,1,0:T(2,128)S(1)} all-to-all(f32[128,2,128]{2,1,0:T(2,128)S(1)} %bitcast.28), channel_id=1, replica_groups=mesh['depth'=2,'batch_0'=4,'batch_1'=4,'batch_2'=4] {'depth','batch_0','..., dimensions={0} | all-to-all | bytes 262144 | tf_op jit(solution)/shard_map/all_to_all | solution.py:355
  106.4 2.3 %coarse.1 = (f32[32,32,128]{2,1,0:T(8,128)S(1)}, f32[32,32,128]{2,1,0:T(8,128)S(1)}, f32[256,128]{1,0:T(8,128)S(1)}) custom-call(f32[256,128]{1,0:T(8,128)S(1)} %bitcast.27, f32[32,32,128]{2,1,0:T(8,128)S(1)} %get-tuple-element.60.z_ref, f32[32,32,128]{2,1,0:T(8,128)S(1)} %get-tuple-element.61.u_ref.first_ref, ...), custom_call_target="tpu_custom_call" | custom-call | flops 1610612736 | bytes 5111808 | tf_op jit(solution)/shard_map/coarse/pallas_call | solution.py:318
  108.7 0.1 collective-permute-start.3
  108.8 13.7 %all_to_all.46 = f32[128,2,128]{2,1,0:T(2,128)S(1)} all-to-all(f32[128,2,128]{2,1,0:T(2,128)S(1)} %bitcast.25), channel_id=1, replica_groups=mesh['depth'=2,'batch_0'=4,'batch_1'=4,'batch_2'=4] {'depth','batch_0','..., dimensions={0} | all-to-all | bytes 262144 | tf_op jit(solution)/shard_map/all_to_all | solution.py:355
  122.5 2.3 %second.1 = (f32[32,32,128]{2,1,0:T(8,128)S(1)}, f32[32,32,128]{2,1,0:T(8,128)S(1)}, f32[256,128]{1,0:T(8,128)S(1)}) custom-call(f32[256,128]{1,0:T(8,128)S(1)} %bitcast.29, f32[32,32,128]{2,1,0:T(8,128)S(1)} %get-tuple-element.65.refs_1_, f32[32,32,128]{2,1,0:T(8,128)S(1)} %get-tuple-element.66.refs_2_, bf16[4,128,768]{2,1,0:T(8,128)(2,1)S(1)} %get-tuple-element.67.refs_3_, ...), custom_call_target="tpu_custom_call" | custom-call | flops 1610612736 | bytes 3932160 | tf_op jit(solution)/shard_map/second/pallas_call | solution.py:318
  124.8 13.3 %all_to_all.47 = f32[128,2,128]{2,1,0:T(2,128)S(1)} all-to-all(f32[128,2,128]{2,1,0:T(2,128)S(1)} %bitcast.34), channel_id=1, replica_groups=mesh['depth'=2,'batch_0'=4,'batch_1'=4,'batch_2'=4] {'depth','batch_0','..., dimensions={0} | all-to-all | bytes 262144 | tf_op jit(solution)/shard_map/all_to_all | solution.py:355
  138.1 2.0 %close.1 = f32[32,32,128]{2,1,0:T(8,128)} custom-call(f32[256,128]{1,0:T(8,128)S(1)} %bitcast.20, f32[32,32,128]{2,1,0:T(8,128)S(1)} %get-tuple-element.70.z_ref, f32[32,32,128]{2,1,0:T(8,128)S(1)} %get-tuple-element.71.u_ref, bf16[4,128,768]{2,1,0:T(8,128)(2,1)S(1)} %get-tuple-element.72.ending_ref, ...), custom_call_target="tpu_custom_call" | custom-call | flops 805306368 | bytes 4587520 | tf_op jit(solution)/shard_map/close/pallas_call | solution.py:318
  (6 shorter events, 0.0 us)
Async XLA Ops:
  0.6 3.2 %collective-permute-start = (f32[32,32,128]{2,1,0:T(8,128)}, f32[32,32,128]{2,1,0:T(8,128)S(1)}, u32[]{:S(2)}, u32[]{:S(2)}) collective-permute-start(f32[32,32,128]{2,1,0:T(8,128)} %bitcast.38), channel_id=1, source_target_pairs={{0,64},{64,0},{1,65},{65,1},{2,66},{66,2},{3,67},{67,3},{4,68},{68... | collective-permute-start | bytes 1572872 | tf_op jit(solution)/shard_map/ppermute | solution.py:350
  2.1 23.2 %copy-start = (f32[4,3,3,128,128]{4,3,2,1,0:T(8,128)S(1)}, f32[4,3,3,128,128]{4,3,2,1,0:T(8,128)}, u32[]{:S(2)}) copy-start(f32[4,3,3,128,128]{4,3,2,1,0:T(8,128)} %win_ref.5) | copy-start | bytes 7077892
  2.1 23.2 %copy-start.1 = (f32[4,3,3,128,128]{4,3,2,1,0:T(8,128)S(1)}, f32[4,3,3,128,128]{4,3,2,1,0:T(8,128)}, u32[]{:S(2)}) copy-start(f32[4,3,3,128,128]{4,3,2,1,0:T(8,128)} %wout_ref.7) | copy-start | bytes 7077892
  28.0 46.4 %collective-permute-start.1 = (f32[2,3,3,128,128]{4,3,2,1,0:T(8,128)S(1)}, f32[2,3,3,128,128]{4,3,2,1,0:T(8,128)S(1)}, u32[]{:S(2)}, u32[]{:S(2)}) collective-permute-start(f32[2,3,3,128,128]{4,3,2,1,0:T(8,128)S(1)} %get-tuple-element.52), channel_id=1, source_target_pairs={{0,64},{64,0},{1,65},{65,1},{2,66},{66,2},{3,67},{67,3},{4,68},{68... | collective-permute-start | bytes 3538952 | tf_op jit(solution)/shard_map/ppermute | solution.py:350
  76.9 13.9 %collective-permute-start.2 = (f32[2,32,32,128]{3,2,1,0:T(8,128)S(1)}, f32[2,32,32,128]{3,2,1,0:T(8,128)S(1)}, u32[]{:S(2)}, u32[]{:S(2)}) collective-permute-start(f32[2,32,32,128]{3,2,1,0:T(8,128)S(1)} %get-tuple-element.54.both_ref), channel_id=1, source_target_pairs={{0,64},{64,0},{1,65},{65,1},{2,66},{66,2},{3,67},{67,3},{4,68},{68... | collective-permute-start | bytes 3145736 | tf_op jit(solution)/shard_map/ppermute | solution.py:350
  108.7 29.4 %collective-permute-start.3 = (f32[32,32,128]{2,1,0:T(8,128)S(1)}, f32[32,32,128]{2,1,0:T(8,128)S(1)}, u32[]{:S(2)}, u32[]{:S(2)}) collective-permute-start(f32[32,32,128]{2,1,0:T(8,128)S(1)} %get-tuple-element.66.refs_2_), channel_id=1, source_target_pairs={{0,64},{64,0},{1,65},{65,1},{2,66},{66,2},{3,67},{67,3},{4,68},{68... | collective-permute-start | bytes 1572872 | tf_op jit(solution)/shard_map/ppermute | solution.py:350

commit v8 on v7

--- a/solution.py
+++ b/solution.py
@@ -20,10 +20,9 @@
 CHANNELS = 128
 PAIRS = ROWS // 2
 CELLS = ROWS * COLS
-CHUNKS = 2
-PART = PAIRS // CHUNKS
+ENDING_PARTS = (10, 6)
+BEGUN_PARTS = (9, 7)
 VMEM_LIMIT = 24 * 2**20
-READY_LIMIT = 24 * 2**20
 
 
 def split(x):
@@ -56,9 +55,9 @@
     return add
 
 
-def convolve(held_ref, weights_ref, chunk):
-    many = PART * COLS
-    at = slice(chunk * many, (chunk + 1) * many)
+def convolve(held_ref, weights_ref, first, pairs):
+    many = pairs * COLS
+    at = slice(first * COLS, first * COLS + many)
     wide = 3 * CHANNELS
 
     def product(kind):
@@ -81,30 +80,34 @@
     return across(m0 + (m1 + m2)), across((m1 - m2) - m3)
 
 
+def starts(parts):
+    return [(sum(parts[:i]), pairs) for i, pairs in enumerate(parts)]
+
+
 def branch_blocks(held_ref, weights_ref):
-    for chunk in range(CHUNKS):
-        halves = convolve(held_ref, weights_ref, chunk)
-        for pair in range(PART):
+    for first, pairs in starts(ENDING_PARTS):
+        halves = convolve(held_ref, weights_ref, first, pairs)
+        for pair in range(pairs):
             for half in range(2):
-                yield 2 * (chunk * PART + pair) + half, halves[half][pair * COLS : (pair + 1) * COLS]
+                yield 2 * (first + pair) + half, halves[half][pair * COLS : (pair + 1) * COLS]
 
 
 def into_conv(held_ref, weights_ref, z_ref, send_ref):
     totals, squares = [], []
-    for chunk in range(CHUNKS):
-        halves = convolve(held_ref, weights_ref, chunk)
-        for half, out in enumerate(halves):
-            for pair in range(PART):
-                z_ref[2 * (chunk * PART + pair) + half] = out[pair * COLS : (pair + 1) * COLS]
+    for first, pairs in starts(BEGUN_PARTS):
+        cells = pairs * COLS
+        for half, out in enumerate(convolve(held_ref, weights_ref, first, pairs)):
+            for pair in range(pairs):
+                z_ref[2 * (first + pair) + half] = out[pair * COLS : (pair + 1) * COLS]
             total = jnp.sum(out, axis=0, keepdims=True)
-            away = out - total * (1.0 / (PART * COLS))
-            totals.append(total)
+            away = out - total * (1.0 / cells)
+            totals.append((total, cells))
             squares.append(jnp.sum(away * away, axis=0, keepdims=True))
-    total = functools.reduce(jnp.add, totals)
+    total = functools.reduce(jnp.add, [part for part, _ in totals])
     square = functools.reduce(jnp.add, squares)
-    for part in totals:
-        away = part * (1.0 / (PART * COLS)) - total * (1.0 / CELLS)
-        square = square + (PART * COLS) * (away * away)
+    for part, cells in totals:
+        away = part * (1.0 / cells) - total * (1.0 / CELLS)
+        square = square + cells * (away * away)
     is_sum = lax.broadcasted_iota(jnp.int32, send_ref.shape, 0) % 2 == 0
     send_ref[...] = jnp.where(is_sum, total, square)
 
@@ -153,13 +156,17 @@
             weights_ref[kind, :, (3 + across) * CHANNELS : (4 + across) * CHANNELS] = low
 
 
-def ready_kernel(initial_hbm, win_hbm, initial_ref, weights_ref, raw_ref, sem):
-    weights = pltpu.make_async_copy(win_hbm.at[pl.ds(0, 1)], raw_ref, sem.at[0])
-    state = pltpu.make_async_copy(initial_hbm, initial_ref, sem.at[1])
-    weights.start()
-    state.start()
-    weights.wait()
-    split_weights(raw_ref, 0, weights_ref)
+def ready_kernel(initial_hbm, win_hbm, wout_hbm, initial_ref, begun_ref, ending_ref, raw_ref, sem):
+    weights = [
+        pltpu.make_async_copy(hbm.at[0], raw_ref.at[at], sem.at[at])
+        for at, hbm in enumerate((win_hbm, wout_hbm))
+    ]
+    state = pltpu.make_async_copy(initial_hbm, initial_ref, sem.at[2])
+    for copy in (*weights, state):
+        copy.start()
+    for at, ready_ref in enumerate((begun_ref, ending_ref)):
+        weights[at].wait()
+        split_weights(raw_ref, at, ready_ref)
     state.wait()
 
 
@@ -180,10 +187,9 @@
 
 
 def begin_kernel(
-    received_ref, z_ref, u_ref, wout_ref, win_ref,
-    unew_ref, znew_ref, send_ref, ending_ref, begun_ref, rest_ref, packed_ref, held_ref, onto_ref,
-):
-    split_weights(wout_ref, 0, ending_ref)
+    received_ref, z_ref, u_ref, ending_ref, wout_ref, win_ref,
+    unew_ref, znew_ref, send_ref, begun_ref, rest_ref, packed_ref, held_ref, onto_ref,
+):
     normalise(received_ref, own_rows(received_ref), z_ref, held_ref)
     put = placer(onto_ref)
     for row, block in branch_blocks(held_ref, ending_ref):
@@ -289,8 +295,8 @@
             begun, first = arrived_ref[0, row], first_ref[row]
             tau = fine - (begun + FACTOR * (first - begun))
             out_ref[row] = coarse_ref[row] + tau
-            if (row + 1) % (2 * PART) == 0:
-                rows = pl.ds(row + 1 - 2 * PART, 2 * PART)
+            if (row + 1) % 8 == 0:
+                rows = pl.ds(row - 7, 8)
                 copies.append(
                     pltpu.make_async_copy(out_ref.at[rows], out_hbm.at[rows], sem.at[len(copies)])
                 )
@@ -308,7 +314,7 @@
 TWO = HELD * 2
 CLOSE = HELD + [
     pltpu.VMEM((ROWS, COLS, CHANNELS), jnp.float32),
-    pltpu.SemaphoreType.DMA((CHUNKS,)),
+    pltpu.SemaphoreType.DMA((ROWS // 8,)),
 ]
 CONV_FLOPS = 2 * 4 * 512 * 256 * 768
 
@@ -329,21 +335,21 @@
     )(*args)
 
 
-def ready(initial, conv_in):
+def ready(initial, conv_in, conv_out):
     shape = conv_in.shape[1:]
     return pl.pallas_call(
         ready_kernel,
         name="ready",
-        out_shape=(STATE, READY),
-        in_specs=[pl.BlockSpec(memory_space=pltpu.HBM)] * 2,
-        out_specs=(VMEM,) * 2,
+        out_shape=(STATE, READY, READY),
+        in_specs=[pl.BlockSpec(memory_space=pltpu.HBM)] * 3,
+        out_specs=(VMEM,) * 3,
         scratch_shapes=[
-            pltpu.VMEM((1,) + shape, jnp.float32),
-            pltpu.SemaphoreType.DMA((2,)),
+            pltpu.VMEM((2,) + shape, jnp.float32),
+            pltpu.SemaphoreType.DMA((3,)),
         ],
-        compiler_params=pltpu.CompilerParams(vmem_limit_bytes=READY_LIMIT),
-        cost_estimate=pl.CostEstimate(flops=1000, bytes_accessed=3000000, transcendentals=0),
-    )(*(pltpu.with_memory_space_constraint(x, pltpu.HBM) for x in (initial, conv_in)))
+        compiler_params=pltpu.CompilerParams(vmem_limit_bytes=VMEM_LIMIT),
+        cost_estimate=pl.CostEstimate(flops=1000, bytes_accessed=4000000, transcendentals=0),
+    )(*(pltpu.with_memory_space_constraint(x, pltpu.HBM) for x in (initial, conv_in, conv_out)))
 
 
 def swapped(x):
@@ -361,15 +367,16 @@
     outs = (STATE, STATE, sent)
 
     before = swapped(guess[0, 0])
-    held, weights = ready(initial[0], conv_in)
+    held, weights, ending0 = ready(initial[0], conv_in, conv_out)
+    before, conv_in, conv_out = lax.optimization_barrier((before, conv_in, conv_out))
     z, u, send = call(open_kernel, "open", outs, 1, HELD, held, before, weights)
     received = exchange(send)
     packed = jax.ShapeDtypeStruct((2,) + conv_in.shape[1:], jnp.float32)
-    u, z, send, ending, begun, rest, packed = call(
-        begin_kernel, "begin", outs + (READY, READY, STATE, packed), 2, TWO,
-        received, z, u, conv_out, conv_in,
-    )
-    endings, beginnings = [ending], [None, begun]
+    u, z, send, begun, rest, packed = call(
+        begin_kernel, "begin", outs + (READY, STATE, packed), 2, TWO,
+        received, z, u, ending0, conv_out, conv_in,
+    )
+    endings, beginnings = [ending0], [None, begun]
     moved = swapped(packed)
     received = exchange(send)
     for layer in (1, 2):

time: 140 us -> 141 us (level)
  no operation moved by 1% of the time
where the time goes in v8:
time: 141 us
  blocking collectives  114 us (81%)
  Pallas kernels  22.6 us (16%)
  starting transfers between devices  3.01 us (2%)
    all_to_all x8, blocking collectives, exchange(): return lax.all_to_all(apart, WORLD, 0, 0).reshape(send.shape)  114 us
    pallas_call x9, Pallas kernels, call(): pl.pallas_call(kernel, name=name, out_shape=tuple(outs), in_specs=[VMEM]...  21 us
    ppermute x4, starting transfers between devices, swapped(): return lax.ppermute(x, 'depth', [(0, 1), (1, 0)])  3.01 us
  transfers between devices with their start and end apart: 4, of which 1 were waited for; matrix products, arithmetic and copies ran while one was open for 0% of the time, Pallas kernels for 6%

profile of v8, /device:TPU:1, one launch (start us, length us, event | category | flops | bytes accessed | tf_op | source)
XLA Modules:
  0.0 141.0 jit_solution(1513236394330307657)
XLA Ops:
  0.6 1.5 %collective-permute-start = (f32[32,32,128]{2,1,0:T(8,128)}, f32[32,32,128]{2,1,0:T(8,128)S(1)}, u32[]{:S(2)}, u32[]{:S(2)}) collective-permute-start(f32[32,32,128]{2,1,0:T(8,128)} %bitcast.38), channel_id=1, source_target_pairs={{0,64},{64,0},{1,65},{65,1},{2,66},{66,2},{3,67},{67,3},{4,68},{68... | collective-permute-start | bytes 1572872 | tf_op jit(solution)/shard_map/ppermute | solution.py:356
  2.1 1.6 %ready.1 = (f32[32,32,128]{2,1,0:T(8,128)S(1)}, bf16[4,128,768]{2,1,0:T(8,128)(2,1)S(1)}, bf16[4,128,768]{2,1,0:T(8,128)(2,1)S(1)}) custom-call(f32[32,32,128]{2,1,0:T(8,128)} %bitcast.36, f32[4,3,3,128,128]{4,3,2,1,0:T(8,128)} %win_ref.2, f32[4,3,3,128,128]{4,3,2,1,0:T(8,128)} %wout_ref.3), custom_call_target="tpu_custom_call" | custom-call | flops 1000 | bytes 4000000 | tf_op jit(solution)/shard_map/ready/pallas_call | solution.py:340
  3.7 0.0 copy-start
  3.7 0.1 collective-permute-done.before_ref
  3.9 1.2 open.1
  5.1 20.3 %all_to_all.40 = f32[128,2,128]{2,1,0:T(2,128)S(1)} all-to-all(f32[128,2,128]{2,1,0:T(2,128)S(1)} %bitcast.35), channel_id=1, replica_groups=mesh['depth'=2,'batch_0'=4,'batch_1'=4,'batch_2'=4] {'depth','batch_0','..., dimensions={0} | all-to-all | bytes 262144 | tf_op jit(solution)/shard_map/all_to_all | solution.py:361
  25.3 2.6 %begin.1 = (f32[32,32,128]{2,1,0:T(8,128)S(1)}, f32[32,32,128]{2,1,0:T(8,128)S(1)}, f32[256,128]{1,0:T(8,128)S(1)}, bf16[4,128,768]{2,1,0:T(8,128)(2,1)S(1)}, f3...) custom-call(f32[256,128]{1,0:T(8,128)S(1)} %bitcast.21, f32[32,32,128]{2,1,0:T(8,128)S(1)} %get-tuple-element.45.z_ref, ...), custom_call_target="tpu_custom_call" | custom-call | flops 1610612736 | bytes 10354688 | tf_op jit(solution)/shard_map/begin/pallas_call | solution.py:324
  27.9 0.6 collective-permute-start.1
  28.6 13.2 %all_to_all.41 = f32[128,2,128]{2,1,0:T(2,128)S(1)} all-to-all(f32[128,2,128]{2,1,0:T(2,128)S(1)} %bitcast.22), channel_id=1, replica_groups=mesh['depth'=2,'batch_0'=4,'batch_1'=4,'batch_2'=4] {'depth','batch_0','..., dimensions={0} | all-to-all | bytes 262144 | tf_op jit(solution)/shard_map/all_to_all | solution.py:361
  41.8 2.5 %step.2 = (f32[32,32,128]{2,1,0:T(8,128)S(1)}, f32[32,32,128]{2,1,0:T(8,128)S(1)}, f32[256,128]{1,0:T(8,128)S(1)}, bf16[4,128,768]{2,1,0:T(8,128)(2,1)S(1)}, bf16[4,128,768]{2,1,0:T(8,128)(2,1)S(1)}) custom-call(f32[256,128]{1,0:T(8,128)S(1)} %bitcast.30, f32[32,32,128]{2,1,0:T(8,128)S(1)} %get-tuple-element.51.z_ref, ...), custom_call_target="tpu_custom_call" | custom-call | flops 1610612736 | bytes 8650752 | tf_op jit(solution)/shard_map/step/pallas_call | solution.py:324
  44.3 13.7 %all_to_all.42 = f32[128,2,128]{2,1,0:T(2,128)S(1)} all-to-all(f32[128,2,128]{2,1,0:T(2,128)S(1)} %bitcast.31), channel_id=1, replica_groups=mesh['depth'=2,'batch_0'=4,'batch_1'=4,'batch_2'=4] {'depth','batch_0','..., dimensions={0} | all-to-all | bytes 262144 | tf_op jit(solution)/shard_map/all_to_all | solution.py:361
  58.0 2.5 %step.3 = (f32[32,32,128]{2,1,0:T(8,128)S(1)}, f32[32,32,128]{2,1,0:T(8,128)S(1)}, f32[256,128]{1,0:T(8,128)S(1)}, bf16[4,128,768]{2,1,0:T(8,128)(2,1)S(1)}, bf16[4,128,768]{2,1,0:T(8,128)(2,1)S(1)}) custom-call(f32[256,128]{1,0:T(8,128)S(1)} %bitcast.32, f32[32,32,128]{2,1,0:T(8,128)S(1)} %get-tuple-element.54.z_ref, ...), custom_call_target="tpu_custom_call" | custom-call | flops 1610612736 | bytes 8650752 | tf_op jit(solution)/shard_map/step/pallas_call | solution.py:324
  60.5 13.7 %all_to_all.43 = f32[128,2,128]{2,1,0:T(2,128)S(1)} all-to-all(f32[128,2,128]{2,1,0:T(2,128)S(1)} %bitcast.33), channel_id=1, replica_groups=mesh['depth'=2,'batch_0'=4,'batch_1'=4,'batch_2'=4] {'depth','batch_0','..., dimensions={0} | all-to-all | bytes 262144 | tf_op jit(solution)/shard_map/all_to_all | solution.py:361
  74.2 3.2 %turn.1 = (f32[2,32,32,128]{3,2,1,0:T(8,128)S(1)}, f32[32,32,128]{2,1,0:T(8,128)}, f32[256,128]{1,0:T(8,128)S(1)}, bf16[4,128,768]{2,1,0:T(8,128)(2,1)S(1)}, bf16[4,128,768]{2,1,0:T(8,128)(2,1)S(1)}) custom-call(f32[256,128]{1,0:T(8,128)S(1)} %bitcast.24, f32[32,32,128]{2,1,0:T(8,128)S(1)} %get-tuple-element.57.z_ref, ...), custom_call_target="tpu_custom_call" | custom-call | flops 1610612736 | bytes 7995392 | tf_op jit(solution)/shard_map/turn/pallas_call | solution.py:324
  77.4 0.6 collective-permute-start.2
  78.0 13.2 %all_to_all.44 = f32[128,2,128]{2,1,0:T(2,128)S(1)} all-to-all(f32[128,2,128]{2,1,0:T(2,128)S(1)} %bitcast.25), channel_id=1, replica_groups=mesh['depth'=2,'batch_0'=4,'batch_1'=4,'batch_2'=4] {'depth','batch_0','..., dimensions={0} | all-to-all | bytes 262144 | tf_op jit(solution)/shard_map/all_to_all | solution.py:361
  91.2 2.3 %fork.1 = (f32[32,32,128]{2,1,0:T(8,128)S(1)}, f32[32,32,128]{2,1,0:T(8,128)S(1)}, f32[256,128]{1,0:T(8,128)S(1)}) custom-call(f32[256,128]{1,0:T(8,128)S(1)} %bitcast.23, f32[2,32,32,128]{3,2,1,0:T(8,128)S(1)} %collective-permute-done.2.arrived_ref, f32[2,32,32,128]{3,2,1,0:T(8,128)S(1)} %get-tuple-element.61.both_ref, ...), custom_call_target="tpu_custom_call" | custom-call | flops 1610612736 | bytes 6291456 | tf_op jit(solution)/shard_map/fork/pallas_call | solution.py:324
  93.5 13.3 %all_to_all.45 = f32[128,2,128]{2,1,0:T(2,128)S(1)} all-to-all(f32[128,2,128]{2,1,0:T(2,128)S(1)} %bitcast.28), channel_id=1, replica_groups=mesh['depth'=2,'batch_0'=4,'batch_1'=4,'batch_2'=4] {'depth','batch_0','..., dimensions={0} | all-to-all | bytes 262144 | tf_op jit(solution)/shard_map/all_to_all | solution.py:361
  106.8 2.3 %coarse.1 = (f32[32,32,128]{2,1,0:T(8,128)S(1)}, f32[32,32,128]{2,1,0:T(8,128)S(1)}, f32[256,128]{1,0:T(8,128)S(1)}) custom-call(f32[256,128]{1,0:T(8,128)S(1)} %bitcast.27, f32[32,32,128]{2,1,0:T(8,128)S(1)} %get-tuple-element.66.z_ref, f32[32,32,128]{2,1,0:T(8,128)S(1)} %get-tuple-element.67.u_ref.first_ref, ...), custom_call_target="tpu_custom_call" | custom-call | flops 1610612736 | bytes 5111808 | tf_op jit(solution)/shard_map/coarse/pallas_call | solution.py:324
  109.2 0.3 collective-permute-start.3
  109.5 13.7 %all_to_all.46 = f32[128,2,128]{2,1,0:T(2,128)S(1)} all-to-all(f32[128,2,128]{2,1,0:T(2,128)S(1)} %bitcast.26), channel_id=1, replica_groups=mesh['depth'=2,'batch_0'=4,'batch_1'=4,'batch_2'=4] {'depth','batch_0','..., dimensions={0} | all-to-all | bytes 262144 | tf_op jit(solution)/shard_map/all_to_all | solution.py:361
  123.1 2.3 %second.1 = (f32[32,32,128]{2,1,0:T(8,128)S(1)}, f32[32,32,128]{2,1,0:T(8,128)S(1)}, f32[256,128]{1,0:T(8,128)S(1)}) custom-call(f32[256,128]{1,0:T(8,128)S(1)} %bitcast.29, f32[32,32,128]{2,1,0:T(8,128)S(1)} %get-tuple-element.71.refs_1_, f32[32,32,128]{2,1,0:T(8,128)S(1)} %get-tuple-element.72.refs_2_, bf16[4,128,768]{2,1,0:T(8,128)(2,1)S(1)} %get-tuple-element.73.refs_3_, ...), custom_call_target="tpu_custom_call" | custom-call | flops 1610612736 | bytes 3932160 | tf_op jit(solution)/shard_map/second/pallas_call | solution.py:324
  125.5 13.3 %all_to_all.47 = f32[128,2,128]{2,1,0:T(2,128)S(1)} all-to-all(f32[128,2,128]{2,1,0:T(2,128)S(1)} %bitcast.34), channel_id=1, replica_groups=mesh['depth'=2,'batch_0'=4,'batch_1'=4,'batch_2'=4] {'depth','batch_0','..., dimensions={0} | all-to-all | bytes 262144 | tf_op jit(solution)/shard_map/all_to_all | solution.py:361
  138.8 2.0 %close.1 = f32[32,32,128]{2,1,0:T(8,128)} custom-call(f32[256,128]{1,0:T(8,128)S(1)} %bitcast.20, f32[32,32,128]{2,1,0:T(8,128)S(1)} %get-tuple-element.76.z_ref, f32[32,32,128]{2,1,0:T(8,128)S(1)} %get-tuple-element.77.u_ref, bf16[4,128,768]{2,1,0:T(8,128)(2,1)S(1)} %get-tuple-element.78.ending_ref, ...), custom_call_target="tpu_custom_call" | custom-call | flops 805306368 | bytes 4587520 | tf_op jit(solution)/shard_map/close/pallas_call | solution.py:324
  (6 shorter events, 0.0 us)
Async XLA Ops:
  0.6 3.2 %collective-permute-start = (f32[32,32,128]{2,1,0:T(8,128)}, f32[32,32,128]{2,1,0:T(8,128)S(1)}, u32[]{:S(2)}, u32[]{:S(2)}) collective-permute-start(f32[32,32,128]{2,1,0:T(8,128)} %bitcast.38), channel_id=1, source_target_pairs={{0,64},{64,0},{1,65},{65,1},{2,66},{66,2},{3,67},{67,3},{4,68},{68... | collective-permute-start | bytes 1572872 | tf_op jit(solution)/shard_map/ppermute | solution.py:356
  2.1 23.2 %copy-start.1 = (f32[4,3,3,128,128]{4,3,2,1,0:T(8,128)S(1)}, f32[4,3,3,128,128]{4,3,2,1,0:T(8,128)}, u32[]{:S(2)}) copy-start(f32[4,3,3,128,128]{4,3,2,1,0:T(8,128)} %wout_ref.3) | copy-start | bytes 7077892
  3.7 21.6 %copy-start = (f32[4,3,3,128,128]{4,3,2,1,0:T(8,128)S(1)}, f32[4,3,3,128,128]{4,3,2,1,0:T(8,128)}, u32[]{:S(2)}) copy-start(f32[4,3,3,128,128]{4,3,2,1,0:T(8,128)} %win_ref.2) | copy-start | bytes 7077892
  27.9 46.3 %collective-permute-start.1 = (f32[2,3,3,128,128]{4,3,2,1,0:T(8,128)S(1)}, f32[2,3,3,128,128]{4,3,2,1,0:T(8,128)S(1)}, u32[]{:S(2)}, u32[]{:S(2)}) collective-permute-start(f32[2,3,3,128,128]{4,3,2,1,0:T(8,128)S(1)} %get-tuple-element.59), channel_id=1, source_target_pairs={{0,64},{64,0},{1,65},{65,1},{2,66},{66,2},{3,67},{67,3},{4,68},{68... | collective-permute-start | bytes 3538952 | tf_op jit(solution)/shard_map/ppermute | solution.py:356
  77.4 13.8 %collective-permute-start.2 = (f32[2,32,32,128]{3,2,1,0:T(8,128)S(1)}, f32[2,32,32,128]{3,2,1,0:T(8,128)S(1)}, u32[]{:S(2)}, u32[]{:S(2)}) collective-permute-start(f32[2,32,32,128]{3,2,1,0:T(8,128)S(1)} %get-tuple-element.61.both_ref), channel_id=1, source_target_pairs={{0,64},{64,0},{1,65},{65,1},{2,66},{66,2},{3,67},{67,3},{4,68},{68... | collective-permute-start | bytes 3145736 | tf_op jit(solution)/shard_map/ppermute | solution.py:356
  109.2 29.6 %collective-permute-start.3 = (f32[32,32,128]{2,1,0:T(8,128)S(1)}, f32[32,32,128]{2,1,0:T(8,128)S(1)}, u32[]{:S(2)}, u32[]{:S(2)}) collective-permute-start(f32[32,32,128]{2,1,0:T(8,128)S(1)} %get-tuple-element.72.refs_2_), channel_id=1, source_target_pairs={{0,64},{64,0},{1,65},{65,1},{2,66},{66,2},{3,67},{67,3},{4,68},{68... | collective-permute-start | bytes 1572872 | tf_op jit(solution)/shard_map/ppermute | solution.py:356

commit v9 on v7

--- a/solution.py
+++ b/solution.py
@@ -23,7 +23,6 @@
 CHUNKS = 2
 PART = PAIRS // CHUNKS
 VMEM_LIMIT = 24 * 2**20
-READY_LIMIT = 24 * 2**20
 
 
 def split(x):
@@ -153,13 +152,19 @@
             weights_ref[kind, :, (3 + across) * CHANNELS : (4 + across) * CHANNELS] = low
 
 
-def ready_kernel(initial_hbm, win_hbm, initial_ref, weights_ref, raw_ref, sem):
-    weights = pltpu.make_async_copy(win_hbm.at[pl.ds(0, 1)], raw_ref, sem.at[0])
-    state = pltpu.make_async_copy(initial_hbm, initial_ref, sem.at[1])
-    weights.start()
-    state.start()
-    weights.wait()
-    split_weights(raw_ref, 0, weights_ref)
+def ready_kernel(
+    initial_hbm, win_hbm, wout_hbm, initial_ref, begun0_ref, ending0_ref, begun1_ref, raw_ref, sem
+):
+    weights = [
+        pltpu.make_async_copy(source, raw_ref.at[at], sem.at[at])
+        for at, source in enumerate((win_hbm.at[0], wout_hbm.at[0], win_hbm.at[1]))
+    ]
+    state = pltpu.make_async_copy(initial_hbm, initial_ref, sem.at[3])
+    for copy in (*weights, state):
+        copy.start()
+    for at, ready_ref in enumerate((begun0_ref, ending0_ref, begun1_ref)):
+        weights[at].wait()
+        split_weights(raw_ref, at, ready_ref)
     state.wait()
 
 
@@ -180,10 +185,9 @@
 
 
 def begin_kernel(
-    received_ref, z_ref, u_ref, wout_ref, win_ref,
-    unew_ref, znew_ref, send_ref, ending_ref, begun_ref, rest_ref, packed_ref, held_ref, onto_ref,
-):
-    split_weights(wout_ref, 0, ending_ref)
+    received_ref, z_ref, u_ref, ending_ref, begun_ref, wout_ref, win_ref,
+    unew_ref, znew_ref, send_ref, rest_ref, packed_ref, held_ref, onto_ref,
+):
     normalise(received_ref, own_rows(received_ref), z_ref, held_ref)
     put = placer(onto_ref)
     for row, block in branch_blocks(held_ref, ending_ref):
@@ -195,7 +199,6 @@
         rest_ref[row] = coarse - (before + FACTOR * (after - before))
     packed_ref[0] = win_ref[0]
     packed_ref[1] = wout_ref[0]
-    split_weights(win_ref, 1, begun_ref)
     into_conv(onto_ref, begun_ref, znew_ref, send_ref)
 
 
@@ -329,21 +332,21 @@
     )(*args)
 
 
-def ready(initial, conv_in):
+def ready(initial, conv_in, conv_out):
     shape = conv_in.shape[1:]
     return pl.pallas_call(
         ready_kernel,
         name="ready",
-        out_shape=(STATE, READY),
-        in_specs=[pl.BlockSpec(memory_space=pltpu.HBM)] * 2,
-        out_specs=(VMEM,) * 2,
+        out_shape=(STATE, READY, READY, READY),
+        in_specs=[pl.BlockSpec(memory_space=pltpu.HBM)] * 3,
+        out_specs=(VMEM,) * 4,
         scratch_shapes=[
-            pltpu.VMEM((1,) + shape, jnp.float32),
-            pltpu.SemaphoreType.DMA((2,)),
+            pltpu.VMEM((3,) + shape, jnp.float32),
+            pltpu.SemaphoreType.DMA((4,)),
         ],
-        compiler_params=pltpu.CompilerParams(vmem_limit_bytes=READY_LIMIT),
-        cost_estimate=pl.CostEstimate(flops=1000, bytes_accessed=3000000, transcendentals=0),
-    )(*(pltpu.with_memory_space_constraint(x, pltpu.HBM) for x in (initial, conv_in)))
+        compiler_params=pltpu.CompilerParams(vmem_limit_bytes=VMEM_LIMIT),
+        cost_estimate=pl.CostEstimate(flops=1000, bytes_accessed=5000000, transcendentals=0),
+    )(*(pltpu.with_memory_space_constraint(x, pltpu.HBM) for x in (initial, conv_in, conv_out)))
 
 
 def swapped(x):
@@ -361,15 +364,15 @@
     outs = (STATE, STATE, sent)
 
     before = swapped(guess[0, 0])
-    held, weights = ready(initial[0], conv_in)
+    held, weights, ending0, begun1 = ready(initial[0], conv_in, conv_out)
     z, u, send = call(open_kernel, "open", outs, 1, HELD, held, before, weights)
     received = exchange(send)
     packed = jax.ShapeDtypeStruct((2,) + conv_in.shape[1:], jnp.float32)
-    u, z, send, ending, begun, rest, packed = call(
-        begin_kernel, "begin", outs + (READY, READY, STATE, packed), 2, TWO,
-        received, z, u, conv_out, conv_in,
-    )
-    endings, beginnings = [ending], [None, begun]
+    u, z, send, rest, packed = call(
+        begin_kernel, "begin", outs + (STATE, packed), 2, TWO,
+        received, z, u, ending0, begun1, conv_out, conv_in,
+    )
+    endings, beginnings = [ending0], [None, begun1]
     moved = swapped(packed)
     received = exchange(send)
     for layer in (1, 2):

time: 140 us -> 140 us (level)
  transfers between devices with their start and end apart: 4 -> 4, of which waited for: 1 -> 0; matrix products, arithmetic and copies ran while one was open for 0% -> 0% of each run, Pallas kernels for 6% -> 7%
where the time goes in v9:
time: 140 us
  blocking collectives  114 us (81%)
  Pallas kernels  21.8 us (16%)
  starting transfers between devices  2.88 us (2%)
    all_to_all x8, blocking collectives, exchange(): return lax.all_to_all(apart, WORLD, 0, 0).reshape(send.shape)  114 us
    pallas_call x9, Pallas kernels, call(): pl.pallas_call(kernel, name=name, out_shape=tuple(outs), in_specs=[VMEM]...  20.1 us
    ppermute x4, starting transfers between devices, swapped(): return lax.ppermute(x, 'depth', [(0, 1), (1, 0)])  2.88 us
  transfers between devices with their start and end apart: 4, of which 0 were waited for; matrix products, arithmetic and copies ran while one was open for 0% of the time, Pallas kernels for 7%

profile of v9, /device:TPU:1, one launch (start us, length us, event | category | flops | bytes accessed | tf_op | source)
XLA Modules:
  0.0 139.9 jit_solution(13163667760006087573)
XLA Ops:
  0.6 1.5 %collective-permute-start = (f32[32,32,128]{2,1,0:T(8,128)}, f32[32,32,128]{2,1,0:T(8,128)S(1)}, u32[]{:S(2)}, u32[]{:S(2)}) collective-permute-start(f32[32,32,128]{2,1,0:T(8,128)} %bitcast.38), channel_id=1, source_target_pairs={{0,64},{64,0},{1,65},{65,1},{2,66},{66,2},{3,67},{67,3},{4,68},{68... | collective-permute-start | bytes 1572872 | tf_op jit(solution)/shard_map/ppermute | solution.py:353
  2.1 1.8 %ready.1 = (f32[32,32,128]{2,1,0:T(8,128)S(1)}, bf16[4,128,768]{2,1,0:T(8,128)(2,1)S(1)}, bf16[4,128,768]{2,1,0:T(8,128)(2,1)S(1)}, bf16[4,128,768]{2,1,0:T(8,128)(2,1)S(1)}) custom-call(f32[32,32,128]{2,1,0:T(8,128)} %bitcast.36, f32[4,3,3,128,128]{4,3,2,1,0:T(8,128)} %win_ref.5, f32[4,3,3,128,128]{4,3,2,1,0:T(8,128)} %wout_ref.7), custom_call_target="tpu_custom_call" | custom-call | flops 1000 | bytes 5000000 | tf_op jit(solution)/shard_map/ready/pallas_call | solution.py:337
  3.9 0.0 copy-start
  3.9 0.0 collective-permute-done.before_ref
  3.9 1.2 open.1
  5.1 20.2 %all_to_all.40 = f32[128,2,128]{2,1,0:T(2,128)S(1)} all-to-all(f32[128,2,128]{2,1,0:T(2,128)S(1)} %bitcast.35), channel_id=1, replica_groups=mesh['depth'=2,'batch_0'=4,'batch_1'=4,'batch_2'=4] {'depth','batch_0','..., dimensions={0} | all-to-all | bytes 262144 | tf_op jit(solution)/shard_map/all_to_all | solution.py:358
  25.3 2.3 %begin.1 = (f32[32,32,128]{2,1,0:T(8,128)S(1)}, f32[32,32,128]{2,1,0:T(8,128)S(1)}, f32[256,128]{1,0:T(8,128)S(1)}, f32[32,32,128]{2,1,0:T(8,128)S(1)}, f32[2,3,3,128,128]{4,3,2,1,0:T(8,128)S(1)}) custom-call(f32[256,128]{1,0:T(8,128)S(1)} %bitcast.20, f32[32,32,128]{2,1,0:T(8,128)S(1)} %get-tuple-element.41.z_ref, ...), custom_call_target="tpu_custom_call" | custom-call | flops 1610612736 | bytes 10354688 | tf_op jit(solution)/shard_map/begin/pallas_call | solution.py:321
  27.6 0.6 collective-permute-start.1
  28.3 13.2 %all_to_all.41 = f32[128,2,128]{2,1,0:T(2,128)S(1)} all-to-all(f32[128,2,128]{2,1,0:T(2,128)S(1)} %bitcast.23), channel_id=1, replica_groups=mesh['depth'=2,'batch_0'=4,'batch_1'=4,'batch_2'=4] {'depth','batch_0','..., dimensions={0} | all-to-all | bytes 262144 | tf_op jit(solution)/shard_map/all_to_all | solution.py:358
  41.5 2.6 %step.2 = (f32[32,32,128]{2,1,0:T(8,128)S(1)}, f32[32,32,128]{2,1,0:T(8,128)S(1)}, f32[256,128]{1,0:T(8,128)S(1)}, bf16[4,128,768]{2,1,0:T(8,128)(2,1)S(1)}, bf16[4,128,768]{2,1,0:T(8,128)(2,1)S(1)}) custom-call(f32[256,128]{1,0:T(8,128)S(1)} %bitcast.30, f32[32,32,128]{2,1,0:T(8,128)S(1)} %get-tuple-element.46.z_ref, ...), custom_call_target="tpu_custom_call" | custom-call | flops 1610612736 | bytes 8650752 | tf_op jit(solution)/shard_map/step/pallas_call | solution.py:321
  44.1 13.7 %all_to_all.42 = f32[128,2,128]{2,1,0:T(2,128)S(1)} all-to-all(f32[128,2,128]{2,1,0:T(2,128)S(1)} %bitcast.31), channel_id=1, replica_groups=mesh['depth'=2,'batch_0'=4,'batch_1'=4,'batch_2'=4] {'depth','batch_0','..., dimensions={0} | all-to-all | bytes 262144 | tf_op jit(solution)/shard_map/all_to_all | solution.py:358
  57.7 2.6 %step.3 = (f32[32,32,128]{2,1,0:T(8,128)S(1)}, f32[32,32,128]{2,1,0:T(8,128)S(1)}, f32[256,128]{1,0:T(8,128)S(1)}, bf16[4,128,768]{2,1,0:T(8,128)(2,1)S(1)}, bf16[4,128,768]{2,1,0:T(8,128)(2,1)S(1)}) custom-call(f32[256,128]{1,0:T(8,128)S(1)} %bitcast.32, f32[32,32,128]{2,1,0:T(8,128)S(1)} %get-tuple-element.49.z_ref, ...), custom_call_target="tpu_custom_call" | custom-call | flops 1610612736 | bytes 8650752 | tf_op jit(solution)/shard_map/step/pallas_call | solution.py:321
  60.3 13.7 %all_to_all.43 = f32[128,2,128]{2,1,0:T(2,128)S(1)} all-to-all(f32[128,2,128]{2,1,0:T(2,128)S(1)} %bitcast.33), channel_id=1, replica_groups=mesh['depth'=2,'batch_0'=4,'batch_1'=4,'batch_2'=4] {'depth','batch_0','..., dimensions={0} | all-to-all | bytes 262144 | tf_op jit(solution)/shard_map/all_to_all | solution.py:358
  74.0 2.6 %turn.1 = (f32[2,32,32,128]{3,2,1,0:T(8,128)S(1)}, f32[32,32,128]{2,1,0:T(8,128)}, f32[256,128]{1,0:T(8,128)S(1)}, bf16[4,128,768]{2,1,0:T(8,128)(2,1)S(1)}, bf16[4,128,768]{2,1,0:T(8,128)(2,1)S(1)}) custom-call(f32[256,128]{1,0:T(8,128)S(1)} %bitcast.24, f32[32,32,128]{2,1,0:T(8,128)S(1)} %get-tuple-element.52.z_ref, ...), custom_call_target="tpu_custom_call" | custom-call | flops 1610612736 | bytes 7995392 | tf_op jit(solution)/shard_map/turn/pallas_call | solution.py:321
  76.6 0.6 collective-permute-start.2
  77.2 13.2 %all_to_all.44 = f32[128,2,128]{2,1,0:T(2,128)S(1)} all-to-all(f32[128,2,128]{2,1,0:T(2,128)S(1)} %bitcast.25), channel_id=1, replica_groups=mesh['depth'=2,'batch_0'=4,'batch_1'=4,'batch_2'=4] {'depth','batch_0','..., dimensions={0} | all-to-all | bytes 262144 | tf_op jit(solution)/shard_map/all_to_all | solution.py:358
  90.4 2.3 %fork.1 = (f32[32,32,128]{2,1,0:T(8,128)S(1)}, f32[32,32,128]{2,1,0:T(8,128)S(1)}, f32[256,128]{1,0:T(8,128)S(1)}) custom-call(f32[256,128]{1,0:T(8,128)S(1)} %bitcast.22, f32[2,32,32,128]{3,2,1,0:T(8,128)S(1)} %collective-permute-done.2.arrived_ref, f32[2,32,32,128]{3,2,1,0:T(8,128)S(1)} %get-tuple-element.56.both_ref, ...), custom_call_target="tpu_custom_call" | custom-call | flops 1610612736 | bytes 6291456 | tf_op jit(solution)/shard_map/fork/pallas_call | solution.py:321
  92.7 13.3 %all_to_all.45 = f32[128,2,128]{2,1,0:T(2,128)S(1)} all-to-all(f32[128,2,128]{2,1,0:T(2,128)S(1)} %bitcast.28), channel_id=1, replica_groups=mesh['depth'=2,'batch_0'=4,'batch_1'=4,'batch_2'=4] {'depth','batch_0','..., dimensions={0} | all-to-all | bytes 262144 | tf_op jit(solution)/shard_map/all_to_all | solution.py:358
  106.1 2.3 %coarse.1 = (f32[32,32,128]{2,1,0:T(8,128)S(1)}, f32[32,32,128]{2,1,0:T(8,128)S(1)}, f32[256,128]{1,0:T(8,128)S(1)}) custom-call(f32[256,128]{1,0:T(8,128)S(1)} %bitcast.27, f32[32,32,128]{2,1,0:T(8,128)S(1)} %get-tuple-element.60.z_ref, f32[32,32,128]{2,1,0:T(8,128)S(1)} %get-tuple-element.61.u_ref.first_ref, ...), custom_call_target="tpu_custom_call" | custom-call | flops 1610612736 | bytes 5111808 | tf_op jit(solution)/shard_map/coarse/pallas_call | solution.py:321
  108.4 0.1 collective-permute-start.3
  108.5 13.7 %all_to_all.46 = f32[128,2,128]{2,1,0:T(2,128)S(1)} all-to-all(f32[128,2,128]{2,1,0:T(2,128)S(1)} %bitcast.26), channel_id=1, replica_groups=mesh['depth'=2,'batch_0'=4,'batch_1'=4,'batch_2'=4] {'depth','batch_0','..., dimensions={0} | all-to-all | bytes 262144 | tf_op jit(solution)/shard_map/all_to_all | solution.py:358
  122.1 2.3 %second.1 = (f32[32,32,128]{2,1,0:T(8,128)S(1)}, f32[32,32,128]{2,1,0:T(8,128)S(1)}, f32[256,128]{1,0:T(8,128)S(1)}) custom-call(f32[256,128]{1,0:T(8,128)S(1)} %bitcast.29, f32[32,32,128]{2,1,0:T(8,128)S(1)} %get-tuple-element.65.refs_1_, f32[32,32,128]{2,1,0:T(8,128)S(1)} %get-tuple-element.66.refs_2_, bf16[4,128,768]{2,1,0:T(8,128)(2,1)S(1)} %get-tuple-element.67.refs_3_, ...), custom_call_target="tpu_custom_call" | custom-call | flops 1610612736 | bytes 3932160 | tf_op jit(solution)/shard_map/second/pallas_call | solution.py:321
  124.5 13.3 %all_to_all.47 = f32[128,2,128]{2,1,0:T(2,128)S(1)} all-to-all(f32[128,2,128]{2,1,0:T(2,128)S(1)} %bitcast.34), channel_id=1, replica_groups=mesh['depth'=2,'batch_0'=4,'batch_1'=4,'batch_2'=4] {'depth','batch_0','..., dimensions={0} | all-to-all | bytes 262144 | tf_op jit(solution)/shard_map/all_to_all | solution.py:358
  137.8 2.0 %close.1 = f32[32,32,128]{2,1,0:T(8,128)} custom-call(f32[256,128]{1,0:T(8,128)S(1)} %bitcast.21, f32[32,32,128]{2,1,0:T(8,128)S(1)} %get-tuple-element.70.z_ref, f32[32,32,128]{2,1,0:T(8,128)S(1)} %get-tuple-element.71.u_ref, bf16[4,128,768]{2,1,0:T(8,128)(2,1)S(1)} %get-tuple-element.72.ending_ref, ...), custom_call_target="tpu_custom_call" | custom-call | flops 805306368 | bytes 4587520 | tf_op jit(solution)/shard_map/close/pallas_call | solution.py:321
  (6 shorter events, 0.0 us)
Async XLA Ops:
  0.6 3.3 %collective-permute-start = (f32[32,32,128]{2,1,0:T(8,128)}, f32[32,32,128]{2,1,0:T(8,128)S(1)}, u32[]{:S(2)}, u32[]{:S(2)}) collective-permute-start(f32[32,32,128]{2,1,0:T(8,128)} %bitcast.38), channel_id=1, source_target_pairs={{0,64},{64,0},{1,65},{65,1},{2,66},{66,2},{3,67},{67,3},{4,68},{68... | collective-permute-start | bytes 1572872 | tf_op jit(solution)/shard_map/ppermute | solution.py:353
  2.1 23.2 %copy-start.1 = (f32[4,3,3,128,128]{4,3,2,1,0:T(8,128)S(1)}, f32[4,3,3,128,128]{4,3,2,1,0:T(8,128)}, u32[]{:S(2)}) copy-start(f32[4,3,3,128,128]{4,3,2,1,0:T(8,128)} %wout_ref.7) | copy-start | bytes 7077892
  3.9 21.4 %copy-start = (f32[4,3,3,128,128]{4,3,2,1,0:T(8,128)S(1)}, f32[4,3,3,128,128]{4,3,2,1,0:T(8,128)}, u32[]{:S(2)}) copy-start(f32[4,3,3,128,128]{4,3,2,1,0:T(8,128)} %win_ref.5) | copy-start | bytes 7077892
  27.6 46.4 %collective-permute-start.1 = (f32[2,3,3,128,128]{4,3,2,1,0:T(8,128)S(1)}, f32[2,3,3,128,128]{4,3,2,1,0:T(8,128)S(1)}, u32[]{:S(2)}, u32[]{:S(2)}) collective-permute-start(f32[2,3,3,128,128]{4,3,2,1,0:T(8,128)S(1)} %get-tuple-element.54), channel_id=1, source_target_pairs={{0,64},{64,0},{1,65},{65,1},{2,66},{66,2},{3,67},{67,3},{4,68},{68... | collective-permute-start | bytes 3538952 | tf_op jit(solution)/shard_map/ppermute | solution.py:353
  76.6 13.9 %collective-permute-start.2 = (f32[2,32,32,128]{3,2,1,0:T(8,128)S(1)}, f32[2,32,32,128]{3,2,1,0:T(8,128)S(1)}, u32[]{:S(2)}, u32[]{:S(2)}) collective-permute-start(f32[2,32,32,128]{3,2,1,0:T(8,128)S(1)} %get-tuple-element.56.both_ref), channel_id=1, source_target_pairs={{0,64},{64,0},{1,65},{65,1},{2,66},{66,2},{3,67},{67,3},{4,68},{68... | collective-permute-start | bytes 3145736 | tf_op jit(solution)/shard_map/ppermute | solution.py:353
  108.4 29.4 %collective-permute-start.3 = (f32[32,32,128]{2,1,0:T(8,128)S(1)}, f32[32,32,128]{2,1,0:T(8,128)S(1)}, u32[]{:S(2)}, u32[]{:S(2)}) collective-permute-start(f32[32,32,128]{2,1,0:T(8,128)S(1)} %get-tuple-element.66.refs_2_), channel_id=1, source_target_pairs={{0,64},{64,0},{1,65},{65,1},{2,66},{66,2},{3,67},{67,3},{4,68},{68... | collective-permute-start | bytes 1572872 | tf_op jit(solution)/shard_map/ppermute | solution.py:353

commit v10 on v9

--- a/solution.py
+++ b/solution.py
@@ -215,7 +215,7 @@
 
 def turn_kernel(
     received_ref, z_ref, u_ref, wout_ref, moved_ref,
-    both_ref, ends_ref, send_ref, ending_ref, begun_ref, held_ref, onto_ref,
+    both_ref, send_ref, ending_ref, begun_ref, held_ref, onto_ref,
 ):
     split_weights(wout_ref, FACTOR - 1, ending_ref)
     normalise(received_ref, own_rows(received_ref), z_ref, held_ref)
@@ -223,7 +223,6 @@
     for row, block in branch_blocks(held_ref, ending_ref):
         after = u_ref[row] + STEP_SIZE * block
         both_ref[0, row] = after
-        ends_ref[row] = after
         put(row, after)
     split_weights(moved_ref, 0, begun_ref)
     into_conv(onto_ref, begun_ref, both_ref.at[1], send_ref)
@@ -231,8 +230,11 @@
 
 def fork_kernel(
     received_ref, arrived_ref, both_ref, rest_ref, moved_ref, ending_ref, begun_ref,
-    unew_ref, znew_ref, send_ref, held_ref, onto_ref,
-):
+    unew_ref, znew_ref, send_ref, ends_hbm, held_ref, onto_ref, sem,
+):
+    ends = pltpu.make_async_copy(both_ref.at[0], ends_hbm, sem)
+    ends.start()
+
     @pl.when(core() == 0)
     def _():
         put = placer(held_ref)
@@ -247,6 +249,8 @@
         normalise(received_ref, 0, arrived_ref.at[1], held_ref)
         add_branch(held_ref, ending_ref, STEP_SIZE, arrived_ref.at[0], unew_ref, onto_ref)
         into_conv(onto_ref, begun_ref, znew_ref, send_ref)
+
+    ends.wait()
 
 
 def coarse_kernel(
@@ -305,6 +309,7 @@
 STATE = jax.ShapeDtypeStruct((ROWS, COLS, CHANNELS), jnp.float32)
 BOTH = jax.ShapeDtypeStruct((2, ROWS, COLS, CHANNELS), jnp.float32)
 VMEM = pl.BlockSpec(memory_space=pltpu.VMEM)
+HBM = pl.BlockSpec(memory_space=pltpu.HBM)
 HELD = [pltpu.VMEM((4, PAIRS * COLS, 2 * CHANNELS), jnp.bfloat16)]
 WEIGHTS = [pltpu.VMEM((4, CHANNELS, 6 * CHANNELS), jnp.bfloat16)]
 READY = jax.ShapeDtypeStruct(WEIGHTS[0].shape, jnp.bfloat16)
@@ -316,14 +321,14 @@
 CONV_FLOPS = 2 * 4 * 512 * 256 * 768
 
 
-def call(kernel, name, outs, convs, scratch, *args, out_space=VMEM):
+def call(kernel, name, outs, convs, scratch, *args, spaces=None):
     touched = sum(a.size * a.dtype.itemsize for a in (*args, *outs))
     return pl.pallas_call(
         kernel,
         name=name,
         out_shape=tuple(outs),
         in_specs=[VMEM] * len(args),
-        out_specs=(out_space,) * len(outs),
+        out_specs=spaces or (VMEM,) * len(outs),
         scratch_shapes=scratch,
         compiler_params=pltpu.CompilerParams(vmem_limit_bytes=VMEM_LIMIT),
         cost_estimate=pl.CostEstimate(
@@ -383,16 +388,17 @@
         endings.append(ending)
         beginnings.append(begun)
         received = exchange(send)
-    both, ends, send, ending, coarse_in = call(
-        turn_kernel, "turn", (BOTH, STATE, sent, READY, READY), 2, TWO,
+    both, send, ending, coarse_in = call(
+        turn_kernel, "turn", (BOTH, sent, READY, READY), 2, TWO,
         received, z, u, conv_out, moved,
     )
     endings.append(ending)
     arrived = swapped(both)
     received = exchange(send)
-    first, z, send = call(
-        fork_kernel, "fork", outs, 2, TWO,
+    first, z, send, ends = call(
+        fork_kernel, "fork", outs + (STATE,), 2, TWO + [pltpu.SemaphoreType.DMA(())],
         received, arrived, both, rest, coarse_in, endings[0], beginnings[1],
+        spaces=(VMEM, VMEM, VMEM, HBM),
     )
     received = exchange(send)
     u, z, send = call(
@@ -408,7 +414,7 @@
     (result,) = call(
         close_kernel, "close", (STATE,), 1, CLOSE,
         received, z, u, endings[3], arrived, first, coarse,
-        out_space=pl.BlockSpec(memory_space=pltpu.HBM),
+        spaces=(HBM,),
     )
     return (result[None, None], ends[None, None])
 

time: 140 us -> 140 us (level)
  no operation moved by 1% of the time
where the time goes in v10:
time: 140 us
  blocking collectives  114 us (81%)
  Pallas kernels  21.9 us (16%)
  starting transfers between devices  2.87 us (2%)
    all_to_all x8, blocking collectives, exchange(): return lax.all_to_all(apart, WORLD, 0, 0).reshape(send.shape)  114 us
    pallas_call x9, Pallas kernels, call(): pl.pallas_call(kernel, name=name, out_shape=tuple(outs), in_specs=[VMEM]...  20.1 us
    ppermute x4, starting transfers between devices, swapped(): return lax.ppermute(x, 'depth', [(0, 1), (1, 0)])  2.87 us
  transfers between devices with their start and end apart: 4, of which 0 were waited for; matrix products, arithmetic and copies ran while one was open for 0% of the time, Pallas kernels for 7%

profile of v10, /device:TPU:1, one launch (start us, length us, event | category | flops | bytes accessed | tf_op | source)
XLA Modules:
  0.0 139.9 jit_solution(7702544441902142971)
XLA Ops:
  0.6 1.5 %collective-permute-start = (f32[32,32,128]{2,1,0:T(8,128)}, f32[32,32,128]{2,1,0:T(8,128)S(1)}, u32[]{:S(2)}, u32[]{:S(2)}) collective-permute-start(f32[32,32,128]{2,1,0:T(8,128)} %bitcast.38), channel_id=1, source_target_pairs={{0,64},{64,0},{1,65},{65,1},{2,66},{66,2},{3,67},{67,3},{4,68},{68... | collective-permute-start | bytes 1572872 | tf_op jit(solution)/shard_map/ppermute | solution.py:358
  2.1 1.8 %ready.1 = (f32[32,32,128]{2,1,0:T(8,128)S(1)}, bf16[4,128,768]{2,1,0:T(8,128)(2,1)S(1)}, bf16[4,128,768]{2,1,0:T(8,128)(2,1)S(1)}, bf16[4,128,768]{2,1,0:T(8,128)(2,1)S(1)}) custom-call(f32[32,32,128]{2,1,0:T(8,128)} %bitcast.36, f32[4,3,3,128,128]{4,3,2,1,0:T(8,128)} %win_ref.5, f32[4,3,3,128,128]{4,3,2,1,0:T(8,128)} %wout_ref.7), custom_call_target="tpu_custom_call" | custom-call | flops 1000 | bytes 5000000 | tf_op jit(solution)/shard_map/ready/pallas_call | solution.py:342
  3.9 0.0 copy-start
  3.9 0.0 collective-permute-done.before_ref
  3.9 1.2 open.1
  5.1 20.2 %all_to_all.40 = f32[128,2,128]{2,1,0:T(2,128)S(1)} all-to-all(f32[128,2,128]{2,1,0:T(2,128)S(1)} %bitcast.35), channel_id=1, replica_groups=mesh['depth'=2,'batch_0'=4,'batch_1'=4,'batch_2'=4] {'depth','batch_0','..., dimensions={0} | all-to-all | bytes 262144 | tf_op jit(solution)/shard_map/all_to_all | solution.py:363
  25.3 2.3 %begin.1 = (f32[32,32,128]{2,1,0:T(8,128)S(1)}, f32[32,32,128]{2,1,0:T(8,128)S(1)}, f32[256,128]{1,0:T(8,128)S(1)}, f32[32,32,128]{2,1,0:T(8,128)S(1)}, f32[2,3,3,128,128]{4,3,2,1,0:T(8,128)S(1)}) custom-call(f32[256,128]{1,0:T(8,128)S(1)} %bitcast.20, f32[32,32,128]{2,1,0:T(8,128)S(1)} %get-tuple-element.41.z_ref, ...), custom_call_target="tpu_custom_call" | custom-call | flops 1610612736 | bytes 10354688 | tf_op jit(solution)/shard_map/begin/pallas_call | solution.py:326
  27.6 0.6 collective-permute-start.1
  28.3 13.2 %all_to_all.41 = f32[128,2,128]{2,1,0:T(2,128)S(1)} all-to-all(f32[128,2,128]{2,1,0:T(2,128)S(1)} %bitcast.23), channel_id=1, replica_groups=mesh['depth'=2,'batch_0'=4,'batch_1'=4,'batch_2'=4] {'depth','batch_0','..., dimensions={0} | all-to-all | bytes 262144 | tf_op jit(solution)/shard_map/all_to_all | solution.py:363
  41.5 2.6 %step.2 = (f32[32,32,128]{2,1,0:T(8,128)S(1)}, f32[32,32,128]{2,1,0:T(8,128)S(1)}, f32[256,128]{1,0:T(8,128)S(1)}, bf16[4,128,768]{2,1,0:T(8,128)(2,1)S(1)}, bf16[4,128,768]{2,1,0:T(8,128)(2,1)S(1)}) custom-call(f32[256,128]{1,0:T(8,128)S(1)} %bitcast.30, f32[32,32,128]{2,1,0:T(8,128)S(1)} %get-tuple-element.46.z_ref, ...), custom_call_target="tpu_custom_call" | custom-call | flops 1610612736 | bytes 8650752 | tf_op jit(solution)/shard_map/step/pallas_call | solution.py:326
  44.1 13.7 %all_to_all.42 = f32[128,2,128]{2,1,0:T(2,128)S(1)} all-to-all(f32[128,2,128]{2,1,0:T(2,128)S(1)} %bitcast.31), channel_id=1, replica_groups=mesh['depth'=2,'batch_0'=4,'batch_1'=4,'batch_2'=4] {'depth','batch_0','..., dimensions={0} | all-to-all | bytes 262144 | tf_op jit(solution)/shard_map/all_to_all | solution.py:363
  57.7 2.6 %step.3 = (f32[32,32,128]{2,1,0:T(8,128)S(1)}, f32[32,32,128]{2,1,0:T(8,128)S(1)}, f32[256,128]{1,0:T(8,128)S(1)}, bf16[4,128,768]{2,1,0:T(8,128)(2,1)S(1)}, bf16[4,128,768]{2,1,0:T(8,128)(2,1)S(1)}) custom-call(f32[256,128]{1,0:T(8,128)S(1)} %bitcast.32, f32[32,32,128]{2,1,0:T(8,128)S(1)} %get-tuple-element.49.z_ref, ...), custom_call_target="tpu_custom_call" | custom-call | flops 1610612736 | bytes 8650752 | tf_op jit(solution)/shard_map/step/pallas_call | solution.py:326
  60.3 13.7 %all_to_all.43 = f32[128,2,128]{2,1,0:T(2,128)S(1)} all-to-all(f32[128,2,128]{2,1,0:T(2,128)S(1)} %bitcast.33), channel_id=1, replica_groups=mesh['depth'=2,'batch_0'=4,'batch_1'=4,'batch_2'=4] {'depth','batch_0','..., dimensions={0} | all-to-all | bytes 262144 | tf_op jit(solution)/shard_map/all_to_all | solution.py:363
  74.0 2.6 %turn.1 = (f32[2,32,32,128]{3,2,1,0:T(8,128)S(1)}, f32[256,128]{1,0:T(8,128)S(1)}, bf16[4,128,768]{2,1,0:T(8,128)(2,1)S(1)}, bf16[4,128,768]{2,1,0:T(8,128)(2,1)S(1)}) custom-call(f32[256,128]{1,0:T(8,128)S(1)} %bitcast.25, f32[32,32,128]{2,1,0:T(8,128)S(1)} %get-tuple-element.52.z_ref, f32[32,32,128]{2,1,0:T(8,128)S(1)} %get-tuple-element.53.u_ref, ...), custom_call_target="tpu_custom_call" | custom-call | flops 1610612736 | bytes 7471104 | tf_op jit(solution)/shard_map/turn/pallas_call | solution.py:326
  76.6 0.6 collective-permute-start.2
  77.2 13.2 %all_to_all.44 = f32[128,2,128]{2,1,0:T(2,128)S(1)} all-to-all(f32[128,2,128]{2,1,0:T(2,128)S(1)} %bitcast.26), channel_id=1, replica_groups=mesh['depth'=2,'batch_0'=4,'batch_1'=4,'batch_2'=4] {'depth','batch_0','..., dimensions={0} | all-to-all | bytes 262144 | tf_op jit(solution)/shard_map/all_to_all | solution.py:363
  90.4 2.3 %fork.1 = (f32[32,32,128]{2,1,0:T(8,128)S(1)}, f32[32,32,128]{2,1,0:T(8,128)S(1)}, f32[256,128]{1,0:T(8,128)S(1)}, f32[32,32,128]{2,1,0:T(8,128)}) custom-call(f32[256,128]{1,0:T(8,128)S(1)} %bitcast.22, f32[2,32,32,128]{3,2,1,0:T(8,128)S(1)} %collective-permute-done.2.arrived_ref, f32[2,32,32,128]{3,2,1,0:T(8,128)S(1)} %get-tuple-element.56.both_ref, ...), custom_call_target="tpu_custom_call" | custom-call | flops 1610612736 | bytes 6815744 | tf_op jit(solution)/shard_map/fork/pallas_call | solution.py:326
  92.8 13.3 %all_to_all.45 = f32[128,2,128]{2,1,0:T(2,128)S(1)} all-to-all(f32[128,2,128]{2,1,0:T(2,128)S(1)} %bitcast.27), channel_id=1, replica_groups=mesh['depth'=2,'batch_0'=4,'batch_1'=4,'batch_2'=4] {'depth','batch_0','..., dimensions={0} | all-to-all | bytes 262144 | tf_op jit(solution)/shard_map/all_to_all | solution.py:363
  106.1 2.3 %coarse.1 = (f32[32,32,128]{2,1,0:T(8,128)S(1)}, f32[32,32,128]{2,1,0:T(8,128)S(1)}, f32[256,128]{1,0:T(8,128)S(1)}) custom-call(f32[256,128]{1,0:T(8,128)S(1)} %bitcast.28, f32[32,32,128]{2,1,0:T(8,128)S(1)} %get-tuple-element.60.z_ref, f32[32,32,128]{2,1,0:T(8,128)S(1)} %get-tuple-element.61.u_ref.first_ref, ...), custom_call_target="tpu_custom_call" | custom-call | flops 1610612736 | bytes 5111808 | tf_op jit(solution)/shard_map/coarse/pallas_call | solution.py:326
  108.4 0.1 collective-permute-start.3
  108.5 13.7 %all_to_all.46 = f32[128,2,128]{2,1,0:T(2,128)S(1)} all-to-all(f32[128,2,128]{2,1,0:T(2,128)S(1)} %bitcast.24), channel_id=1, replica_groups=mesh['depth'=2,'batch_0'=4,'batch_1'=4,'batch_2'=4] {'depth','batch_0','..., dimensions={0} | all-to-all | bytes 262144 | tf_op jit(solution)/shard_map/all_to_all | solution.py:363
  122.2 2.3 %second.1 = (f32[32,32,128]{2,1,0:T(8,128)S(1)}, f32[32,32,128]{2,1,0:T(8,128)S(1)}, f32[256,128]{1,0:T(8,128)S(1)}) custom-call(f32[256,128]{1,0:T(8,128)S(1)} %bitcast.29, f32[32,32,128]{2,1,0:T(8,128)S(1)} %get-tuple-element.65.refs_1_, f32[32,32,128]{2,1,0:T(8,128)S(1)} %get-tuple-element.66.refs_2_, bf16[4,128,768]{2,1,0:T(8,128)(2,1)S(1)} %get-tuple-element.67.refs_3_, ...), custom_call_target="tpu_custom_call" | custom-call | flops 1610612736 | bytes 3932160 | tf_op jit(solution)/shard_map/second/pallas_call | solution.py:326
  124.5 13.3 %all_to_all.47 = f32[128,2,128]{2,1,0:T(2,128)S(1)} all-to-all(f32[128,2,128]{2,1,0:T(2,128)S(1)} %bitcast.34), channel_id=1, replica_groups=mesh['depth'=2,'batch_0'=4,'batch_1'=4,'batch_2'=4] {'depth','batch_0','..., dimensions={0} | all-to-all | bytes 262144 | tf_op jit(solution)/shard_map/all_to_all | solution.py:363
  137.8 2.0 %close.1 = f32[32,32,128]{2,1,0:T(8,128)} custom-call(f32[256,128]{1,0:T(8,128)S(1)} %bitcast.21, f32[32,32,128]{2,1,0:T(8,128)S(1)} %get-tuple-element.70.z_ref, f32[32,32,128]{2,1,0:T(8,128)S(1)} %get-tuple-element.71.u_ref, bf16[4,128,768]{2,1,0:T(8,128)(2,1)S(1)} %get-tuple-element.72.ending_ref, ...), custom_call_target="tpu_custom_call" | custom-call | flops 805306368 | bytes 4587520 | tf_op jit(solution)/shard_map/close/pallas_call | solution.py:326
  (6 shorter events, 0.0 us)
Async XLA Ops:
  0.6 3.3 %collective-permute-start = (f32[32,32,128]{2,1,0:T(8,128)}, f32[32,32,128]{2,1,0:T(8,128)S(1)}, u32[]{:S(2)}, u32[]{:S(2)}) collective-permute-start(f32[32,32,128]{2,1,0:T(8,128)} %bitcast.38), channel_id=1, source_target_pairs={{0,64},{64,0},{1,65},{65,1},{2,66},{66,2},{3,67},{67,3},{4,68},{68... | collective-permute-start | bytes 1572872 | tf_op jit(solution)/shard_map/ppermute | solution.py:358
  2.1 23.2 %copy-start.1 = (f32[4,3,3,128,128]{4,3,2,1,0:T(8,128)S(1)}, f32[4,3,3,128,128]{4,3,2,1,0:T(8,128)}, u32[]{:S(2)}) copy-start(f32[4,3,3,128,128]{4,3,2,1,0:T(8,128)} %wout_ref.7) | copy-start | bytes 7077892
  3.9 21.4 %copy-start = (f32[4,3,3,128,128]{4,3,2,1,0:T(8,128)S(1)}, f32[4,3,3,128,128]{4,3,2,1,0:T(8,128)}, u32[]{:S(2)}) copy-start(f32[4,3,3,128,128]{4,3,2,1,0:T(8,128)} %win_ref.5) | copy-start | bytes 7077892
  27.6 46.4 %collective-permute-start.1 = (f32[2,3,3,128,128]{4,3,2,1,0:T(8,128)S(1)}, f32[2,3,3,128,128]{4,3,2,1,0:T(8,128)S(1)}, u32[]{:S(2)}, u32[]{:S(2)}) collective-permute-start(f32[2,3,3,128,128]{4,3,2,1,0:T(8,128)S(1)} %get-tuple-element.54), channel_id=1, source_target_pairs={{0,64},{64,0},{1,65},{65,1},{2,66},{66,2},{3,67},{67,3},{4,68},{68... | collective-permute-start | bytes 3538952 | tf_op jit(solution)/shard_map/ppermute | solution.py:358
  76.6 13.9 %collective-permute-start.2 = (f32[2,32,32,128]{3,2,1,0:T(8,128)S(1)}, f32[2,32,32,128]{3,2,1,0:T(8,128)S(1)}, u32[]{:S(2)}, u32[]{:S(2)}) collective-permute-start(f32[2,32,32,128]{3,2,1,0:T(8,128)S(1)} %get-tuple-element.56.both_ref), channel_id=1, source_target_pairs={{0,64},{64,0},{1,65},{65,1},{2,66},{66,2},{3,67},{67,3},{4,68},{68... | collective-permute-start | bytes 3145736 | tf_op jit(solution)/shard_map/ppermute | solution.py:358
  108.4 29.4 %collective-permute-start.3 = (f32[32,32,128]{2,1,0:T(8,128)S(1)}, f32[32,32,128]{2,1,0:T(8,128)S(1)}, u32[]{:S(2)}, u32[]{:S(2)}) collective-permute-start(f32[32,32,128]{2,1,0:T(8,128)S(1)} %get-tuple-element.66.refs_2_), channel_id=1, source_target_pairs={{0,64},{64,0},{1,65},{65,1},{2,66},{66,2},{3,67},{67,3},{4,68},{68... | collective-permute-start | bytes 1572872 | tf_op jit(solution)/shard_map/ppermute | solution.py:358
